TPU v7x, 128 devices: a whole 4x4x4 slice. The times are simulated.
128 devices in a mesh: section: 2 (over y_hi), ctx: 8 (over x, y_lo), wt: 8 (over z, core).
Axes of the slice: x: 4, y: 4 (y_hi: 2, y_lo: 2; y = y_hi * 2 + y_lo), z: 4, core: 2. Of those that a mesh axis runs over, the one named last changes fastest.
Arguments:
- inputs: bfloat16 [2, 1536, 2048], P(None, 'ctx', 'wt'), may hold values from -6 to 6
- cotangent: bfloat16 [2, 1536, 2048], P(None, 'ctx', 'wt'), may hold values from -6 to 6
- doc_bounds: int32 [2, 2], replicated, may hold values from 1 to 1535, as said below
- attn_gain: bfloat16 [2, 2048], P('section'), may hold values from 0.5 to 1.5
- w_query: bfloat16 [2, 2048, 2048], P('section', None, 'wt'), may hold values from -0.125 to 0.125
- w_key: bfloat16 [2, 2048, 512], P('section', None, 'wt'), may hold values from -0.125 to 0.125
- w_value: bfloat16 [2, 2048, 512], P('section', None, 'wt'), may hold values from -0.125 to 0.125
- w_out: bfloat16 [2, 2048, 2048], P('section', 'wt'), may hold values from -0.75 to 0.75
- mlp_gain: bfloat16 [2, 2048], P('section'), may hold values from 0.5 to 1.5
- w_gate: bfloat16 [2, 2048, 8192], P('section', None, 'wt'), may hold values from -0.125 to 0.125
- w_up: bfloat16 [2, 2048, 8192], P('section', None, 'wt'), may hold values from -0.125 to 0.125
- w_down: bfloat16 [2, 8192, 2048], P('section', 'wt'), may hold values from -0.125 to 0.125
Outputs:
- boundary: bfloat16 [2, 2, 1536, 2048], P('section', None, 'ctx', 'wt')
- gain_attn_grad: float32 [2, 2048], P('section', 'ctx')
- query_grad: float32 [2, 2048, 2048], P('section', 'ctx', 'wt')
- key_grad: float32 [2, 2048, 512], P('section', 'ctx', 'wt')
- value_grad: float32 [2, 2048, 512], P('section', 'ctx', 'wt')
- out_grad: float32 [2, 2048, 2048], P('section', 'wt', 'ctx')
- gain_mlp_grad: float32 [2, 2048], P('section', 'ctx')
- gate_grad: float32 [2, 2048, 8192], P('section', 'ctx', 'wt')
- up_grad: float32 [2, 2048, 8192], P('section', 'ctx', 'wt')
- down_grad: float32 [2, 8192, 2048], P('section', 'wt', 'ctx')
Inputs may be any that keep to these rules, and one draw needn't show every extreme that they name: `doc_bounds`: row b: document 1 of micro-batch b begins at a position from 1 to 191, document 2 at a position from 1345 to 1535; document 0 begins at 0. In some row document 1 begins at 1, and in some row document 2 begins at 1535.
All inputs are finite; a program needn't handle non-finite values.
Results may differ from a plain program's by a relative error of at most 0.038.
Values may be sent and summed in bfloat16 or wider, within the bound.
A program may use at most 192 MiB of HBM per device.

v0:
```python
import jax
import jax.numpy as jnp
from jax import lax
from jax.sharding import PartitionSpec as P

HD = 64


eps = 1e-05
theta = 500000.0
neg_big = -1e30


def laid_out(parts, dim):
    lengths = list(parts.shape[1:])
    lengths[dim] *= parts.shape[0]
    return jnp.moveaxis(parts, 0, dim).reshape(lengths)


def copy_for_each(shard, axis):
    length = lax.axis_size(axis)
    return lax.all_to_all(
        jnp.broadcast_to(shard[None], (length, *shard.shape)), axis, 0, 0, tiled=True
    )


def gather_directly(shard, axis, dim):
    return laid_out(copy_for_each(shard, axis), dim)


def filled_up(lines, length):
    spare = -lines.shape[0] % length
    if not spare:
        return lines
    return jnp.concatenate([lines, jnp.zeros((spare, *lines.shape[1:]), lines.dtype)])


def sum_by_parts(shard, axis):
    lines = shard.reshape(-1, *shard.shape[1:][-1:])
    padded = filled_up(lines, lax.axis_size(axis))
    own = lax.psum_scatter(padded, axis, scatter_dimension=0, tiled=True)
    whole = lax.all_gather(own, axis, axis=0, tiled=True)
    return whole[: len(lines)].reshape(shard.shape)


def cut_along(shard, dim, length):
    before, after = (shard.shape[:dim], shard.shape[dim + 1 :])
    return jnp.moveaxis(shard.reshape(*before, length, -1, *after), dim, 0)


def sum_at_owner(shard, axis, dim):
    parts = cut_along(shard, dim, lax.axis_size(axis))
    arrived = lax.all_to_all(parts, axis, split_axis=0, concat_axis=0, tiled=True)
    return arrived.astype(jnp.float32).sum(axis=0)


def shifted_2(shard, axis, by):
    length = lax.axis_size(axis)
    pairs = [(i, i + by) for i in range(length) if 0 <= i + by < length]
    return lax.ppermute(shard, axis, pairs)


def side_by_side(arrays, axis, dim, along):
    widths = [a.shape[along] for a in arrays]
    both = jnp.concatenate(arrays, axis=along)
    out = lax.psum_scatter(both, axis, scatter_dimension=dim, tiled=True)
    return tuple(jnp.split(out, [sum(widths[:k]) for k in range(1, len(widths))], axis=along))


def rope_freqs(head_width):
    index_steps = jnp.arange(head_width // 2, dtype=jnp.float32)
    inverse = theta ** (-2.0 * index_steps / head_width)
    wavelen = 2.0 * jnp.pi / inverse
    smooth = (8192.0 / wavelen - 1.0) / 3.0
    blended = (1.0 - smooth) * inverse / 32.0 + smooth * inverse
    return jnp.where(
        wavelen < 2048.0, inverse, jnp.where(wavelen > 8192.0, inverse / 32.0, blended)
    )


def doc_info(bounds, places):
    starts = jnp.concatenate([jnp.zeros((1,), jnp.int32), bounds])
    started = places[:, None] >= starts[None, :]
    doc_ids = jnp.sum(started.astype(jnp.int32), axis=1) - 1
    doc_begin = jnp.max(jnp.where(started, starts[None, :], 0), axis=1)
    return (doc_ids, places - doc_begin)


def rope_tables(offsets, head_width):
    angles = offsets.astype(jnp.float32)[:, None] * rope_freqs(head_width)[None, :]
    return (
        jnp.concatenate([jnp.cos(angles)] * 2, axis=1),
        jnp.concatenate([jnp.sin(angles)] * 2, axis=1),
    )


def rotate(vectors, cosine_table, sine_table):
    half_width = vectors.shape[-1] // 2
    turned = jnp.concatenate([-vectors[..., half_width:], vectors[..., :half_width]], axis=-1)
    return vectors * cosine_table + turned * sine_table


def unrotate(gradient, cosine_table, sine_table):
    half_width = gradient.shape[-1] // 2
    shifted = gradient * sine_table
    turned = jnp.concatenate([shifted[..., half_width:], -shifted[..., :half_width]], axis=-1)
    return gradient * cosine_table + turned


def contract_rows(left, right):
    return lax.dot_general(
        left, right, (((0,), (0,)), ((), ())), preferred_element_type=jnp.float32
    )


def times_transposed(left, right):
    return lax.dot_general(
        left, right, (((1,), (1,)), ((), ())), preferred_element_type=jnp.float32
    )


def normalize(hidden):
    factor = lax.rsqrt(jnp.mean(hidden * hidden, axis=-1, keepdims=True) + eps)
    return (hidden * factor, factor)


def norm_backward(grad_normed, normed, factor, gain):
    scaled = grad_normed * gain
    return factor * (scaled - normed * jnp.mean(scaled * normed, axis=-1, keepdims=True))


def per_device(
    inputs,
    cotangent,
    doc_bounds,
    attn_gain,
    w_query,
    w_key,
    w_value,
    w_out,
    mlp_gain,
    w_gate,
    w_up,
    w_down,
):
    section_rank = lax.axis_index("section")
    ctx_rank = lax.axis_index("ctx")
    wt_rank = lax.axis_index("wt")
    micro_count = inputs.shape[0]
    block_rows = inputs.shape[1]
    share_width = inputs.shape[2]
    seq_len = block_rows * lax.axis_size("ctx")
    head_dim = HD
    local_heads = w_query.shape[2] // head_dim
    local_kv = w_key.shape[2] // head_dim
    groups = local_heads // local_kv
    rows_heads = groups * block_rows
    kv_width = local_kv * head_dim
    key_block = min(seq_len, 512)
    key_starts = jnp.arange(seq_len // key_block, dtype=jnp.int32) * key_block
    scale_factor = head_dim ** (-0.5)
    all_places = jnp.arange(seq_len, dtype=jnp.int32)
    params = {
        "gain_attn": attn_gain[0].astype(jnp.float32),
        "query": w_query[0],
        "key": w_key[0],
        "value": w_value[0],
        "out": w_out[0],
        "gain_mlp": mlp_gain[0].astype(jnp.float32),
        "gate": w_gate[0],
        "up": w_up[0],
        "down": w_down[0],
    }

    def widen_rows(piece):
        return gather_directly(piece, "wt", 1).astype(jnp.float32)

    def branch_total(partial_value):
        return sum_by_parts(partial_value.astype(jnp.bfloat16), "wt").astype(jnp.float32)

    def own_share(full):
        return lax.dynamic_slice_in_dim(full, wt_rank * share_width, share_width, 1)

    def token_tables(bounds):
        local_places = ctx_rank * block_rows + jnp.arange(block_rows, dtype=jnp.int32)
        local_docs, local_offsets = doc_info(bounds, local_places)
        key_docs, key_offsets = doc_info(bounds, all_places)
        cosine_table, sine_table = rope_tables(local_offsets, head_dim)
        return {
            "query_place": jnp.tile(local_places, groups),
            "query_doc": jnp.tile(local_docs, groups),
            "key_doc": key_docs,
            "cosine": cosine_table[:, None, :],
            "sine": sine_table[:, None, :],
        }

    def to_heads(flat):
        return (
            flat.reshape(block_rows, local_kv, groups, head_dim)
            .transpose(1, 2, 0, 3)
            .reshape(local_kv, rows_heads, head_dim)
        )

    def from_heads(stacked):
        return (
            stacked.reshape(local_kv, groups, block_rows, head_dim)
            .transpose(2, 0, 1, 3)
            .reshape(block_rows, local_heads * head_dim)
        )

    def split_kv(kv_all):
        key_rows = kv_all[:, :kv_width].reshape(seq_len, local_kv, head_dim).transpose(1, 0, 2)
        value_rows = kv_all[:, kv_width:].reshape(seq_len, local_kv, head_dim).transpose(1, 0, 2)
        return (key_rows, value_rows)

    def block_scores(queries, key_rows, tables, key_start):
        key_part = lax.dynamic_slice_in_dim(key_rows, key_start, key_block, 1)
        scores = (
            jnp.einsum("gqd,gkd->gqk", queries, key_part, preferred_element_type=jnp.float32)
            * scale_factor
        )
        key_place = key_start + jnp.arange(key_block, dtype=jnp.int32)
        key_doc = lax.dynamic_slice_in_dim(tables["key_doc"], key_start, key_block, 0)
        visible = (key_place[None, :] <= tables["query_place"][:, None]) & (
            key_doc[None, :] == tables["query_doc"][:, None]
        )
        return (jnp.where(visible[None], scores, neg_big), visible[None], key_part)

    incoming = jnp.zeros((block_rows, share_width), jnp.bfloat16)
    stored = []
    forward_shares = []
    for tick_index in range(micro_count + 1):
        micro_index = jnp.clip(tick_index - section_rank, 0, micro_count - 1)
        piece = jnp.where(section_rank == 0, inputs[min(tick_index, micro_count - 1)], incoming)
        hidden = widen_rows(piece)
        forward_tables = token_tables(doc_bounds[micro_index])
        forward_normed, forward_factor = normalize(hidden)
        attn_in = (forward_normed * params["gain_attn"]).astype(jnp.bfloat16)
        query_pre = jnp.dot(attn_in, params["query"], preferred_element_type=jnp.float32)
        key_pre = jnp.dot(attn_in, params["key"], preferred_element_type=jnp.float32)
        value_pre = jnp.dot(attn_in, params["value"], preferred_element_type=jnp.float32)
        query_rot = rotate(
            query_pre.reshape(block_rows, local_heads, head_dim),
            forward_tables["cosine"],
            forward_tables["sine"],
        ).astype(jnp.bfloat16)
        key_rot = rotate(
            key_pre.reshape(block_rows, local_kv, head_dim),
            forward_tables["cosine"],
            forward_tables["sine"],
        ).astype(jnp.bfloat16)
        kv_local = jnp.concatenate(
            [key_rot.reshape(block_rows, kv_width), value_pre.astype(jnp.bfloat16)], axis=1
        )
        forward_kv_all = gather_directly(kv_local, "ctx", 0)
        forward_key_rows, forward_value_rows = split_kv(forward_kv_all)
        forward_queries = to_heads(query_rot.reshape(block_rows, local_heads * head_dim))

        def peak_step(carry, key_start):
            running_max, running_sum = carry
            scores, visible, key_part = block_scores(
                forward_queries, forward_key_rows, forward_tables, key_start
            )
            new_max = jnp.maximum(running_max, jnp.max(scores, axis=-1))
            visible_terms = jnp.where(visible, jnp.exp(scores - new_max[..., None]), 0.0)
            return (
                (
                    new_max,
                    running_sum * jnp.exp(running_max - new_max) + jnp.sum(visible_terms, axis=-1),
                ),
                None,
            )

        initial = (
            jnp.full((local_kv, rows_heads), neg_big, jnp.float32),
            jnp.zeros((local_kv, rows_heads), jnp.float32),
        )
        (running_max, running_sum), unused = lax.scan(peak_step, initial, key_starts)
        forward_log_total = running_max + jnp.log(running_sum)

        def value_step(accumulated, key_start):
            scores, visible, key_part = block_scores(
                forward_queries, forward_key_rows, forward_tables, key_start
            )
            probabilities = jnp.where(
                visible, jnp.exp(scores - forward_log_total[..., None]), 0.0
            ).astype(jnp.bfloat16)
            value_part = lax.dynamic_slice_in_dim(forward_value_rows, key_start, key_block, 1)
            return (
                accumulated
                + jnp.einsum(
                    "gqk,gkd->gqd", probabilities, value_part, preferred_element_type=jnp.float32
                ),
                None,
            )

        attn_acc, unused = lax.scan(
            value_step, jnp.zeros((local_kv, rows_heads, head_dim), jnp.float32), key_starts
        )
        attn_out = from_heads(attn_acc.astype(jnp.bfloat16))
        hidden_mid = hidden + branch_total(
            jnp.dot(attn_out, params["out"], preferred_element_type=jnp.float32)
        )
        forward_normed_mid, forward_factor_mid = normalize(hidden_mid)
        mlp_in = (forward_normed_mid * params["gain_mlp"]).astype(jnp.bfloat16)
        gate_proj = jnp.dot(mlp_in, params["gate"], preferred_element_type=jnp.float32)
        up_proj = jnp.dot(mlp_in, params["up"], preferred_element_type=jnp.float32)
        inner = (jax.nn.silu(gate_proj) * up_proj).astype(jnp.bfloat16)
        hidden_out = hidden_mid + branch_total(
            jnp.dot(inner, params["down"], preferred_element_type=jnp.float32)
        )
        forward_saved = {
            "hidden": hidden,
            "hidden_mid": hidden_mid,
            "attn_in": attn_in,
            "mlp_in": mlp_in,
            "gate_proj": gate_proj,
            "up_proj": up_proj,
            "inner": inner,
            "queries": forward_queries,
            "kv_all": forward_kv_all,
            "log_total": forward_log_total,
            "attn_acc": attn_acc,
            "attn_out": attn_out,
        }
        hidden_out, saved = (hidden_out, forward_saved)
        sending = own_share(hidden_out).astype(jnp.bfloat16)
        forward_shares.append(sending)
        incoming = shifted_2(sending, "section", 1)
        stored.append(saved)
    stacked_saved = jax.tree.map(lambda *parts: jnp.stack(parts), *stored)
    returning = jnp.zeros((block_rows, share_width), jnp.bfloat16)
    backward_shares = []
    totals = None
    gain_totals = None
    for tick_index in range(micro_count + 1):
        micro_raw = jnp.where(section_rank == 0, tick_index - 1, tick_index)
        valid = ((micro_raw >= 0) & (micro_raw < micro_count)).astype(jnp.float32)
        micro_index = jnp.clip(micro_raw, 0, micro_count - 1)
        saved_index = jnp.clip(
            jnp.where(section_rank == 0, tick_index - 1, tick_index + 1), 0, micro_count
        )
        saved = jax.tree.map(lambda stacked_part: stacked_part[saved_index], stacked_saved)
        piece = jnp.where(section_rank == 1, cotangent[min(tick_index, micro_count - 1)], returning)
        grad_out = widen_rows(piece)
        backward_tables = token_tables(doc_bounds[micro_index])
        grad_mlp = grad_out.astype(jnp.bfloat16)
        grad_inner = times_transposed(grad_mlp, params["down"])
        sigmoid_gate = jax.nn.sigmoid(saved["gate_proj"])
        silu_gate = saved["gate_proj"] * sigmoid_gate
        grad_gate = (
            grad_inner
            * saved["up_proj"]
            * sigmoid_gate
            * (1.0 + saved["gate_proj"] * (1.0 - sigmoid_gate))
        ).astype(jnp.bfloat16)
        grad_up = (grad_inner * silu_gate).astype(jnp.bfloat16)
        grad_mlp_in = branch_total(
            times_transposed(grad_gate, params["gate"]) + times_transposed(grad_up, params["up"])
        )
        normed_mid, factor_mid = normalize(saved["hidden_mid"])
        gain_mlp_term = jnp.sum(grad_mlp_in * normed_mid, axis=0)
        grad_mid = grad_out + norm_backward(grad_mlp_in, normed_mid, factor_mid, params["gain_mlp"])
        grad_attn = grad_mid.astype(jnp.bfloat16)
        grad_heads = times_transposed(grad_attn, params["out"]).astype(jnp.bfloat16)
        grad_acc = to_heads(grad_heads)
        backward_queries = saved["queries"]
        backward_key_rows, backward_value_rows = split_kv(saved["kv_all"])
        log_total = saved["log_total"]
        row_dot = jnp.sum(grad_acc.astype(jnp.float32) * saved["attn_acc"], axis=-1)

        def grad_step(grad_query, key_start):
            scores, visible, key_part = block_scores(
                backward_queries, backward_key_rows, backward_tables, key_start
            )
            probabilities = jnp.where(visible, jnp.exp(scores - log_total[..., None]), 0.0)
            value_part = lax.dynamic_slice_in_dim(backward_value_rows, key_start, key_block, 1)
            grad_probs = jnp.einsum(
                "gqd,gkd->gqk", grad_acc, value_part, preferred_element_type=jnp.float32
            )
            grad_scores = (probabilities * (grad_probs - row_dot[..., None])).astype(jnp.bfloat16)
            grad_query = (
                grad_query
                + jnp.einsum(
                    "gqk,gkd->gqd", grad_scores, key_part, preferred_element_type=jnp.float32
                )
                * scale_factor
            )
            grad_keys = (
                jnp.einsum(
                    "gqk,gqd->kgd",
                    grad_scores,
                    backward_queries,
                    preferred_element_type=jnp.float32,
                )
                * scale_factor
            )
            grad_values = jnp.einsum(
                "gqk,gqd->kgd",
                probabilities.astype(jnp.bfloat16),
                grad_acc,
                preferred_element_type=jnp.float32,
            )
            return (
                grad_query,
                jnp.concatenate(
                    [
                        grad_keys.reshape(key_block, kv_width),
                        grad_values.reshape(key_block, kv_width),
                    ],
                    axis=1,
                ),
            )

        grad_query, kv_terms = lax.scan(
            grad_step, jnp.zeros((local_kv, rows_heads, head_dim), jnp.float32), key_starts
        )
        kv_grads = sum_at_owner(
            kv_terms.reshape(seq_len, 2 * kv_width).astype(jnp.bfloat16), "ctx", 0
        )
        grad_key = (
            unrotate(
                kv_grads[:, :kv_width].reshape(block_rows, local_kv, head_dim),
                backward_tables["cosine"],
                backward_tables["sine"],
            )
            .reshape(block_rows, kv_width)
            .astype(jnp.bfloat16)
        )
        grad_value = kv_grads[:, kv_width:].astype(jnp.bfloat16)
        grad_query_b = (
            unrotate(
                from_heads(grad_query).reshape(block_rows, local_heads, head_dim),
                backward_tables["cosine"],
                backward_tables["sine"],
            )
            .reshape(block_rows, local_heads * head_dim)
            .astype(jnp.bfloat16)
        )
        grad_attn_in = branch_total(
            times_transposed(grad_query_b, params["query"])
            + times_transposed(grad_key, params["key"])
            + times_transposed(grad_value, params["value"])
        )
        normed, factor = normalize(saved["hidden"])
        gain_attn_term = jnp.sum(grad_attn_in * normed, axis=0)
        grad_in = grad_mid + norm_backward(grad_attn_in, normed, factor, params["gain_attn"])
        pieces = {
            "attn_in": saved["attn_in"],
            "mlp_in": saved["mlp_in"],
            "inner": saved["inner"],
            "attn_out": saved["attn_out"],
            "grad_query": grad_query_b,
            "grad_key": grad_key,
            "grad_value": grad_value,
            "grad_attn": grad_attn,
            "grad_mlp": grad_mlp,
            "grad_gate": grad_gate,
            "grad_up": grad_up,
            "gain_attn": gain_attn_term,
            "gain_mlp": gain_mlp_term,
        }
        grad_in, pieces = (grad_in, pieces)
        sending = own_share(grad_in).astype(jnp.bfloat16)
        backward_shares.append(sending)
        returning = shifted_2(sending, "section", -1)
        gain_terms = (valid * pieces["gain_attn"], valid * pieces["gain_mlp"])
        grad_terms = (
            contract_rows(pieces["attn_in"], pieces["grad_query"]),
            contract_rows(pieces["attn_in"], pieces["grad_key"]),
            contract_rows(pieces["attn_in"], pieces["grad_value"]),
            contract_rows(pieces["attn_out"], pieces["grad_attn"]),
            contract_rows(pieces["mlp_in"], pieces["grad_gate"]),
            contract_rows(pieces["mlp_in"], pieces["grad_up"]),
            contract_rows(pieces["inner"], pieces["grad_mlp"]),
        )
        grad_terms = tuple((valid * single for single in grad_terms))
        if totals is None:
            totals = grad_terms
            gain_totals = gain_terms
        else:
            totals = tuple((earlier + current for earlier, current in zip(totals, grad_terms)))
            gain_totals = tuple(
                (earlier + current for earlier, current in zip(gain_totals, gain_terms))
            )
    summed = (
        *tuple(
            (
                part.astype(jnp.float32)
                for part in side_by_side(
                    (
                        totals[0].astype(jnp.bfloat16),
                        totals[1].astype(jnp.bfloat16),
                        totals[2].astype(jnp.bfloat16),
                    ),
                    "ctx",
                    0,
                    1,
                )
            )
        ),
        lax.psum_scatter(
            totals[3].astype(jnp.bfloat16), "ctx", scatter_dimension=1, tiled=True
        ).astype(jnp.float32),
        *tuple(
            (
                part.astype(jnp.float32)
                for part in side_by_side(
                    (totals[4].astype(jnp.bfloat16), totals[5].astype(jnp.bfloat16)), "ctx", 0, 1
                )
            )
        ),
        lax.psum_scatter(
            totals[6].astype(jnp.bfloat16), "ctx", scatter_dimension=1, tiled=True
        ).astype(jnp.float32),
        lax.psum_scatter(
            gain_totals[0].astype(jnp.bfloat16), "ctx", scatter_dimension=0, tiled=True
        ).astype(jnp.float32),
        lax.psum_scatter(
            gain_totals[1].astype(jnp.bfloat16), "ctx", scatter_dimension=0, tiled=True
        ).astype(jnp.float32),
    )
    weight_grads = summed[:7]
    gain_grads = summed[7:]
    boundary = jnp.stack(
        [
            jnp.where(
                section_rank == 0, backward_shares[batch_index + 1], forward_shares[batch_index + 1]
            )
            for batch_index in range(micro_count)
        ]
    )[None]
    return (
        boundary,
        gain_grads[0][None],
        weight_grads[0][None],
        weight_grads[1][None],
        weight_grads[2][None],
        weight_grads[3][None],
        gain_grads[1][None],
        weight_grads[4][None],
        weight_grads[5][None],
        weight_grads[6][None],
    )


def solution(mesh):
    return jax.shard_map(
        per_device,
        mesh=mesh,
        in_specs=(
            P(None, "ctx", "wt"),
            P(None, "ctx", "wt"),
            P(),
            P("section", None),
            P("section", None, "wt"),
            P("section", None, "wt"),
            P("section", None, "wt"),
            P("section", "wt", None),
            P("section", None),
            P("section", None, "wt"),
            P("section", None, "wt"),
            P("section", "wt", None),
        ),
        out_specs=(
            P("section", None, "ctx", "wt"),
            P("section", "ctx"),
            P("section", "ctx", "wt"),
            P("section", "ctx", "wt"),
            P("section", "ctx", "wt"),
            P("section", "wt", "ctx"),
            P("section", "ctx"),
            P("section", "ctx", "wt"),
            P("section", "ctx", "wt"),
            P("section", "wt", "ctx"),
        ),
        check_vma=False,
    )
```

profile of v0, /device:TPU:1, one launch (start us, length us, event | category | flops | bytes accessed | tf_op | source)
XLA Modules:
  0.0 1440.5 jit_solution(6135216502982829528)
XLA Ops:
  9.2 6.8 all-to-all-start.1
  21.2 7.2 all-to-all-done.1
  46.9 15.4 %while.111 = (s32[]{:T(128)}, f32[1,768]{1,0:T(1,128)S(1)}, f32[1,768]{1,0:T(1,128)S(1)}, s32[3]{0:T(128)}, s32[1536]{0:T(1024)S(1)}, /*index=5*/bf16[1,1536,64]...) while((s32[]{:T(128)}, f32[1,768]{1,0:T(1,128)S(1)}, ...), condition=%wide.region_7.8_spmd.clone, body=%wide.region_4.7_spmd.clone.sunk | while | flops 55054596 | bytes 3565250 | solution.py:278
  62.4 15.2 %while.112 = (s32[]{:T(128)}, f32[1,768,64]{1,2,0:T(8,128)S(1)}, s32[3]{0:T(128)}, s32[1536]{0:T(1024)S(1)}, bf16[1,1536,64]{2,1,0:T(8,128)(2,1)S(1)}, /*index=5...) while((s32[]{:T(128)}, f32[1,768,64]{1,2,0:T(8,128)S(1)}, ...), condition=%wide.region_9.10_spmd.clone, body=%wide.region_8.9_spmd.clone.sunk | while | flops 103907848 | bytes 902352 | solution.py:297
  83.7 25.0 %reduce-scatter.17.cloned.1.call-done = bf16[24,2048]{1,0:T(8,128)(2,1)} async-done(((bf16[192,2048]{1,0:T(8,128)(2,1)}), bf16[24,2048]{1,0:T(8,128)(2,1)}) %reduce-scatter.17.cloned.1.call-update) | async-done | bytes 98320 | tf_op jit(solution)/shard_map/reduce_scatter | solution.py:41
  108.7 17.2 %all_gather.36 = bf16[192,2048]{1,0:T(8,128)(2,1)S(1)} all-gather(bf16[24,2048]{1,0:T(8,128)(2,1)} %reduce-scatter.17.cloned.1.call-done), channel_id=1, replica_groups=mesh['section'=2,'ctx'=8,'wt'=8] {'wt'}, dimensions={0}, use_global_device_ids=true | all-gather | bytes 884736 | tf_op jit(solution)/shard_map/all_gather | solution.py:42
  135.1 27.9 %reduce-scatter.19.cloned.1.call-done = bf16[24,2048]{1,0:T(8,128)(2,1)} async-done(((bf16[192,2048]{1,0:T(8,128)(2,1)}), bf16[24,2048]{1,0:T(8,128)(2,1)}) %reduce-scatter.19.cloned.1.call-update) | async-done | bytes 98320 | tf_op jit(solution)/shard_map/reduce_scatter | solution.py:41
  163.0 17.4 %all_gather.37 = bf16[192,2048]{1,0:T(8,128)(2,1)S(1)} all-gather(bf16[24,2048]{1,0:T(8,128)(2,1)} %reduce-scatter.19.cloned.1.call-done), channel_id=1, replica_groups=mesh['section'=2,'ctx'=8,'wt'=8] {'wt'}, dimensions={0}, use_global_device_ids=true | all-gather | bytes 884736 | tf_op jit(solution)/shard_map/all_gather | solution.py:42
  193.4 12.2 all-to-all-done.3
  226.6 18.4 %while.113 = (s32[]{:T(128)}, f32[1,768]{1,0:T(1,128)S(1)}, f32[1,768]{1,0:T(1,128)S(1)}, s32[3]{0:T(128)}, s32[1536]{0:T(1024)S(1)}, /*index=5*/bf16[1,1536,64]...) while((s32[]{:T(128)}, f32[1,768]{1,0:T(1,128)S(1)}, ...), condition=%wide.region_20.21_spmd.clone, body=%wide.region_17.20_spmd.clone.sunk | while | flops 55054596 | bytes 3563202 | solution.py:278
  245.1 20.5 %while.114 = (s32[]{:T(128)}, f32[1,768,64]{1,2,0:T(8,128)}, s32[3]{0:T(128)}, s32[1536]{0:T(1024)S(1)}, bf16[1,1536,64]{2,1,0:T(8,128)(2,1)}, /*index=5*/bf16[1...) while((s32[]{:T(128)}, f32[1,768,64]{1,2,0:T(8,128)}, ...), condition=%wide.region_22.23_spmd.clone, body=%wide.region_21.22_spmd.clone.sunk | while | flops 103907848 | bytes 899280 | solution.py:297
  273.1 27.7 %reduce-scatter.21.cloned.1.call-done = bf16[24,2048]{1,0:T(8,128)(2,1)} async-done(((bf16[192,2048]{1,0:T(8,128)(2,1)}), bf16[24,2048]{1,0:T(8,128)(2,1)}) %reduce-scatter.21.cloned.1.call-update) | async-done | bytes 98320 | tf_op jit(solution)/shard_map/reduce_scatter | solution.py:41
  300.8 17.2 %all_gather.38 = bf16[192,2048]{1,0:T(8,128)(2,1)S(1)} all-gather(bf16[24,2048]{1,0:T(8,128)(2,1)} %reduce-scatter.21.cloned.1.call-done), channel_id=1, replica_groups=mesh['section'=2,'ctx'=8,'wt'=8] {'wt'}, dimensions={0}, use_global_device_ids=true | all-gather | bytes 884736 | tf_op jit(solution)/shard_map/all_gather | solution.py:42
  327.2 27.9 %reduce-scatter.23.cloned.1.call-done = bf16[24,2048]{1,0:T(8,128)(2,1)} async-done(((bf16[192,2048]{1,0:T(8,128)(2,1)}), bf16[24,2048]{1,0:T(8,128)(2,1)}) %reduce-scatter.23.cloned.1.call-update) | async-done | bytes 98320 | tf_op jit(solution)/shard_map/reduce_scatter | solution.py:41
  355.1 17.1 %all_gather.39 = bf16[192,2048]{1,0:T(8,128)(2,1)S(1)} all-gather(bf16[24,2048]{1,0:T(8,128)(2,1)} %reduce-scatter.23.cloned.1.call-done), channel_id=1, replica_groups=mesh['section'=2,'ctx'=8,'wt'=8] {'wt'}, dimensions={0}, use_global_device_ids=true | all-gather | bytes 884736 | tf_op jit(solution)/shard_map/all_gather | solution.py:42
  388.8 10.0 all-to-all-done.5
  418.8 5.3 all-to-all-start
  426.2 18.4 %while.115 = (s32[]{:T(128)}, f32[1,768]{1,0:T(1,128)S(1)}, f32[1,768]{1,0:T(1,128)S(1)}, s32[3]{0:T(128)}, s32[1536]{0:T(1024)S(1)}, /*index=5*/bf16[1,1536,64]...) while((s32[]{:T(128)}, f32[1,768]{1,0:T(1,128)S(1)}, ...), condition=%wide.region_33.34_spmd.clone, body=%wide.region_30.33_spmd.clone.sunk | while | flops 55054596 | bytes 3563202 | solution.py:278
  444.7 20.5 %while.116 = (s32[]{:T(128)}, f32[1,768,64]{1,2,0:T(8,128)}, s32[3]{0:T(128)}, s32[1536]{0:T(1024)S(1)}, bf16[1,1536,64]{2,1,0:T(8,128)(2,1)}, /*index=5*/bf16[1...) while((s32[]{:T(128)}, f32[1,768,64]{1,2,0:T(8,128)}, ...), condition=%wide.region_35.36_spmd.clone, body=%wide.region_34.35_spmd.clone.sunk | while | flops 103907848 | bytes 899280 | solution.py:297
  486.8 14.9 %reduce-scatter.25.cloned.1.call-done = bf16[24,2048]{1,0:T(8,128)(2,1)} async-done(((bf16[192,2048]{1,0:T(8,128)(2,1)}), bf16[24,2048]{1,0:T(8,128)(2,1)}) %reduce-scatter.25.cloned.1.call-update) | async-done | bytes 98320 | tf_op jit(solution)/shard_map/reduce_scatter | solution.py:41
  501.7 17.4 %all_gather.40 = bf16[192,2048]{1,0:T(8,128)(2,1)S(1)} all-gather(bf16[24,2048]{1,0:T(8,128)(2,1)} %reduce-scatter.25.cloned.1.call-done), channel_id=1, replica_groups=mesh['section'=2,'ctx'=8,'wt'=8] {'wt'}, dimensions={0}, use_global_device_ids=true | all-gather | bytes 884736 | tf_op jit(solution)/shard_map/all_gather | solution.py:42
  543.0 21.3 %reduce-scatter.27.cloned.1.call-done = bf16[24,2048]{1,0:T(8,128)(2,1)} async-done(((bf16[192,2048]{1,0:T(8,128)(2,1)}), bf16[24,2048]{1,0:T(8,128)(2,1)}) %reduce-scatter.27.cloned.1.call-update) | async-done | bytes 98320 | tf_op jit(solution)/shard_map/reduce_scatter | solution.py:41
  564.3 17.1 %all_gather.41 = bf16[192,2048]{1,0:T(8,128)(2,1)S(1)} all-gather(bf16[24,2048]{1,0:T(8,128)(2,1)} %reduce-scatter.27.cloned.1.call-done), channel_id=1, replica_groups=mesh['section'=2,'ctx'=8,'wt'=8] {'wt'}, dimensions={0}, use_global_device_ids=true | all-gather | bytes 884736 | tf_op jit(solution)/shard_map/all_gather | solution.py:42
  591.8 37.6 %while.117 = (s32[]{:T(128)}, f32[1,768,64]{1,2,0:T(8,128)}, bf16[3,512,128]{2,1,0:T(8,128)(2,1)}, s32[3]{0:T(128)}, s32[1536]{0:T(1024)S(1)}, /*index=5*/bf16[1...) while((s32[]{:T(128)}, f32[1,768,64]{1,2,0:T(8,128)}, ...), condition=%wide.region_46.47_spmd.clone, body=%wide.region_45.46_spmd.clone.sunk | while | flops 256459264 | bytes 9426685 | solution.py:415
  662.4 10.4 reduce-scatter.29.cloned.1.call-done
  672.8 17.1 %all_gather.42 = bf16[192,2048]{1,0:T(8,128)(2,1)S(1)} all-gather(bf16[24,2048]{1,0:T(8,128)(2,1)} %reduce-scatter.29.cloned.1.call-done), channel_id=1, replica_groups=mesh['section'=2,'ctx'=8,'wt'=8] {'wt'}, dimensions={0}, use_global_device_ids=true | all-gather | bytes 884736 | tf_op jit(solution)/shard_map/all_gather | solution.py:42
  694.9 6.3 collective-permute-done.2
  701.4 16.4 %all_to_all.60 = bf16[8,192,256]{2,1,0:T(8,128)(2,1)S(1)} all-to-all(bf16[8,192,256]{2,1,0:T(8,128)(2,1)S(1)} %broadcast_in_dim.219), channel_id=1, replica_groups=mesh['section'=2,'ctx'=8,'wt'=8] {'wt'}, dimensions={0} | all-to-all | bytes 1572864 | tf_op jit(solution)/shard_map/all_to_all | solution.py:22
  728.2 24.9 %reduce-scatter.31.cloned.1.call-done = bf16[24,2048]{1,0:T(8,128)(2,1)} async-done(((bf16[192,2048]{1,0:T(8,128)(2,1)}), bf16[24,2048]{1,0:T(8,128)(2,1)}) %reduce-scatter.31.cloned.1.call-update) | async-done | bytes 98320 | tf_op jit(solution)/shard_map/reduce_scatter | solution.py:41
  753.1 17.1 %all_gather.43 = bf16[192,2048]{1,0:T(8,128)(2,1)S(1)} all-gather(bf16[24,2048]{1,0:T(8,128)(2,1)} %reduce-scatter.31.cloned.1.call-done), channel_id=1, replica_groups=mesh['section'=2,'ctx'=8,'wt'=8] {'wt'}, dimensions={0}, use_global_device_ids=true | all-gather | bytes 884736 | tf_op jit(solution)/shard_map/all_gather | solution.py:42
  779.3 37.6 %while.118 = (s32[]{:T(128)}, f32[1,768,64]{1,2,0:T(8,128)}, bf16[3,512,128]{2,1,0:T(8,128)(2,1)}, s32[3]{0:T(128)}, s32[1536]{0:T(1024)S(1)}, /*index=5*/bf16[1...) while((s32[]{:T(128)}, f32[1,768,64]{1,2,0:T(8,128)}, ...), condition=%wide.region_59.60_spmd.clone, body=%wide.region_58.59_spmd.clone.sunk | while | flops 256459264 | bytes 9426685 | solution.py:415
  823.1 6.8 all-to-all-done.9
  833.6 26.9 %reduce-scatter.33.cloned.1.call-done = bf16[24,2048]{1,0:T(8,128)(2,1)} async-done(((bf16[192,2048]{1,0:T(8,128)(2,1)}), bf16[24,2048]{1,0:T(8,128)(2,1)}) %reduce-scatter.33.cloned.1.call-update) | async-done | bytes 98320 | tf_op jit(solution)/shard_map/reduce_scatter | solution.py:41
  860.5 17.1 %all_gather.44 = bf16[192,2048]{1,0:T(8,128)(2,1)S(1)} all-gather(bf16[24,2048]{1,0:T(8,128)(2,1)} %reduce-scatter.33.cloned.1.call-done), channel_id=1, replica_groups=mesh['section'=2,'ctx'=8,'wt'=8] {'wt'}, dimensions={0}, use_global_device_ids=true | all-gather | bytes 884736 | tf_op jit(solution)/shard_map/all_gather | solution.py:42
  883.3 6.3 collective-permute-done.3
  889.7 16.1 %all_to_all.61 = bf16[8,192,256]{2,1,0:T(8,128)(2,1)S(1)} all-to-all(bf16[8,192,256]{2,1,0:T(8,128)(2,1)S(1)} %broadcast_in_dim.220), channel_id=1, replica_groups=mesh['section'=2,'ctx'=8,'wt'=8] {'wt'}, dimensions={0} | all-to-all | bytes 1572864 | tf_op jit(solution)/shard_map/all_to_all | solution.py:22
  920.1 21.0 %reduce-scatter.35.cloned.1.call-done = bf16[24,2048]{1,0:T(8,128)(2,1)} async-done(((bf16[192,2048]{1,0:T(8,128)(2,1)}), bf16[24,2048]{1,0:T(8,128)(2,1)}) %reduce-scatter.35.cloned.1.call-update) | async-done | bytes 98320 | tf_op jit(solution)/shard_map/reduce_scatter | solution.py:41
  941.1 17.1 %all_gather.45 = bf16[192,2048]{1,0:T(8,128)(2,1)S(1)} all-gather(bf16[24,2048]{1,0:T(8,128)(2,1)} %reduce-scatter.35.cloned.1.call-done), channel_id=1, replica_groups=mesh['section'=2,'ctx'=8,'wt'=8] {'wt'}, dimensions={0}, use_global_device_ids=true | all-gather | bytes 884736 | tf_op jit(solution)/shard_map/all_gather | solution.py:42
  967.3 37.6 %while.119 = (s32[]{:T(128)}, f32[1,768,64]{1,2,0:T(8,128)}, bf16[3,512,128]{2,1,0:T(8,128)(2,1)}, s32[3]{0:T(128)}, s32[1536]{0:T(1024)S(1)}, /*index=5*/bf16[1...) while((s32[]{:T(128)}, f32[1,768,64]{1,2,0:T(8,128)}, ...), condition=%wide.region_72.73_spmd.clone, body=%wide.region_71.72_spmd.clone.sunk | while | flops 256459264 | bytes 9426685 | solution.py:415
  1061.2 6.0 add_convert_fusion.1
  1067.2 6.1 add_convert_fusion.2
  1073.3 8.5 pad_maximum_fusion
  1083.8 14.5 %all_gather.47 = bf16[192,2048]{1,0:T(8,128)(2,1)S(1)} all-gather(bf16[24,2048]{1,0:T(8,128)(2,1)} %reduce-scatter.39.cloned.1.call-done), channel_id=1, replica_groups=mesh['section'=2,'ctx'=8,'wt'=8] {'wt'}, dimensions={0}, use_global_device_ids=true | all-gather | bytes 884736 | tf_op jit(solution)/shard_map/all_gather | solution.py:42
  1098.3 13.7 all_gather.46
  1115.7 14.5 %all-reduce.2 = (bf16[2048]{0:T(1024)(128)(2,1)S(1)}, bf16[2048]{0:T(1024)(128)(2,1)S(1)}) all-reduce(bf16[2048]{0:T(1024)(128)(2,1)S(1)} %add_convert_fusion.4, bf16[2048]{0:T(1024)(128)(2,1)S(1)} %add_convert_fusion.3), channel_id=14, replica_groups=mesh['section'=2,'ctx'=8,'wt'=8] {'ctx'}, use_global_device_ids=true, to_apply=%region_81.82.clone | all-reduce | flops 4096 | bytes 16384
  1135.1 26.9 %reduce-scatter.41.cloned.1.call-done = bf16[256,384]{0,1:T(8,128)(2,1)} async-done(((bf16[2048,384]{0,1:T(8,128)(2,1)}), bf16[256,384]{0,1:T(8,128)(2,1)}) %reduce-scatter.41.cloned.1.call-update) | async-done | bytes 196624 | tf_op jit(solution)/shard_map/reduce_scatter | solution.py:66
  1165.2 92.0 %reduce-scatter.47.cloned.1.call-done = bf16[1024,256]{1,0:T(8,128)(2,1)} async-done(((bf16[1024,2048]{1,0:T(8,128)(2,1)}), bf16[1024,256]{1,0:T(8,128)(2,1)}) %reduce-scatter.47.cloned.1.call-update) | async-done | bytes 524304 | tf_op jit(solution)/shard_map/reduce_scatter | solution.py:513
  1259.3 170.3 %reduce-scatter.45.cloned.1.call-done = bf16[256,2048]{0,1:T(8,128)(2,1)} async-done(((bf16[2048,2048]{0,1:T(8,128)(2,1)}), bf16[256,2048]{0,1:T(8,128)(2,1)}) %reduce-scatter.45.cloned.1.call-update) | async-done | bytes 1048592 | tf_op jit(solution)/shard_map/reduce_scatter | solution.py:66
  (1085 shorter events, 522.8 us)
Async XLA Ops:
  7.2 71.3 %copy-start = (bf16[1,256,2048]{2,1,0:T(8,128)(2,1)S(1)}, bf16[1,256,2048]{2,1,0:T(8,128)(2,1)}, u32[]{:S(2)}) copy-start(bf16[1,256,2048]{2,1,0:T(8,128)(2,1)} %param.37) | copy-start | bytes 3145732
  9.2 19.2 %all-to-all-start.1 = ((bf16[8,192,256]{2,1,0:T(8,128)(2,1)}), bf16[8,192,256]{2,1,0:T(8,128)(2,1)}, u32[]{:S(2)}, u32[]{:S(2)}) async-start(bf16[8,192,256]{2,1,0:T(8,128)(2,1)} %broadcast_in_dim.207), calls=%async_computation.1 | async-start | bytes 1572864 | tf_op jit(solution)/shard_map/all_to_all | solution.py:22
  18.5 25.6 %copy-start.30 = (bf16[1,2048,256]{1,2,0:T(8,128)(2,1)}, bf16[1,2048,256]{1,2,0:T(8,128)(2,1)S(1)}, u32[]{:S(2)}) copy-start(bf16[1,2048,256]{1,2,0:T(8,128)(2,1)S(1)} %copy.219) | copy-start | bytes 3145732
  34.5 11.7 all-to-all-start.2
  39.5 69.2 %reduce-scatter.17.cloned.1.call-start = ((), (), s32[]{:S(2)}) async-start(), calls=%async_computation.28 | async-start | bytes 884736 | tf_op jit(solution)/shard_map/reduce_scatter | solution.py:41
  79.8 83.2 %reduce-scatter.19.cloned.1.call-start = ((), (), s32[]{:S(2)}) async-start(), calls=%async_computation.29 | async-start | bytes 884736 | tf_op jit(solution)/shard_map/reduce_scatter | solution.py:41
  108.7 19.0 %copy-start.1 = (bf16[1,2048,1024]{2,1,0:T(8,128)(2,1)S(1)}, bf16[1,2048,1024]{2,1,0:T(8,128)(2,1)}, u32[]{:S(2)}) copy-start(bf16[1,2048,1024]{2,1,0:T(8,128)(2,1)} %param.39) | copy-start | bytes 12582916
  127.7 412.1 %copy-start.18 = (f32[192,2048]{1,0:T(8,128)}, f32[192,2048]{1,0:T(8,128)S(1)}, u32[]{:S(2)}) copy-start(f32[192,2048]{1,0:T(8,128)S(1)} %get-tuple-element.1648) | copy-start | bytes 4718596
  180.4 6.6 collective-permute-start
  188.8 16.7 %all-to-all-start.3 = ((bf16[8,192,256]{2,1,0:T(8,128)(2,1)}), bf16[8,192,256]{2,1,0:T(8,128)(2,1)S(1)}, u32[]{:S(2)}, u32[]{:S(2)}) async-start(bf16[8,192,256]{2,1,0:T(8,128)(2,1)} %broadcast_in_dim.210), calls=%async_computation.5 | async-start | bytes 1572864 | tf_op jit(solution)/shard_map/all_to_all | solution.py:22
  211.3 13.2 all-to-all-start.4
  215.4 85.3 %reduce-scatter.21.cloned.1.call-start = ((), (), s32[]{:S(2)}) async-start(), calls=%async_computation.30 | async-start | bytes 884736 | tf_op jit(solution)/shard_map/reduce_scatter | solution.py:41
  270.2 84.8 %reduce-scatter.23.cloned.1.call-start = ((), (), s32[]{:S(2)}) async-start(), calls=%async_computation.31 | async-start | bytes 884736 | tf_op jit(solution)/shard_map/reduce_scatter | solution.py:41
  300.8 19.0 %copy-start.2 = (bf16[1,2048,1024]{2,1,0:T(8,128)(2,1)S(1)}, bf16[1,2048,1024]{2,1,0:T(8,128)(2,1)}, u32[]{:S(2)}) copy-start(bf16[1,2048,1024]{2,1,0:T(8,128)(2,1)} %param.39) | copy-start | bytes 12582916
  372.2 14.4 copy-start.168
  372.2 14.5 %copy-start.174 = (s32[192]{0:T(256)S(1)}, s32[192]{0:T(256)}, u32[]{:S(2)}) copy-start(s32[192]{0:T(256)} %get-tuple-element.1435) | copy-start | bytes 2308
  373.2 6.7 collective-permute-start.1
  381.7 17.1 %all-to-all-start.5 = ((bf16[8,192,256]{2,1,0:T(8,128)(2,1)}), bf16[8,192,256]{2,1,0:T(8,128)(2,1)S(1)}, u32[]{:S(2)}, u32[]{:S(2)}) async-start(bf16[8,192,256]{2,1,0:T(8,128)(2,1)} %broadcast_in_dim.212), calls=%async_computation.9 | async-start | bytes 1572864 | tf_op jit(solution)/shard_map/all_to_all | solution.py:22
  404.6 13.2 all-to-all-start.6
  418.8 54.0 %all-to-all-start = ((bf16[8,192,256]{2,1,0:T(8,128)(2,1)}), bf16[8,192,256]{2,1,0:T(8,128)(2,1)}, u32[]{:S(2)}, u32[]{:S(2)}) async-start(bf16[8,192,256]{2,1,0:T(8,128)(2,1)} %broadcast_in_dim.205), calls=%async_computation | async-start | bytes 1572864 | tf_op jit(solution)/shard_map/all_to_all | solution.py:22
  424.1 77.6 %reduce-scatter.25.cloned.1.call-start = ((), (), s32[]{:S(2)}) async-start(), calls=%async_computation.32 | async-start | bytes 884736 | tf_op jit(solution)/shard_map/reduce_scatter | solution.py:41
  469.8 94.5 %reduce-scatter.27.cloned.1.call-start = ((), (), s32[]{:S(2)}) async-start(), calls=%async_computation.33 | async-start | bytes 884736 | tf_op jit(solution)/shard_map/reduce_scatter | solution.py:41
  501.7 19.2 %copy-start.3 = (bf16[1,2048,1024]{2,1,0:T(8,128)(2,1)S(1)}, bf16[1,2048,1024]{2,1,0:T(8,128)(2,1)}, u32[]{:S(2)}) copy-start(bf16[1,2048,1024]{2,1,0:T(8,128)(2,1)} %param.39) | copy-start | bytes 12582916
  591.8 42.7 %copy-start.148 = (bf16[1,2048]{1,0:T(2,128)(2,1)S(1)}, bf16[1,2048]{1,0:T(2,128)(2,1)}, u32[]{:S(2)}) copy-start(bf16[1,2048]{1,0:T(2,128)(2,1)} %param.33) | copy-start | bytes 12292
  629.4 12.9 all-to-all-start.7
  634.3 38.5 %reduce-scatter.29.cloned.1.call-start = ((), (), s32[]{:S(2)}) async-start(), calls=%async_computation.34 | async-start | bytes 884736 | tf_op jit(solution)/shard_map/reduce_scatter | solution.py:41
  645.9 107.2 %reduce-scatter.31.cloned.1.call-start = ((), (), s32[]{:S(2)}) async-start(), calls=%async_computation.35 | async-start | bytes 884736 | tf_op jit(solution)/shard_map/reduce_scatter | solution.py:41
  693.6 7.6 collective-permute-start.2
  701.3 16.6 %copy-start.15 = (bf16[1,1024,2048]{2,1,0:T(8,128)(2,1)S(1)}, bf16[1,1024,2048]{2,1,0:T(8,128)(2,1)}, u32[]{:S(2)}) copy-start(bf16[1,1024,2048]{2,1,0:T(8,128)(2,1)} %param.41) | copy-start | bytes 12582916
  717.8 55.0 %copy-start.53 = (bf16[8,24,8,256]{3,2,0,1:T(8,128)(2,1)}, bf16[8,24,8,256]{3,2,0,1:T(8,128)(2,1)S(1)}, u32[]{:S(2)}) copy-start(bf16[8,24,8,256]{3,2,0,1:T(8,128)(2,1)S(1)} %copy.322) | copy-start | bytes 2359300
  816.9 13.3 copy-start.132
  816.9 13.1 all-to-all-start.9
  821.9 38.6 %reduce-scatter.33.cloned.1.call-start = ((), (), s32[]{:S(2)}) async-start(), calls=%async_computation.36 | async-start | bytes 884736 | tf_op jit(solution)/shard_map/reduce_scatter | solution.py:41
  833.5 107.6 %reduce-scatter.35.cloned.1.call-start = ((), (), s32[]{:S(2)}) async-start(), calls=%async_computation.37 | async-start | bytes 884736 | tf_op jit(solution)/shard_map/reduce_scatter | solution.py:41
  882.0 7.6 collective-permute-start.3
  889.6 16.3 %copy-start.16 = (bf16[1,1024,2048]{2,1,0:T(8,128)(2,1)S(1)}, bf16[1,1024,2048]{2,1,0:T(8,128)(2,1)}, u32[]{:S(2)}) copy-start(bf16[1,1024,2048]{2,1,0:T(8,128)(2,1)} %param.41) | copy-start | bytes 12582916
  905.9 54.9 %copy-start.49 = (bf16[8,24,8,256]{3,2,0,1:T(8,128)(2,1)}, bf16[8,24,8,256]{3,2,0,1:T(8,128)(2,1)S(1)}, u32[]{:S(2)}) copy-start(bf16[8,24,8,256]{3,2,0,1:T(8,128)(2,1)S(1)} %copy.323) | copy-start | bytes 2359300
  1004.9 12.9 all-to-all-start.11
  1009.8 74.0 %reduce-scatter.39.cloned.1.call-start = ((), (), s32[]{:S(2)}) async-start(), calls=%async_computation.39 | async-start | bytes 884736 | tf_op jit(solution)/shard_map/reduce_scatter | solution.py:41
  1014.1 84.3 %reduce-scatter.37.cloned.1.call-start = ((), (), s32[]{:S(2)}) async-start(), calls=%async_computation.38 | async-start | bytes 884736 | tf_op jit(solution)/shard_map/reduce_scatter | solution.py:41
  1021.3 112.1 %reduce-scatter.43.cloned.1.call-start = ((), (), s32[]{:S(2)}) async-start(), calls=%async_computation.41 | async-start | bytes 1179648 | tf_op jit(solution)/shard_map/reduce_scatter | solution.py:502
  1029.7 132.3 %reduce-scatter.41.cloned.1.call-start = ((), (), s32[]{:S(2)}) async-start(), calls=%async_computation.40 | async-start | bytes 1769472 | tf_op jit(solution)/shard_map/reduce_scatter | solution.py:66
  1036.3 220.8 %reduce-scatter.47.cloned.1.call-start = ((), (), s32[]{:S(2)}) async-start(), calls=%async_computation.43 | async-start | bytes 4718592 | tf_op jit(solution)/shard_map/reduce_scatter | solution.py:513
  1043.9 385.7 %reduce-scatter.45.cloned.1.call-start = ((), (), s32[]{:S(2)}) async-start(), calls=%async_computation.42 | async-start | bytes 9437184 | tf_op jit(solution)/shard_map/reduce_scatter | solution.py:66
  1081.8 16.5 %copy-start.142 = (f32[2048]{0:T(1024)S(1)}, f32[2048]{0:T(1024)}, u32[]{:S(2)}) copy-start(f32[2048]{0:T(1024)} %get-tuple-element.1399) | copy-start | bytes 24580
  1081.8 16.5 %copy-start.144 = (f32[2048]{0:T(1024)S(1)}, f32[2048]{0:T(1024)}, u32[]{:S(2)}) copy-start(f32[2048]{0:T(1024)} %get-tuple-element.1401) | copy-start | bytes 24580
  1081.8 16.5 %copy-start.146 = (f32[2048]{0:T(1024)S(1)}, f32[2048]{0:T(1024)}, u32[]{:S(2)}) copy-start(f32[2048]{0:T(1024)} %get-tuple-element.1403) | copy-start | bytes 24580
  1112.0 20.8 %copy-start.118 = (bf16[1,192,256]{2,1,0:T(8,128)(2,1)S(1)}, bf16[1,192,256]{2,1,0:T(8,128)(2,1)}, u32[]{:S(2)}) copy-start(bf16[1,192,256]{2,1,0:T(8,128)(2,1)} %get-tuple-element.1638) | copy-start | bytes 294916
  (163 other events, 465.2 us)
Sparse Core Ops, SparseCore 0:
  79.9 28.7 reduce-scatter.16
  135.3 27.6 reduce-scatter.18
  270.4 30.3 reduce-scatter.20
  327.3 27.6 reduce-scatter.22
  470.0 31.7 reduce-scatter.24
  536.6 27.6 reduce-scatter.26
  646.0 26.7 reduce-scatter.28
  726.3 26.7 reduce-scatter.30
  833.6 26.8 reduce-scatter.32
  914.4 26.6 reduce-scatter.34
  1014.2 28.1 reduce-scatter.38
  1045.3 30.2 reduce-scatter.36
  1078.6 36.6 reduce-scatter.42
  1117.5 44.4 reduce-scatter.40
  1164.3 92.8 reduce-scatter.46
  1259.4 170.0 reduce-scatter.44
where the time goes:
time: 1460 us; the launch traced here: 1440 us
  waiting for transfers between devices  578 us (40%)
  blocking collectives  247 us (17%)
  matrix products  195 us (13%)
  local copies, waits for them, and re-layouts  165 us (11%)
  other arithmetic  121 us (8%)
  starting transfers between devices  62.5 us (4%)
  loops' own time  53.9 us (4%)
  between operations  17.8 us (1%)
    reduce_scatter x12, waiting for transfers between devices, sum_by_parts(): own = lax.psum_scatter(padded, axis, scatter_dimension=0, tiled=True)  228 us
    all_gather x12, blocking collectives, sum_by_parts(): whole = lax.all_gather(own, axis, axis=0, tiled=True)  200 us
    reduce_scatter x2, waiting for transfers between devices, side_by_side(): out = lax.psum_scatter(both, axis, scatter_dimension=dim, tiled=True)  197 us
    reduce_scatter x1, waiting for transfers between devices, per_device(): lax.psum_scatter(totals[6].astype(jnp.bfloat16), 'ctx', scatter_dimension...  92 us
    unnamed x381, local copies, waits for them, and re-layouts  51 us
    dot_general x21, matrix products, contract_rows(): lax.dot_general(left, right, (((0,), (0,)), ((), ())), preferred_element_...  40.9 us
    all_to_all x7, starting transfers between devices, copy_for_each(): lax.all_to_all(jnp.broadcast_to(shard[None], (length, *shard.shape)), axi...  34.6 us
    dynamic_slice x27, local copies, waits for them, and re-layouts, per_device(): lax.scan(peak_step, initial, key_starts)  34 us
  transfers between devices with their start and end apart: 30, of which 24 were waited for; matrix products, arithmetic and copies ran while one was open for 13% of the time, Pallas kernels for 0%

commit v1 on v0

v1 whole, which is shorter than its diff:
```python
import functools

import jax
import jax.numpy as jnp
from jax import lax
from jax.experimental import pallas as pl
from jax.experimental.pallas import tpu as pltpu
from jax.sharding import PartitionSpec as P

HD = 64
eps = 1e-05
theta = 500000.0
neg_big = -1e30
MESH = pl.DeviceIdType.MESH
f32 = jnp.float32
bf16 = jnp.bfloat16
MiB = 1024 * 1024


def rope_freqs(head_width):
    index_steps = jnp.arange(head_width // 2, dtype=jnp.float32)
    inverse = theta ** (-2.0 * index_steps / head_width)
    wavelen = 2.0 * jnp.pi / inverse
    smooth = (8192.0 / wavelen - 1.0) / 3.0
    blended = (1.0 - smooth) * inverse / 32.0 + smooth * inverse
    return jnp.where(
        wavelen < 2048.0, inverse, jnp.where(wavelen > 8192.0, inverse / 32.0, blended)
    )


def doc_begins(bounds, places):
    starts = jnp.concatenate([jnp.zeros((1,), jnp.int32), bounds])
    started = places[:, None] >= starts[None, :]
    return jnp.max(jnp.where(started, starts[None, :], 0), axis=1)


def contract_rows(left, right):
    return lax.dot_general(
        left, right, (((0,), (0,)), ((), ())), preferred_element_type=jnp.float32
    )


def times_transposed(left, right):
    return lax.dot_general(
        left, right, (((1,), (1,)), ((), ())), preferred_element_type=jnp.float32
    )


def greet(peers):
    barrier = pltpu.get_barrier_semaphore()
    for peer in peers:
        pl.semaphore_signal(barrier, inc=1, device_id=peer, device_id_type=MESH)
    pl.semaphore_wait(barrier, len(peers))


def remote(src, dst, send, recv, peer):
    return pltpu.make_async_remote_copy(
        src_ref=src, dst_ref=dst, send_sem=send, recv_sem=recv, device_id=peer,
        device_id_type=MESH,
    )


FAR_FIRST = (2, 1, 3)


class WtPlace:
    def __init__(self, width):
        self.me = lax.axis_index("wt")
        self.z = self.me // 2
        self.core = self.me % 2
        self.sib = self.me + 1 - 2 * self.core
        self.width = width

    def peer(self, k):
        return lax.rem(self.z + k, 4) * 2 + self.core

    def cols(self, index):
        return pl.ds(pl.multiple_of(index * self.width, self.width), self.width)


class Gather:
    def __init__(self, place, out, sems, chunk, rows):
        self.place, self.out, self.chunk, self.rows = place, out, chunk, rows
        self.send, self.recv, self.fsend, self.frecv, self.local = sems

    def piece(self, index):
        return self.out.at[self.rows, self.place.cols(index)]

    def start(self, src):
        p, q = self.place, self.chunk
        mine = self.piece(p.me)
        self.own = pltpu.make_async_copy(src, mine, self.local.at[q])
        self.sent = [
            remote(src, mine, self.send.at[q, k], self.recv.at[q, k], {"wt": p.peer(k)})
            for k in FAR_FIRST
        ]
        self.sent.append(
            remote(src, mine, self.send.at[q, 0], self.recv.at[q, 0], {"wt": p.sib})
        )
        for copy in self.sent:
            copy.start()
        self.own.start()

    def forward(self):
        p, q = self.place, self.chunk
        self.passed = []
        for k in (1, 3, 2):
            got = self.piece(p.peer(4 - k))
            remote(got, got, self.send.at[q, k], self.recv.at[q, k], {"wt": p.sib}).wait_recv()
            copy = remote(got, got, self.fsend.at[q, k], self.frecv.at[q, k], {"wt": p.sib})
            copy.start()
            self.passed.append(copy)

    def finish(self):
        for copy in self.passed:
            copy.wait()
        self.sent[-1].wait_recv()
        for copy in self.sent:
            copy.wait_send()
        self.own.wait()


def gather_scratch(chunks):
    return [pltpu.SemaphoreType.DMA((chunks, 4)) for _ in range(4)] + [
        pltpu.SemaphoreType.DMA((chunks,))
    ]


def greet_wt(place, more=()):
    greet([{"wt": place.sib}] + [{"wt": place.peer(k)} for k in (1, 2, 3)] + list(more))


def gather_kernel(chunks, x, out, *sems):
    place = WtPlace(x.shape[1])
    greet_wt(place)
    rows = x.shape[0] // chunks
    parts = []
    for q in range(chunks):
        chunk_rows = pl.ds(q * rows, rows)
        part = Gather(place, out, sems, q, chunk_rows)
        part.start(x.at[chunk_rows])
        parts.append(part)
    for part in parts:
        part.forward()
    for part in parts:
        part.finish()


def wt_gather(x, collective_id, chunks=2):
    rows, width = x.shape
    return pl.pallas_call(
        functools.partial(gather_kernel, chunks),
        out_shape=jax.ShapeDtypeStruct((rows, 8 * width), x.dtype),
        in_specs=[pl.BlockSpec(memory_space=pltpu.VMEM)],
        out_specs=pl.BlockSpec(memory_space=pl.ANY),
        scratch_shapes=gather_scratch(chunks),
        compiler_params=pltpu.CompilerParams(
            collective_id=collective_id, has_side_effects=True, vmem_limit_bytes=32 * MiB
        ),
        name="gather_wt",
    )(x)


class Reduce:
    def __init__(self, place, part, bufs, chunk, rows):
        self.place, self.part, self.chunk, self.rows = place, part, chunk, rows
        (self.pair, self.out, self.landed, self.s1, self.r1, self.s2, self.r2) = bufs

    def start(self):
        p, q = self.place, self.chunk
        self.first = {}
        for k in (2, 1, 3, 0):
            target = lax.rem(p.z + k, 4) * 2 + 1 - p.core
            copy = remote(
                self.part.at[self.rows, p.cols(target)], self.pair.at[q, k],
                self.s1.at[q, k], self.r1.at[q, k], {"wt": p.sib},
            )
            copy.start()
            self.first[k] = copy

    def pass_on(self):
        p, q = self.place, self.chunk
        self.second = {}
        for k in (2, 1, 3):
            self.first[k].wait_recv()
            own = self.part[self.rows, p.cols(p.peer(k))]
            both = own.astype(f32) + self.pair[q, k].astype(f32)
            self.out[q, k] = both.astype(bf16)
            copy = remote(
                self.out.at[q, k], self.landed.at[q, k], self.s2.at[q, k], self.r2.at[q, k],
                {"wt": p.peer(k)},
            )
            copy.start()
            self.second[k] = copy

    def total(self):
        p, q = self.place, self.chunk
        self.first[0].wait_recv()
        total = self.part[self.rows, p.cols(p.me)].astype(f32) + self.pair[q, 0].astype(f32)
        for k in (1, 3, 2):
            self.second[k].wait_recv()
            total = total + self.landed[q, k].astype(f32)
        return total

    def finish(self):
        for copy in self.first.values():
            copy.wait_send()
        for copy in self.second.values():
            copy.wait_send()


def reduce_scratch(chunks, rows, width):
    return [pltpu.VMEM((chunks, 4, rows, width), bf16) for _ in range(3)] + [
        pltpu.SemaphoreType.DMA((chunks, 4)) for _ in range(4)
    ]


def column(line, blocks):
    eye = lax.broadcasted_iota(jnp.int32, (128, 128), 0) == lax.broadcasted_iota(
        jnp.int32, (128, 128), 1
    )
    parts = [
        jnp.sum(
            jnp.where(eye, jnp.broadcast_to(line[j : j + 1, :], (128, 128)), 0.0),
            axis=1, keepdims=True,
        )
        for j in range(blocks)
    ]
    return jnp.concatenate(parts, axis=0)


def swap_sections(src, dst, send, recv):
    return remote(src, dst, send, recv, {"section": 1 - lax.axis_index("section")})


def forward_mid_kernel(chunks, part, skip, mid, whole, agsrc, *scratch):
    bufs, sems = scratch[:7], scratch[7:]
    place = WtPlace(skip.shape[1])
    greet_wt(place)
    rows = skip.shape[0] // chunks
    spans = [pl.ds(q * rows, rows) for q in range(chunks)]
    sums = [Reduce(place, part, bufs, q, spans[q]) for q in range(chunks)]
    gathers = [Gather(place, whole, sems, q, spans[q]) for q in range(chunks)]
    for one in sums:
        one.start()
    for one in sums:
        one.pass_on()
    for q in range(chunks):
        value = skip[spans[q], :].astype(f32) + sums[q].total()
        mid[spans[q], :] = value
        agsrc[spans[q], :] = value.astype(bf16)
        gathers[q].start(agsrc.at[spans[q]])
    for one in gathers:
        one.forward()
    for one in gathers:
        one.finish()
    for one in sums:
        one.finish()


def forward_mid(part, skip, collective_id, chunks=2):
    rows, width = skip.shape
    return pl.pallas_call(
        functools.partial(forward_mid_kernel, chunks),
        out_shape=(
            jax.ShapeDtypeStruct((rows, width), f32),
            jax.ShapeDtypeStruct((rows, 8 * width), bf16),
        ),
        in_specs=[pl.BlockSpec(memory_space=pltpu.VMEM)] * 2,
        out_specs=(
            pl.BlockSpec(memory_space=pltpu.VMEM),
            pl.BlockSpec(memory_space=pl.ANY),
        ),
        scratch_shapes=[pltpu.VMEM((rows, width), bf16)]
        + reduce_scratch(chunks, rows // chunks, width)
        + gather_scratch(chunks),
        compiler_params=pltpu.CompilerParams(
            collective_id=collective_id, has_side_effects=True, vmem_limit_bytes=32 * MiB
        ),
        name="sum_mid_gather",
    )(part, skip)


def forward_pass_kernel(
    chunks, part, mid, begin, share, whole, agsrc, arrived, xsend, xrecv, *scratch
):
    bufs, sems = scratch[:7], scratch[7:]
    place = WtPlace(mid.shape[1])
    section = lax.axis_index("section")
    greet_wt(place, [{"section": 1 - section}])
    rows = mid.shape[0] // chunks
    spans = [pl.ds(q * rows, rows) for q in range(chunks)]
    sums = [Reduce(place, part, bufs, q, spans[q]) for q in range(chunks)]
    gathers = [Gather(place, whole, sems, q, spans[q]) for q in range(chunks)]
    swaps = []
    for one in sums:
        one.start()
    for one in sums:
        one.pass_on()
    for q in range(chunks):
        agsrc[spans[q], :] = (mid[spans[q], :] + sums[q].total()).astype(bf16)
        swap = swap_sections(
            agsrc.at[spans[q]], arrived.at[spans[q]], xsend.at[q], xrecv.at[q]
        )
        swap.start()
        swaps.append(swap)
    for q in range(chunks):
        swaps[q].wait_recv()
        share[spans[q], :] = jnp.where(
            section == 0, begin[spans[q], :].astype(f32), arrived[spans[q], :].astype(f32)
        ).astype(bf16)
        gathers[q].start(share.at[spans[q]])
    for one in gathers:
        one.forward()
    for one in gathers:
        one.finish()
    for one in sums:
        one.finish()
    for one in swaps:
        one.wait_send()


def forward_pass(part, mid, begin, collective_id, chunks=2):
    rows, width = mid.shape
    return pl.pallas_call(
        functools.partial(forward_pass_kernel, chunks),
        out_shape=(
            jax.ShapeDtypeStruct((rows, width), bf16),
            jax.ShapeDtypeStruct((rows, 8 * width), bf16),
        ),
        in_specs=[pl.BlockSpec(memory_space=pltpu.VMEM)] * 3,
        out_specs=(
            pl.BlockSpec(memory_space=pltpu.VMEM),
            pl.BlockSpec(memory_space=pl.ANY),
        ),
        scratch_shapes=[
            pltpu.VMEM((rows, width), bf16),
            pltpu.VMEM((rows, width), bf16),
            pltpu.SemaphoreType.DMA((chunks,)),
            pltpu.SemaphoreType.DMA((chunks,)),
        ]
        + reduce_scratch(chunks, rows // chunks, width)
        + gather_scratch(chunks),
        compiler_params=pltpu.CompilerParams(
            collective_id=collective_id, has_side_effects=True, vmem_limit_bytes=32 * MiB
        ),
        name="sum_pass_gather",
    )(part, mid, begin)


def forward_last_kernel(chunks, part, mid, result, *bufs):
    place = WtPlace(mid.shape[1])
    greet_wt(place)
    rows = mid.shape[0] // chunks
    spans = [pl.ds(q * rows, rows) for q in range(chunks)]
    sums = [Reduce(place, part, bufs, q, spans[q]) for q in range(chunks)]
    for one in sums:
        one.start()
    for one in sums:
        one.pass_on()
    for q in range(chunks):
        result[spans[q], :] = (mid[spans[q], :] + sums[q].total()).astype(bf16)
    for one in sums:
        one.finish()


def forward_last(part, mid, collective_id, chunks=2):
    rows, width = mid.shape
    return pl.pallas_call(
        functools.partial(forward_last_kernel, chunks),
        out_shape=jax.ShapeDtypeStruct((rows, width), bf16),
        in_specs=[pl.BlockSpec(memory_space=pltpu.VMEM)] * 2,
        out_specs=pl.BlockSpec(memory_space=pltpu.VMEM),
        scratch_shapes=reduce_scratch(chunks, rows // chunks, width),
        compiler_params=pltpu.CompilerParams(
            collective_id=collective_id, has_side_effects=True, vmem_limit_bytes=32 * MiB
        ),
        name="sum_last",
    )(part, mid)


def everyone(place):
    return [lax.rem(place.me + d, 8) for d in range(1, 8)]


class Lines:
    def __init__(self, place, line, slots, send, recv):
        self.line, self.slots = line, slots
        self.copies = [
            remote(line, slots.at[d], send.at[d], recv.at[d], {"wt": lax.rem(place.me + d, 8)})
            for d in range(1, 8)
        ]

    def start(self):
        for copy in self.copies:
            copy.start()

    def total(self):
        total = self.line[...]
        for d, copy in enumerate(self.copies, start=1):
            copy.wait_recv()
            total = total + self.slots[d]
        return total

    def finish(self):
        for copy in self.copies:
            copy.wait_send()


def backward_kernel(
    mode, chunks, part, line, above, own, factor, gain, *rest
):
    if mode == "mid":
        share, piece, whole, agsrc, *scratch = rest
    elif mode == "pass":
        begin, share, whole, agsrc, arrived, xsend, xrecv, *scratch = rest
    else:
        other, share, pieces, piece, gsend, grecv, *scratch = rest
    slots, lsend, lrecv, *scratch = scratch
    bufs, sems = scratch[:7], scratch[7:]
    place = WtPlace(own.shape[1])
    section = lax.axis_index("section")
    greet(
        [{"wt": peer} for peer in everyone(place)]
        + ([{"section": 1 - section}] if mode == "pass" else [])
    )
    rows = own.shape[0] // chunks
    depth = 8 * own.shape[1]
    spans = [pl.ds(q * rows, rows) for q in range(chunks)]
    sums = [Reduce(place, part, bufs, q, spans[q]) for q in range(chunks)]
    gathers = [Gather(place, whole, sems, q, spans[q]) for q in range(chunks)] if (
        mode != "last") else []
    lines = Lines(place, line, slots, lsend, lrecv)
    lines.start()
    for one in sums:
        one.start()
    for one in sums:
        one.pass_on()
    mean = column(lines.total(), own.shape[0] // 128) * (1.0 / depth)
    swaps = []
    terms = jnp.zeros((1, own.shape[1]), f32)
    for q in range(chunks):
        span = spans[q]
        total = sums[q].total()
        scale = factor[span, :]
        normed = own[span, :] * scale
        if mode != "pass":
            terms = terms + jnp.sum(total * normed, axis=0, keepdims=True)
        grad = above[span, :].astype(f32) + scale * (
            total * gain[...] - normed * mean[q * rows : (q + 1) * rows]
        )
        if mode == "mid":
            share[span, :] = grad
            agsrc[span, :] = grad.astype(bf16)
            gathers[q].start(agsrc.at[span])
        elif mode == "pass":
            agsrc[span, :] = grad.astype(bf16)
            swap = swap_sections(agsrc.at[span], arrived.at[span], xsend.at[q], xrecv.at[q])
            swap.start()
            swaps.append(swap)
        else:
            share[span, :] = grad.astype(bf16)
    if mode == "mid":
        piece[...] = jnp.broadcast_to(terms, piece.shape)
    if mode == "pass":
        for q in range(chunks):
            span = spans[q]
            swaps[q].wait_recv()
            share[span, :] = jnp.where(
                section == 1, begin[span, :].astype(f32), arrived[span, :].astype(f32)
            ).astype(bf16)
            gathers[q].start(share.at[span])
    if mode == "last":
        piece[0:8, :] = jnp.broadcast_to(terms, (8, own.shape[1]))
        piece[8:16, :] = other[...]
        copies = [
            remote(
                piece, pieces.at[place.me], gsend.at[d], grecv.at[d],
                {"wt": lax.rem(place.me + d, 8)},
            )
            for d in range(1, 8)
        ]
        for copy in copies:
            copy.start()
        pieces[place.me] = piece[...]
        for copy in copies:
            copy.wait()
    for one in gathers:
        one.forward()
    for one in gathers:
        one.finish()
    for one in sums:
        one.finish()
    for one in swaps:
        one.wait_send()
    lines.finish()


def backward_sum(mode, part, line, above, own, factor, gain, extra, collective_id, chunks=2):
    rows, width = own.shape
    vmem = pl.BlockSpec(memory_space=pltpu.VMEM)
    hbm = pl.BlockSpec(memory_space=pl.ANY)
    whole = jax.ShapeDtypeStruct((rows, 8 * width), bf16)
    if mode == "mid":
        out_shape = (
            jax.ShapeDtypeStruct((rows, width), f32),
            jax.ShapeDtypeStruct((8, width), f32),
            whole,
        )
        out_specs = (vmem, vmem, hbm)
        scratch = [pltpu.VMEM((rows, width), bf16)]
    elif mode == "pass":
        out_shape = (jax.ShapeDtypeStruct((rows, width), bf16), whole)
        out_specs = (vmem, hbm)
        scratch = [pltpu.VMEM((rows, width), bf16)] * 2 + [
            pltpu.SemaphoreType.DMA((chunks,)),
            pltpu.SemaphoreType.DMA((chunks,)),
        ]
    else:
        out_shape = (
            jax.ShapeDtypeStruct((rows, width), bf16),
            jax.ShapeDtypeStruct((8, 16, width), f32),
        )
        out_specs = (vmem, vmem)
        scratch = [
            pltpu.VMEM((16, width), f32),
            pltpu.SemaphoreType.DMA((8,)),
            pltpu.SemaphoreType.DMA((8,)),
        ]
    scratch += [
        pltpu.VMEM((8, 8, 128), f32),
        pltpu.SemaphoreType.DMA((8,)),
        pltpu.SemaphoreType.DMA((8,)),
    ]
    scratch += reduce_scratch(chunks, rows // chunks, width)
    if mode != "last":
        scratch += gather_scratch(chunks)
    operands = [part, line, above, own, factor, gain] + extra
    return pl.pallas_call(
        functools.partial(backward_kernel, mode, chunks),
        out_shape=out_shape,
        in_specs=[vmem] * len(operands),
        out_specs=out_specs,
        scratch_shapes=scratch,
        compiler_params=pltpu.CompilerParams(
            collective_id=collective_id, has_side_effects=True, vmem_limit_bytes=32 * MiB
        ),
        name="sum_back_" + mode,
    )(*operands)


def lanes(shape):
    return lax.broadcasted_iota(jnp.int32, shape, len(shape) - 1)


def turn(u, cosine, sine):
    low_half = jnp.bitwise_and(lanes(u.shape), HD - 1) < HD // 2
    turned = jnp.where(low_half, -pltpu.roll(u, 128 - HD // 2, 1), pltpu.roll(u, HD // 2, 1))
    return u * cosine + turned * sine


def turn_back(y, cosine, sine):
    low_half = jnp.bitwise_and(lanes(y.shape), HD - 1) < HD // 2
    z = y * sine
    turned = jnp.where(low_half, pltpu.roll(z, 128 - HD // 2, 1), -pltpu.roll(z, HD // 2, 1))
    return y * cosine + turned


def kv_gather_kernel(n, kv, cosine, sine, out, mine, send, recv, local):
    me = lax.axis_index("ctx")
    barrier = pltpu.get_barrier_semaphore()
    for d in range(1, n):

        @pl.when(me - d >= 0)
        def _():
            pl.semaphore_signal(
                barrier, inc=1, device_id={"ctx": me - d}, device_id_type=MESH
            )

    rows = kv.shape[0] // 2
    turned = turn(kv[...], cosine[...], sine[...]).astype(bf16)
    mine[0] = turned[:rows]
    mine[1] = turned[rows:]
    own = pltpu.make_async_copy(mine, out.at[me], local)
    own.start()

    @pl.when(me < n - 1)
    def _():
        pl.semaphore_wait(barrier, n - 1 - me)

    def copy(d):
        return remote(mine, out.at[me], send.at[d], recv.at[d], {"ctx": lax.rem(me + d, n)})

    for d in range(1, n):

        @pl.when(me + d < n)
        def _():
            copy(d).start()

    for d in range(1, n):

        @pl.when(me - d >= 0)
        def _():
            copy(d).wait_recv()

    for d in range(1, n):

        @pl.when(me + d < n)
        def _():
            copy(d).wait_send()

    own.wait()


def kv_gather(kv, cosine, sine, collective_id):
    n = 8
    rows = kv.shape[0] // 2
    return pl.pallas_call(
        functools.partial(kv_gather_kernel, n),
        out_shape=jax.ShapeDtypeStruct((n, 2, rows, 128), bf16),
        in_specs=[pl.BlockSpec(memory_space=pltpu.VMEM)] * 3,
        out_specs=pl.BlockSpec(memory_space=pl.ANY),
        scratch_shapes=[
            pltpu.VMEM((2, rows, 128), bf16),
            pltpu.SemaphoreType.DMA((n,)),
            pltpu.SemaphoreType.DMA((n,)),
            pltpu.SemaphoreType.DMA,
        ],
        compiler_params=pltpu.CompilerParams(
            collective_id=collective_id, has_side_effects=True, vmem_limit_bytes=32 * MiB
        ),
        name="gather_kv",
    )(kv, cosine, sine)


def kv_sum_kernel(n, terms, cosine, sine, out, slots, total, send, recv):
    me = lax.axis_index("ctx")
    barrier = pltpu.get_barrier_semaphore()
    for d in range(1, n):

        @pl.when(me + d < n)
        def _():
            pl.semaphore_signal(
                barrier, inc=1, device_id={"ctx": lax.rem(me + d, n)}, device_id_type=MESH
            )

    @pl.when(me > 0)
    def _():
        pl.semaphore_wait(barrier, me)

    def copy(d):
        back = lax.rem(me + n - d, n)
        return remote(terms.at[back], slots.at[d], send.at[d], recv.at[d], {"ctx": back})

    for d in range(1, n):

        @pl.when(me - d >= 0)
        def _():
            copy(d).start()

    total[...] = terms[me].astype(f32)
    for d in range(1, n):

        @pl.when(me + d < n)
        def _():
            copy(d).wait_recv()
            total[...] += slots[d].astype(f32)

    rows = terms.shape[2]
    for b in range(2):
        span = pl.ds(b * rows, rows)
        out[span, :] = turn_back(total[b], cosine[span, :], sine[span, :]).astype(bf16)
    for d in range(1, n):

        @pl.when(me - d >= 0)
        def _():
            copy(d).wait_send()


def kv_sum(terms, cosine, sine, collective_id):
    n, two, rows, width = terms.shape
    return pl.pallas_call(
        functools.partial(kv_sum_kernel, n),
        out_shape=jax.ShapeDtypeStruct((2 * rows, width), bf16),
        in_specs=[pl.BlockSpec(memory_space=pltpu.VMEM)] * 3,
        out_specs=pl.BlockSpec(memory_space=pltpu.VMEM),
        scratch_shapes=[
            pltpu.VMEM((n, 2, rows, width), bf16),
            pltpu.VMEM((2, rows, width), f32),
            pltpu.SemaphoreType.DMA((n,)),
            pltpu.SemaphoreType.DMA((n,)),
        ],
        compiler_params=pltpu.CompilerParams(
            collective_id=collective_id, has_side_effects=True, vmem_limit_bytes=32 * MiB
        ),
        name="sum_kv",
    )(terms, cosine, sine)


def visible_keys(bounds, b, key_block, me, rows, heads):
    row = lax.broadcasted_iota(jnp.int32, (1, heads * rows), 1)
    for head in range(1, heads):
        row = row - jnp.where(lanes((1, heads * rows)) >= head * rows, rows, 0)
    place = me * rows + row
    first, second = bounds[b, 0], bounds[b, 1]
    begin = jnp.where(place >= second, second, jnp.where(place >= first, first, 0))
    key = key_block * rows + lax.broadcasted_iota(jnp.int32, (rows, 1), 0)
    return (key <= place) & (key >= begin)


def stack_queries(flat, cosine, sine, b, rows, stacked):
    span = pl.ds(b * rows, rows)
    low = lanes((rows, 128)) < HD
    for pair in range(2):
        u = turn(flat[span, 128 * pair : 128 * pair + 128], cosine[span, :], sine[span, :])
        u = u.astype(bf16).astype(f32) * (HD**-0.5)
        even = jnp.where(low, u, 0.0)
        odd = jnp.where(low, pltpu.roll(u, HD, 1), 0.0)
        stacked[b, pl.ds(2 * pair * rows, rows), :] = even.astype(bf16)
        stacked[b, pl.ds((2 * pair + 1) * rows, rows), :] = odd.astype(bf16)


def attention_kernel(bounds, flat, cosine, sine, kv, mix, logs, mixed, stacked, acc):
    me = lax.axis_index("ctx")
    rows = kv.shape[2]
    heads = 4
    for b in range(2):
        stack_queries(flat, cosine, sine, b, rows, stacked)
    acc[...] = jnp.zeros_like(acc)

    def block(j, carry):
        after = []
        for b in range(2):
            peak, total = carry[2 * b : 2 * b + 2]
            keys = kv[j, b]
            scores = times_transposed(keys, stacked[b])
            scores = jnp.where(visible_keys(bounds, b, j, me, rows, heads), scores, neg_big)
            new_peak = jnp.maximum(peak, jnp.max(scores, axis=0, keepdims=True))
            shrink = jnp.exp(peak - new_peak)
            weight = jnp.exp(scores - new_peak)
            total = total * shrink + jnp.sum(weight, axis=0, keepdims=True)
            acc[b] = acc[b] * shrink + contract_rows(keys, weight.astype(bf16))
            after += [new_peak, total]
        return tuple(after)

    zero = jnp.zeros((1, heads * rows), f32)
    done = lax.fori_loop(0, me + 1, block, (zero + neg_big, zero) * 2)
    low = lanes((rows, 128)) < HD
    for b in range(2):
        peak, total = done[2 * b : 2 * b + 2]
        out = acc[b] / total
        mixed[b] = out
        logs[b] = peak + jnp.log(total)
        upright = out.T
        for pair in range(2):
            even = upright[2 * pair * rows : (2 * pair + 1) * rows]
            odd = upright[(2 * pair + 1) * rows : (2 * pair + 2) * rows]
            both = jnp.where(low, pltpu.roll(even, HD, 1), odd)
            mix[pl.ds(b * rows, rows), 128 * pair : 128 * pair + 128] = both.astype(bf16)


def attention(bounds, flat, cosine, sine, kv):
    rows = kv.shape[2]
    vmem = pl.BlockSpec(memory_space=pltpu.VMEM)
    return pl.pallas_call(
        attention_kernel,
        out_shape=(
            jax.ShapeDtypeStruct((2 * rows, 256), bf16),
            jax.ShapeDtypeStruct((2, 1, 4 * rows), f32),
            jax.ShapeDtypeStruct((2, 128, 4 * rows), f32),
        ),
        in_specs=[pl.BlockSpec(memory_space=pltpu.SMEM)] + [vmem] * 4,
        out_specs=(vmem, vmem, vmem),
        scratch_shapes=[
            pltpu.VMEM((2, 4 * rows, 128), bf16),
            pltpu.VMEM((2, 128, 4 * rows), f32),
        ],
        compiler_params=pltpu.CompilerParams(vmem_limit_bytes=40 * MiB),
        name="attention",
    )(bounds, flat, cosine, sine, kv)


def attention_back_kernel(
    bounds, flat, cosine, sine, kv, logs, mixed, grad, out, terms, stacked, grads, acc
):
    me = lax.axis_index("ctx")
    rows = kv.shape[2]
    heads = 4
    low = lanes((rows, 128)) < HD
    deltas = []
    for b in range(2):
        stack_queries(flat, cosine, sine, b, rows, stacked)
        for pair in range(2):
            u = grad[pl.ds(b * rows, rows), 128 * pair : 128 * pair + 128].astype(f32)
            even = jnp.where(low, 0.0, pltpu.roll(u, HD, 1))
            odd = jnp.where(low, 0.0, u)
            grads[b, pl.ds(2 * pair * rows, rows), :] = even.astype(bf16)
            grads[b, pl.ds((2 * pair + 1) * rows, rows), :] = odd.astype(bf16)
        deltas.append(
            jnp.sum(mixed[b] * grads[b].astype(f32).T, axis=0, keepdims=True)
        )
    acc[...] = jnp.zeros_like(acc)

    def block(j, carry):
        for b in range(2):
            keys = kv[j, b]
            scores = times_transposed(keys, stacked[b])
            probs = jnp.where(
                visible_keys(bounds, b, j, me, rows, heads), jnp.exp(scores - logs[b]), 0.0
            )
            grad_probs = times_transposed(keys, grads[b])
            grad_scores = (probs * (grad_probs - deltas[b])).astype(bf16)
            acc[b] += contract_rows(keys, grad_scores)
            terms[j, b] = (
                jnp.dot(grad_scores, stacked[b], preferred_element_type=f32)
                + jnp.dot(probs.astype(bf16), grads[b], preferred_element_type=f32)
            ).astype(bf16)
        return carry

    lax.fori_loop(0, me + 1, block, 0)
    for b in range(2):
        span = pl.ds(b * rows, rows)
        upright = acc[b].T * (HD**-0.5)
        for pair in range(2):
            even = upright[2 * pair * rows : (2 * pair + 1) * rows]
            odd = upright[(2 * pair + 1) * rows : (2 * pair + 2) * rows]
            both = jnp.where(low, even, pltpu.roll(odd, HD, 1))
            out[span, 128 * pair : 128 * pair + 128] = turn_back(
                both, cosine[span, :], sine[span, :]
            ).astype(bf16)


def attention_back(bounds, flat, cosine, sine, kv, logs, mixed, grad):
    rows = kv.shape[2]
    vmem = pl.BlockSpec(memory_space=pltpu.VMEM)
    return pl.pallas_call(
        attention_back_kernel,
        out_shape=(
            jax.ShapeDtypeStruct((2 * rows, 256), bf16),
            jax.ShapeDtypeStruct(kv.shape, bf16),
        ),
        in_specs=[pl.BlockSpec(memory_space=pltpu.SMEM)] + [vmem] * 7,
        out_specs=(vmem, vmem),
        scratch_shapes=[
            pltpu.VMEM((2, 4 * rows, 128), bf16),
            pltpu.VMEM((2, 4 * rows, 128), bf16),
            pltpu.VMEM((2, 128, 4 * rows), f32),
        ],
        compiler_params=pltpu.CompilerParams(vmem_limit_bytes=40 * MiB),
        name="attention_back",
    )(bounds, flat, cosine, sine, kv, logs, mixed, grad)


def owners_kernel(n, dims, *refs):
    count = len(dims)
    arrays, outs = refs[:count], refs[count : 2 * count]
    send, recv, local = refs[2 * count :]
    me = lax.axis_index("ctx")
    greet([{"ctx": lax.rem(me + d, n)} for d in range(1, n)])

    def cut(array, dim, owner):
        length = array.shape[dim] // n
        span = pl.ds(pl.multiple_of(owner * length, length), length)
        return array.at[span] if dim == 0 else array.at[:, span]

    copies = []
    for i in range(count):
        for d in range(1, n):
            owner = lax.rem(me + d, n)
            copy = remote(
                cut(arrays[i], dims[i], owner), outs[i].at[me], send.at[i, d], recv.at[i, d],
                {"ctx": owner},
            )
            copy.start()
            copies.append(copy)
    for i in range(count):
        own = pltpu.make_async_copy(
            cut(arrays[i], dims[i], me), outs[i].at[me], local.at[i]
        )
        own.start()
        copies.append(own)
    for copy in copies:
        copy.wait()


def to_owners(arrays, dims, collective_id):
    n = 8
    shapes = []
    for array, dim in zip(arrays, dims):
        shape = list(array.shape)
        shape[dim] //= n
        shapes.append(jax.ShapeDtypeStruct((n, *shape), array.dtype))
    hbm = pl.BlockSpec(memory_space=pl.ANY)
    return pl.pallas_call(
        functools.partial(owners_kernel, n, dims),
        out_shape=tuple(shapes),
        in_specs=[hbm] * len(arrays),
        out_specs=(hbm,) * len(arrays),
        scratch_shapes=[
            pltpu.SemaphoreType.DMA((len(arrays), n)),
            pltpu.SemaphoreType.DMA((len(arrays), n)),
            pltpu.SemaphoreType.DMA((len(arrays),)),
        ],
        compiler_params=pltpu.CompilerParams(
            collective_id=collective_id, has_side_effects=True
        ),
        name="grads_to_owners",
    )(*arrays)


def per_device(
    inputs,
    cotangent,
    doc_bounds,
    attn_gain,
    w_query,
    w_key,
    w_value,
    w_out,
    mlp_gain,
    w_gate,
    w_up,
    w_down,
):
    ctx_rank = lax.axis_index("ctx")
    wt_rank = lax.axis_index("wt")
    micro_count, block_rows, share_width = inputs.shape
    rows = micro_count * block_rows
    gain_attn = attn_gain.astype(f32)
    gain_mlp = mlp_gain.astype(f32)
    own_gain_attn = lax.dynamic_slice_in_dim(gain_attn, wt_rank * share_width, share_width, 1)
    own_gain_mlp = lax.dynamic_slice_in_dim(gain_mlp, wt_rank * share_width, share_width, 1)
    w_qkv = jnp.concatenate([w_query[0], w_key[0], w_value[0]], axis=1)
    w_o, w_g, w_u, w_d = w_out[0], w_gate[0], w_up[0], w_down[0]
    begin = inputs.reshape(rows, share_width)
    cot = cotangent.reshape(rows, share_width)

    places = ctx_rank * block_rows + jnp.arange(block_rows, dtype=jnp.int32)
    offsets = jnp.concatenate(
        [places - doc_begins(doc_bounds[b], places) for b in range(micro_count)]
    )
    angles = offsets.astype(f32)[:, None] * rope_freqs(HD)[None, :]
    cos_half, sin_half = jnp.cos(angles), jnp.sin(angles)
    cosine = jnp.concatenate([cos_half] * 4, axis=1)
    sine = jnp.concatenate([sin_half] * 4, axis=1)
    key_lane = jnp.arange(128)[None, :] < HD
    kv_cosine = jnp.where(key_lane, cosine, 1.0)
    kv_sine = jnp.where(key_lane, sine, 0.0)

    def forward(whole, share, tick):
        hidden = whole.astype(f32)
        factor = lax.rsqrt(jnp.mean(hidden * hidden, axis=-1, keepdims=True) + eps)
        attn_in = (hidden * factor * gain_attn).astype(bf16)
        pre = jnp.dot(attn_in, w_qkv, preferred_element_type=f32)
        q_pre, kv_pre = pre[:, :256], pre[:, 256:]
        kv = kv_gather(kv_pre, kv_cosine, kv_sine, 1)
        mix, logs, mixed = attention(doc_bounds, q_pre, cosine, sine, kv)
        part = jnp.dot(mix, w_o, preferred_element_type=f32).astype(bf16)
        mid, mid_whole = forward_mid(part, share, 2)
        mid_wide = mid_whole.astype(f32)
        mid_factor = lax.rsqrt(jnp.mean(mid_wide * mid_wide, axis=-1, keepdims=True) + eps)
        mlp_in = (mid_wide * mid_factor * gain_mlp).astype(bf16)
        gate = jnp.dot(mlp_in, w_g, preferred_element_type=f32)
        up = jnp.dot(mlp_in, w_u, preferred_element_type=f32)
        inner = (jax.nn.silu(gate) * up).astype(bf16)
        part = jnp.dot(inner, w_d, preferred_element_type=f32).astype(bf16)
        saved = dict(
            whole=whole, share=share, factor=factor, attn_in=attn_in, q_pre=q_pre, kv=kv,
            mix=mix, logs=logs, mixed=mixed, mid=mid, mid_whole=mid_whole,
            mid_factor=mid_factor, mlp_in=mlp_in, gate=gate, up=up, inner=inner,
        )
        return part, saved

    def line_of(part, whole, factor, gain):
        dots = jnp.sum(part * (whole.astype(f32) * factor * gain), axis=1)
        return jnp.concatenate(
            [dots.reshape(rows // 128, 128), jnp.zeros((8 - rows // 128, 128), f32)]
        )

    def backward(grad, grad_share, saved):
        gate, up = saved["gate"], saved["up"]
        grad_inner = times_transposed(grad, w_d)
        sigmoid = jax.nn.sigmoid(gate)
        grad_gate = (grad_inner * up * sigmoid * (1.0 + gate * (1.0 - sigmoid))).astype(bf16)
        grad_up = (grad_inner * gate * sigmoid).astype(bf16)
        part = times_transposed(grad_gate, w_g) + times_transposed(grad_up, w_u)
        line = line_of(part, saved["mid_whole"], saved["mid_factor"], gain_mlp)
        grad_mid, piece, grad_attn = backward_sum(
            "mid", part.astype(bf16), line, grad_share, saved["mid"], saved["mid_factor"],
            own_gain_mlp, [], 3,
        )
        grad_mix = times_transposed(grad_attn, w_o).astype(bf16)
        grad_query, terms = attention_back(
            doc_bounds, saved["q_pre"], cosine, sine, saved["kv"], saved["logs"],
            saved["mixed"], grad_mix,
        )
        grad_kv = kv_sum(terms, kv_cosine, kv_sine, 4)
        grad_pre = jnp.concatenate([grad_query, grad_kv], axis=1)
        part = times_transposed(grad_pre, w_qkv)
        line = line_of(part, saved["whole"], saved["factor"], gain_attn)
        operands = (
            part.astype(bf16), line, grad_mid, saved["share"].astype(f32), saved["factor"],
            own_gain_attn,
        )
        return operands, dict(
            grad_gate=grad_gate, grad_up=grad_up, grad_attn=grad_attn, grad_pre=grad_pre,
            piece=piece,
        )

    whole_cot = wt_gather(cot, 5)
    part, saved = forward(wt_gather(begin, 6), begin, 0)
    share, whole = forward_pass(part, saved["mid"], begin, 7)
    part, saved = forward(whole, share, 1)
    result = forward_last(part, saved["mid"], 8)

    operands, _ = backward(whole_cot, cot, saved)
    section = lax.axis_index("section")
    grad_share, grad = backward_sum("pass", *operands, [cot], 9)
    operands, kept = backward(grad, grad_share, saved)
    first_grad, pieces = backward_sum("last", *operands, [kept["piece"]], 10)

    arrays = (
        contract_rows(saved["inner"], grad).astype(bf16),
        contract_rows(saved["mlp_in"], kept["grad_gate"]).astype(bf16),
        contract_rows(saved["mlp_in"], kept["grad_up"]).astype(bf16),
        contract_rows(saved["mix"], kept["grad_attn"]).astype(bf16),
        contract_rows(saved["attn_in"], kept["grad_pre"]).astype(bf16),
        pieces.reshape(8 * 16, share_width),
    )
    sent = to_owners(arrays, (1, 0, 0, 1, 0, 0), 11)
    down, gate, up, out, pre, gains = (jnp.sum(one.astype(f32), axis=0) for one in sent)
    boundary = jnp.where(section == 0, first_grad, result)
    return (
        boundary.reshape(1, micro_count, block_rows, share_width),
        gains[0][None],
        pre[:, :256][None],
        pre[:, 256:320][None],
        pre[:, 320:][None],
        out[None],
        gains[8][None],
        gate[None],
        up[None],
        down[None],
    )


def solution(mesh):
    return jax.shard_map(
        per_device,
        mesh=mesh,
        in_specs=(
            P(None, "ctx", "wt"),
            P(None, "ctx", "wt"),
            P(),
            P("section", None),
            P("section", None, "wt"),
            P("section", None, "wt"),
            P("section", None, "wt"),
            P("section", "wt", None),
            P("section", None),
            P("section", None, "wt"),
            P("section", None, "wt"),
            P("section", "wt", None),
        ),
        out_specs=(
            P("section", None, "ctx", "wt"),
            P("section", "ctx"),
            P("section", "ctx", "wt"),
            P("section", "ctx", "wt"),
            P("section", "ctx", "wt"),
            P("section", "wt", "ctx"),
            P("section", "ctx"),
            P("section", "ctx", "wt"),
            P("section", "ctx", "wt"),
            P("section", "wt", "ctx"),
        ),
        check_vma=False,
    )
```

time: 1460 us -> 629 us (0.43)
  waiting for transfers between devices: 578 us -> 0 us
  Pallas kernels: 0 us -> 534 us
  blocking collectives: 247 us -> 0 us
  local copies, waits for them, and re-layouts: 165 us -> 9.9 us
  matrix products: 195 us -> 60.3 us
  other arithmetic: 121 us -> 17.6 us
  starting transfers between devices: 62.5 us -> 0 us
  loops' own time: 53.9 us -> 0 us
  between operations: 17.8 us -> 1.63 us
    pallas_call x0 -> x19, Pallas kernels: none -> 534 us  [the longest x1 226 us: to_owners(): pl.pallas_call(functools.partial(owners_kernel, n, dims), out_shape=tuple...]
    reduce_scatter x16 -> x0, waiting for transfers between devices: 517 us -> none  [the longest x12 228 us: sum_by_parts(): own = lax.psum_scatter(padded, axis, scatter_dimension=0, tiled=True)]
    all_gather x12 -> x0, blocking collectives: 200 us -> none  [sum_by_parts(): whole = lax.all_gather(own, axis, axis=0, tiled=True)]
    dot_general x84 -> x9, matrix products: 126 us -> 20.9 us  [the longest x2 10.9 us: forward(): part = jnp.dot(inner, w_d, preferred_element_type=f32).astype(bf16)]
    another operation x9 -> x0, loops' own time: 53.9 us -> none  [the longest x3 18.1 us: per_device(): lax.scan(grad_step, jnp.zeros((local_kv, rows_heads, head_dim), jnp.float...]
    all_to_all x10 -> x0, starting transfers between devices: 49.5 us -> none  [the longest x7 34.6 us: copy_for_each(): lax.all_to_all(jnp.broadcast_to(shard[None], (length, *shard.shape)), axi...]
    unnamed x381 -> x50, local copies, waits for them, and re-layouts: 51 us -> 5.84 us
    all_to_all x10 -> x0, waiting for transfers between devices: 43.6 us -> none  [the longest x7 29.5 us: copy_for_each(): lax.all_to_all(jnp.broadcast_to(shard[None], (length, *shard.shape)), axi...]
  transfers between devices with their start and end apart: 30 -> 0, of which waited for: 24 -> 0; matrix products, arithmetic and copies ran while one was open for 13% -> 0% of each run, Pallas kernels for 0% -> 0%
where the time goes in v1:
time: 629 us; the launch traced here: 624 us
  Pallas kernels  534 us (85%)
  matrix products  60.3 us (10%)
  other arithmetic  17.6 us (3%)
  local copies, waits for them, and re-layouts  9.9 us (2%)
    pallas_call x1, Pallas kernels, to_owners(): pl.pallas_call(functools.partial(owners_kernel, n, dims), out_shape=tuple...  226 us
    pallas_call x4, Pallas kernels, backward_sum(): pl.pallas_call(functools.partial(backward_kernel, mode, chunks), out_shap...  96.5 us
    pallas_call x2, Pallas kernels, forward_mid(): pl.pallas_call(functools.partial(forward_mid_kernel, chunks), out_shape=(...  49.2 us
    pallas_call x2, Pallas kernels, kv_sum(): pl.pallas_call(functools.partial(kv_sum_kernel, n), out_shape=jax.ShapeDt...  44.6 us
    pallas_call x2, Pallas kernels, kv_gather(): pl.pallas_call(functools.partial(kv_gather_kernel, n), out_shape=jax.Shap...  31.8 us
    pallas_call x2, Pallas kernels, wt_gather(): pl.pallas_call(functools.partial(gather_kernel, chunks), out_shape=jax.Sh...  31.1 us
    pallas_call x1, Pallas kernels, forward_pass(): pl.pallas_call(functools.partial(forward_pass_kernel, chunks), out_shape=...  28 us
    dot_general x10, matrix products, times_transposed(): lax.dot_general(left, right, (((1,), (1,)), ((), ())), preferred_element_...  21.9 us

profile of v1, /device:TPU:1, one launch (start us, length us, event | category | flops | bytes accessed | tf_op | source)
XLA Modules:
  0.0 623.5 jit_solution(13778667447038944302)
XLA Ops:
  4.4 1.2 copy.32
  6.0 16.8 %gather_wt.2 = bf16[384,2048]{1,0:T(8,128)(2,1)S(1)} custom-call(bf16[384,256]{1,0:T(8,128)(2,1)S(1)} %bitcast.96), custom_call_target="tpu_custom_call" | custom-call | tf_op jit(solution)/shard_map/gather_wt/pallas_call | solution.py:151
  23.2 1.1 fusion.56
  24.4 12.9 %gather_kv.2.kv = bf16[8,2,192,128]{3,2,1,0:T(8,128)(2,1)S(1)} custom-call(f32[384,128]{1,0:T(8,128)S(1)} %slice.45.kv, f32[384,128]{1,0:T(8,128)S(1)} %get-tuple-element.114.cosine, f32[384,128]{1,0:T(8,128)S(1)} %get-tuple-element.103.sine), custom_call_target="tpu_custom_call" | custom-call | tf_op jit(solution)/shard_map/gather_kv/pallas_call | solution.py:618
  37.3 3.3 attention.2
  41.2 24.9 %sum_mid_gather.2 = (f32[384,256]{1,0:T(8,128)S(1)}, bf16[384,2048]{1,0:T(8,128)(2,1)S(1)}) custom-call(bf16[384,2048]{1,0:T(8,128)(2,1)S(1)} %convolution_convert_fusion.5.part, bf16[384,256]{1,0:T(8,128)(2,1)S(1)} %bitcast.97), custom_call_target="tpu_custom_call" | custom-call | tf_op jit(solution)/shard_map/sum_mid_gather/pallas_call | solution.py:263
  67.2 3.0 fusion.22
  70.2 9.1 %fusion.50.part = bf16[384,2048]{1,0:T(8,128)(2,1)} fusion(bf16[1,1024,2048]{2,1,0:T(8,128)(2,1)} %param.23, f32[384,1024]{1,0:T(8,128)} %fusion.22, bf16[1,2048,1024]{2,1,0:T(8,128)(2,1)} %param.22, bf16[384,2048]{1,0:T(8,128)(2,1)} %copy-done.3, f32[2048]{0:T(1024)S(1)} %bitcast.111, f32[384]{0:T(512)S(1)} %add_rsqrt_fusion.2), kind=kOutput, calls=%fused_computation.61 | convolution fusion | flops 3227516928 | bytes 13116928 | tf_op jit(solution)/shard_map/dot_general | solution.py:966
  79.3 1.4 copy-done.4
  80.7 28.0 %sum_pass_gather.1 = (bf16[384,256]{1,0:T(8,128)(2,1)S(1)}, bf16[384,2048]{1,0:T(8,128)(2,1)S(1)}) custom-call(bf16[384,2048]{1,0:T(8,128)(2,1)S(1)} %copy-done.4, f32[384,256]{1,0:T(8,128)S(1)} %get-tuple-element.41.mid, bf16[384,256]{1,0:T(8,128)(2,1)S(1)} %bitcast.98), custom_call_target="tpu_custom_call" | custom-call | tf_op jit(solution)/shard_map/sum_pass_gather/pallas_call | solution.py:325
  109.3 1.1 fusion.74
  110.4 18.9 %gather_kv.3.kv = bf16[8,2,192,128]{3,2,1,0:T(8,128)(2,1)S(1)} custom-call(f32[384,128]{1,0:T(8,128)S(1)} %slice.47.kv, f32[384,128]{1,0:T(8,128)S(1)} %get-tuple-element.114.cosine, f32[384,128]{1,0:T(8,128)S(1)} %get-tuple-element.103.sine), custom_call_target="tpu_custom_call" | custom-call | tf_op jit(solution)/shard_map/gather_kv/pallas_call | solution.py:618
  129.3 2.3 attention.3
  132.2 24.4 %sum_mid_gather.3 = (f32[384,256]{1,0:T(8,128)S(1)}, bf16[384,2048]{1,0:T(8,128)(2,1)S(1)}) custom-call(bf16[384,2048]{1,0:T(8,128)(2,1)S(1)} %convolution_convert_fusion.4.part, bf16[384,256]{1,0:T(8,128)(2,1)S(1)} %get-tuple-element.46.skip), custom_call_target="tpu_custom_call" | custom-call | tf_op jit(solution)/shard_map/sum_mid_gather/pallas_call | solution.py:263
  157.2 1.9 fusion.20
  159.4 1.9 fusion.12
  161.2 14.2 %gather_wt.3 = bf16[384,2048]{1,0:T(8,128)(2,1)S(1)} custom-call(bf16[384,256]{1,0:T(8,128)(2,1)S(1)} %bitcast.99), custom_call_target="tpu_custom_call" | custom-call | tf_op jit(solution)/shard_map/gather_wt/pallas_call | solution.py:151
  175.5 1.8 fusion.4
  177.3 1.1 copy-done.23
  178.5 3.5 fusion.10
  182.0 5.0 fusion.42
  187.0 25.2 %sum_back_mid.2 = (f32[384,256]{1,0:T(8,128)S(1)}, f32[8,256]{1,0:T(8,128)}, bf16[384,2048]{1,0:T(8,128)(2,1)S(1)}) custom-call(bf16[384,2048]{1,0:T(8,128)(2,1)S(1)} %get-tuple-element.100.part, f32[8,128]{1,0:T(8,128)S(1)} %concatenate.46.line, bf16[384,256]{1,0:T(8,128)(2,1)S(1)} %bitcast.100, f32[384,256]{1,0:T(8,128)S(1)} %get-tuple-element.48.own.mid, ...), custom_call_target="tpu_custom_call" | custom-call | tf_op jit(solution)/shard_map/sum_back_mid/pallas_call | solution.py:539
  212.8 3.5 attention_back.2
  216.4 24.8 %sum_kv.2 = bf16[384,128]{1,0:T(8,128)(2,1)S(1)} custom-call(bf16[8,2,192,128]{3,2,1,0:T(8,128)(2,1)S(1)} %get-tuple-element.51.terms, f32[384,128]{1,0:T(8,128)S(1)} %get-tuple-element.114.cosine, f32[384,128]{1,0:T(8,128)S(1)} %get-tuple-element.103.sine), custom_call_target="tpu_custom_call" | custom-call | tf_op jit(solution)/shard_map/sum_kv/pallas_call | solution.py:682
  241.2 2.6 fusion.35
  243.8 28.0 %sum_back_pass.1 = (bf16[384,256]{1,0:T(8,128)(2,1)S(1)}, bf16[384,2048]{1,0:T(8,128)(2,1)S(1)}) custom-call(bf16[384,2048]{1,0:T(8,128)(2,1)S(1)} %get-tuple-element.98.part, f32[8,128]{1,0:T(8,128)S(1)} %concatenate.48.line, f32[384,256]{1,0:T(8,128)S(1)} %get-tuple-element.52.above, f32[384,256]{1,0:T(8,128)S(1)} %convert_element_type.143.own, ...), custom_call_target="tpu_custom_call" | custom-call | tf_op jit(solution)/shard_map/sum_back_pass/pallas_call | solution.py:539
  271.8 2.4 multiply_convert_fusion
  274.3 1.8 fusion.53.part
  276.1 14.4 %sum_last.1 = bf16[384,256]{1,0:T(8,128)(2,1)S(1)} custom-call(bf16[384,2048]{1,0:T(8,128)(2,1)S(1)} %fusion.53.part, f32[384,256]{1,0:T(8,128)S(1)} %get-tuple-element.48.own.mid), custom_call_target="tpu_custom_call" | custom-call | tf_op jit(solution)/shard_map/sum_last/pallas_call | solution.py:369
  290.5 4.3 convolution_convert_fusion.2.refs_0_
  294.8 1.8 fusion.8
  296.7 2.2 fusion.43
  298.9 24.8 %sum_back_mid.3 = (f32[384,256]{1,0:T(8,128)S(1)}, f32[8,256]{1,0:T(8,128)S(1)}, bf16[384,2048]{1,0:T(8,128)(2,1)S(1)}) custom-call(bf16[384,2048]{1,0:T(8,128)(2,1)S(1)} %get-tuple-element.96.part, f32[8,128]{1,0:T(8,128)S(1)} %concatenate.49.line, bf16[384,256]{1,0:T(8,128)(2,1)S(1)} %get-tuple-element.54.above, f32[384,256]{1,0:T(8,128)S(1)} %get-tuple-element.48.own.mid, ...), custom_call_target="tpu_custom_call" | custom-call | tf_op jit(solution)/shard_map/sum_back_mid/pallas_call | solution.py:539
  324.3 3.4 attention_back.3
  327.7 1.7 convolution_convert_fusion.6.refs_3_
  329.4 19.8 %sum_kv.3 = bf16[384,128]{1,0:T(8,128)(2,1)S(1)} custom-call(bf16[8,2,192,128]{3,2,1,0:T(8,128)(2,1)S(1)} %get-tuple-element.57.terms, f32[384,128]{1,0:T(8,128)S(1)} %get-tuple-element.114.cosine, f32[384,128]{1,0:T(8,128)S(1)} %get-tuple-element.103.sine), custom_call_target="tpu_custom_call" | custom-call | tf_op jit(solution)/shard_map/sum_kv/pallas_call | solution.py:682
  349.3 1.3 fusion.36
  350.5 2.6 convolution_convert_fusion.3.refs_4_
  353.1 18.5 %sum_back_last.1 = (bf16[384,256]{1,0:T(8,128)(2,1)S(1)}, f32[8,16,256]{2,1,0:T(8,128)S(1)}) custom-call(bf16[384,2048]{1,0:T(8,128)(2,1)S(1)} %get-tuple-element.94.part, f32[8,128]{1,0:T(8,128)S(1)} %concatenate.51.line, f32[384,256]{1,0:T(8,128)S(1)} %get-tuple-element.58.above, f32[384,256]{1,0:T(8,128)S(1)} %convert_element_type.143.own, ...), custom_call_target="tpu_custom_call" | custom-call | tf_op jit(solution)/shard_map/sum_back_last/pallas_call | solution.py:539
  372.4 4.4 convolution_convert_fusion.1.refs_1_
  376.8 4.4 convolution_convert_fusion.refs_2_
  381.3 226.0 %grads_to_owners.1 = (bf16[8,1024,256]{2,1,0:T(8,128)(2,1)}, bf16[8,256,1024]{2,1,0:T(8,128)(2,1)}, bf16[8,256,1024]{2,1,0:T(8,128)(2,1)}, bf16[8,256,256]{2,1,0...) custom-call(bf16[1024,2048]{1,0:T(8,128)(2,1)} %convolution_convert_fusion.2.refs_0_, ...), custom_call_target="tpu_custom_call" | custom-call | tf_op jit(solution)/shard_map/grads_to_owners/pallas_call | solution.py:894
  607.2 0.9 reduce_sum.134
  608.7 2.1 convert_reduce_fusion.4
  610.8 1.7 convert_reduce_fusion.3
  614.7 4.3 convert_reduce_fusion.2
  619.0 1.9 convert_reduce_fusion.1
  621.6 1.6 convert_reduce_fusion
  (90 shorter events, 13.7 us)
Async XLA Ops:
  0.6 40.0 %copy-start = (bf16[1,256,2048]{2,1,0:T(8,128)(2,1)S(1)}, bf16[1,256,2048]{2,1,0:T(8,128)(2,1)}, u32[]{:S(2)}) copy-start(bf16[1,256,2048]{2,1,0:T(8,128)(2,1)} %param.19) | copy-start | bytes 3145732
  0.7 5.0 copy-start.9
  0.7 5.3 copy-start.1
  6.0 17.2 %copy-start.14 = (bf16[1,2048,256]{2,1,0:T(8,128)(2,1)S(1)}, bf16[1,2048,256]{2,1,0:T(8,128)(2,1)}, u32[]{:S(2)}) copy-start(bf16[1,2048,256]{2,1,0:T(8,128)(2,1)} %param.16) | copy-start | bytes 3145732
  24.3 12.9 %copy-start.6 = (s32[2,2]{1,0:T(2,128)S(1)}, s32[2,2]{1,0:T(2,128)}, u32[]{:S(2)}) copy-start(s32[2,2]{1,0:T(2,128)} %bounds.7) | copy-start | bytes 52
  40.6 26.6 %copy-start.12 = (bf16[1,2048,1024]{2,1,0:T(8,128)(2,1)S(1)}, bf16[1,2048,1024]{2,1,0:T(8,128)(2,1)}, u32[]{:S(2)}) copy-start(bf16[1,2048,1024]{2,1,0:T(8,128)(2,1)} %param.21) | copy-start | bytes 12582916
  66.0 1.1 copy-start.3
  79.3 1.4 copy-start.4
  80.7 28.5 %copy-start.15 = (bf16[1,2048,256]{2,1,0:T(8,128)(2,1)S(1)}, bf16[1,2048,256]{2,1,0:T(8,128)(2,1)}, u32[]{:S(2)}) copy-start(bf16[1,2048,256]{2,1,0:T(8,128)(2,1)} %param.16) | copy-start | bytes 3145732
  131.6 25.5 %copy-start.13 = (bf16[1,2048,1024]{2,1,0:T(8,128)(2,1)S(1)}, bf16[1,2048,1024]{2,1,0:T(8,128)(2,1)}, u32[]{:S(2)}) copy-start(bf16[1,2048,1024]{2,1,0:T(8,128)(2,1)} %param.21) | copy-start | bytes 12582916
  157.2 2.2 copy-start.11
  159.3 22.7 %copy-start.19 = (f32[384,1024]{1,0:T(8,128)}, f32[384,1024]{1,0:T(8,128)S(1)}, u32[]{:S(2)}) copy-start(f32[384,1024]{1,0:T(8,128)S(1)} %fusion.20) | copy-start | bytes 4718596
  159.3 1.9 copy-start.2
  159.4 16.1 %copy-start.10 = (bf16[1,1024,2048]{2,1,0:T(8,128)(2,1)S(1)}, bf16[1,1024,2048]{2,1,0:T(8,128)(2,1)}, u32[]{:S(2)}) copy-start(bf16[1,1024,2048]{2,1,0:T(8,128)(2,1)} %param.23) | copy-start | bytes 12582916
  161.2 20.8 %copy-start.21 = (f32[384,1024]{1,0:T(8,128)}, f32[384,1024]{1,0:T(8,128)S(1)}, u32[]{:S(2)}) copy-start(f32[384,1024]{1,0:T(8,128)S(1)} %fusion.12) | copy-start | bytes 4718596
  177.3 1.2 copy-start.23
  241.2 30.7 %copy-start.22 = (f32[384,1024]{1,0:T(8,128)S(1)}, f32[384,1024]{1,0:T(8,128)}, u32[]{:S(2)}) copy-start(f32[384,1024]{1,0:T(8,128)} %copy-done.21) | copy-start | bytes 4718596
  243.8 28.1 %copy-start.20 = (f32[384,1024]{1,0:T(8,128)S(1)}, f32[384,1024]{1,0:T(8,128)}, u32[]{:S(2)}) copy-start(f32[384,1024]{1,0:T(8,128)} %copy-done.19) | copy-start | bytes 4718596
  274.3 22.4 %copy-start.17 = (bf16[384,1024]{1,0:T(8,128)(2,1)}, bf16[384,1024]{1,0:T(8,128)(2,1)S(1)}, u32[]{:S(2)}) copy-start(bf16[384,1024]{1,0:T(8,128)(2,1)S(1)} %get-tuple-element.91) | copy-start | bytes 2359300
  327.7 21.6 %copy-start.16 = (bf16[1,2048,256]{2,1,0:T(8,128)(2,1)S(1)}, bf16[1,2048,256]{2,1,0:T(8,128)(2,1)}, u32[]{:S(2)}) copy-start(bf16[1,2048,256]{2,1,0:T(8,128)(2,1)} %param.16) | copy-start | bytes 3145732
  353.1 19.3 %copy-start.18 = (bf16[384,1024]{1,0:T(8,128)(2,1)S(1)}, bf16[384,1024]{1,0:T(8,128)(2,1)}, u32[]{:S(2)}) copy-start(bf16[384,1024]{1,0:T(8,128)(2,1)} %copy-done.17) | copy-start | bytes 2359300
  371.6 5.2 copy-start.5
  614.7 4.3 copy-start.8
  619.0 2.6 copy-start.7

commit v2 on v1

--- a/solution.py
+++ b/solution.py
@@ -60,9 +60,6 @@
     )
 
 
-FAR_FIRST = (2, 1, 3)
-
-
 class WtPlace:
     def __init__(self, width):
         self.me = lax.axis_index("wt")
@@ -72,52 +69,86 @@
         self.width = width
 
     def peer(self, k):
-        return lax.rem(self.z + k, 4) * 2 + self.core
+        return lax.rem(self.z + k + 4, 4) * 2 + self.core
 
     def cols(self, index):
         return pl.ds(pl.multiple_of(index * self.width, self.width), self.width)
+
+
+def way(chunk):
+    return 1 if chunk % 2 == 0 else -1
 
 
 class Gather:
     def __init__(self, place, out, sems, chunk, rows):
         self.place, self.out, self.chunk, self.rows = place, out, chunk, rows
         self.send, self.recv, self.fsend, self.frecv, self.local = sems
+        self.s = way(chunk)
 
     def piece(self, index):
         return self.out.at[self.rows, self.place.cols(index)]
+
+    def aside(self, k):
+        p, q = self.place, self.chunk
+        got = self.piece(p.peer(-k))
+        return remote(got, got, self.fsend.at[q, k % 4], self.frecv.at[q, k % 4], {"wt": p.sib})
 
     def start(self, src):
         p, q = self.place, self.chunk
         mine = self.piece(p.me)
         self.own = pltpu.make_async_copy(src, mine, self.local.at[q])
-        self.sent = [
-            remote(src, mine, self.send.at[q, k], self.recv.at[q, k], {"wt": p.peer(k)})
-            for k in FAR_FIRST
-        ]
-        self.sent.append(
-            remote(src, mine, self.send.at[q, 0], self.recv.at[q, 0], {"wt": p.sib})
-        )
-        for copy in self.sent:
+        self.sent = []
+        for hop in (self.s, -self.s):
+            k = hop % 4
+            copy = remote(
+                src, mine, self.send.at[q, k], self.recv.at[q, k], {"wt": p.peer(hop)}
+            )
             copy.start()
+            self.sent.append(copy)
+        copy = remote(src, mine, self.fsend.at[q, 0], self.frecv.at[q, 0], {"wt": p.sib})
+        copy.start()
+        self.sent.append(copy)
         self.own.start()
 
     def forward(self):
-        p, q = self.place, self.chunk
+        p, q, s = self.place, self.chunk, self.s
         self.passed = []
-        for k in (1, 3, 2):
-            got = self.piece(p.peer(4 - k))
-            remote(got, got, self.send.at[q, k], self.recv.at[q, k], {"wt": p.sib}).wait_recv()
-            copy = remote(got, got, self.fsend.at[q, k], self.frecv.at[q, k], {"wt": p.sib})
-            copy.start()
-            self.passed.append(copy)
+        self.sent[0].wait_recv()
+        got = self.piece(p.peer(-s))
+        copy = remote(got, got, self.send.at[q, 2], self.recv.at[q, 2], {"wt": p.peer(s)})
+        copy.start()
+        self.sent.append(copy)
+        near = self.aside(s)
+        near.start()
+        self.passed.append(near)
+
+    def forward_more(self):
+        s = self.s
+        self.sent[1].wait_recv()
+        near = self.aside(-s)
+        near.start()
+        self.passed.append(near)
+        self.sent[3].wait_recv()
+        near = self.aside(2)
+        near.start()
+        self.passed.append(near)
 
     def finish(self):
         for copy in self.passed:
             copy.wait()
-        self.sent[-1].wait_recv()
+        self.sent[2].wait_recv()
         for copy in self.sent:
             copy.wait_send()
         self.own.wait()
+
+
+def gather_all(gathers):
+    for one in gathers:
+        one.forward()
+    for one in gathers:
+        one.forward_more()
+    for one in gathers:
+        one.finish()
 
 
 def gather_scratch(chunks):
@@ -127,7 +158,7 @@
 
 
 def greet_wt(place, more=()):
-    greet([{"wt": place.sib}] + [{"wt": place.peer(k)} for k in (1, 2, 3)] + list(more))
+    greet([{"wt": place.sib}] + [{"wt": place.peer(k)} for k in (1, -1)] + list(more))
 
 
 def gather_kernel(chunks, x, out, *sems):
@@ -140,13 +171,10 @@
         part = Gather(place, out, sems, q, chunk_rows)
         part.start(x.at[chunk_rows])
         parts.append(part)
-    for part in parts:
-        part.forward()
-    for part in parts:
-        part.finish()
-
-
-def wt_gather(x, collective_id, chunks=2):
+    gather_all(parts)
+
+
+def wt_gather(x, collective_id, chunks=4):
     rows, width = x.shape
     return pl.pallas_call(
         functools.partial(gather_kernel, chunks),
@@ -165,41 +193,53 @@
     def __init__(self, place, part, bufs, chunk, rows):
         self.place, self.part, self.chunk, self.rows = place, part, chunk, rows
         (self.pair, self.out, self.landed, self.s1, self.r1, self.s2, self.r2) = bufs
+        self.s = way(chunk)
 
     def start(self):
-        p, q = self.place, self.chunk
+        p, q, s = self.place, self.chunk, self.s
         self.first = {}
-        for k in (2, 1, 3, 0):
-            target = lax.rem(p.z + k, 4) * 2 + 1 - p.core
+        for k in (2, -s, s, 0):
+            target = lax.rem(p.z + k + 4, 4) * 2 + 1 - p.core
             copy = remote(
-                self.part.at[self.rows, p.cols(target)], self.pair.at[q, k],
-                self.s1.at[q, k], self.r1.at[q, k], {"wt": p.sib},
+                self.part.at[self.rows, p.cols(target)], self.pair.at[q, k % 4],
+                self.s1.at[q, k % 4], self.r1.at[q, k % 4], {"wt": p.sib},
             )
             copy.start()
             self.first[k] = copy
 
+    def both(self, k):
+        p, q = self.place, self.chunk
+        self.first[k].wait_recv()
+        own = self.part[self.rows, p.cols(p.peer(k))]
+        return own.astype(f32) + self.pair[q, k % 4].astype(f32)
+
+    def onward(self, k, value, hop):
+        p, q = self.place, self.chunk
+        self.out[q, k % 4] = value.astype(bf16)
+        copy = remote(
+            self.out.at[q, k % 4], self.landed.at[q, k % 4], self.s2.at[q, k % 4],
+            self.r2.at[q, k % 4], {"wt": p.peer(hop)},
+        )
+        copy.start()
+        self.second[k] = copy
+
     def pass_on(self):
-        p, q = self.place, self.chunk
         self.second = {}
-        for k in (2, 1, 3):
-            self.first[k].wait_recv()
-            own = self.part[self.rows, p.cols(p.peer(k))]
-            both = own.astype(f32) + self.pair[q, k].astype(f32)
-            self.out[q, k] = both.astype(bf16)
-            copy = remote(
-                self.out.at[q, k], self.landed.at[q, k], self.s2.at[q, k], self.r2.at[q, k],
-                {"wt": p.peer(k)},
-            )
-            copy.start()
-            self.second[k] = copy
+        self.onward(2, self.both(2), self.s)
+        self.onward(-self.s, self.both(-self.s), -self.s)
+
+    def pass_more(self):
+        q, s = self.chunk, self.s
+        value = self.both(s)
+        self.second[2].wait_recv()
+        self.onward(s, value + self.landed[q, 2].astype(f32), s)
 
     def total(self):
-        p, q = self.place, self.chunk
-        self.first[0].wait_recv()
-        total = self.part[self.rows, p.cols(p.me)].astype(f32) + self.pair[q, 0].astype(f32)
-        for k in (1, 3, 2):
+        q = self.chunk
+        total = self.both(0)
+        for k in (-self.s, self.s):
             self.second[k].wait_recv()
-            total = total + self.landed[q, k].astype(f32)
+            total = total + self.landed[q, k % 4].astype(f32)
         return total
 
     def finish(self):
@@ -245,20 +285,19 @@
         one.start()
     for one in sums:
         one.pass_on()
+    for one in sums:
+        one.pass_more()
     for q in range(chunks):
         value = skip[spans[q], :].astype(f32) + sums[q].total()
         mid[spans[q], :] = value
         agsrc[spans[q], :] = value.astype(bf16)
         gathers[q].start(agsrc.at[spans[q]])
-    for one in gathers:
-        one.forward()
-    for one in gathers:
-        one.finish()
+    gather_all(gathers)
     for one in sums:
         one.finish()
 
 
-def forward_mid(part, skip, collective_id, chunks=2):
+def forward_mid(part, skip, collective_id, chunks=4):
     rows, width = skip.shape
     return pl.pallas_call(
         functools.partial(forward_mid_kernel, chunks),
@@ -297,6 +336,8 @@
         one.start()
     for one in sums:
         one.pass_on()
+    for one in sums:
+        one.pass_more()
     for q in range(chunks):
         agsrc[spans[q], :] = (mid[spans[q], :] + sums[q].total()).astype(bf16)
         swap = swap_sections(
@@ -310,17 +351,14 @@
             section == 0, begin[spans[q], :].astype(f32), arrived[spans[q], :].astype(f32)
         ).astype(bf16)
         gathers[q].start(share.at[spans[q]])
-    for one in gathers:
-        one.forward()
-    for one in gathers:
-        one.finish()
+    gather_all(gathers)
     for one in sums:
         one.finish()
     for one in swaps:
         one.wait_send()
 
 
-def forward_pass(part, mid, begin, collective_id, chunks=2):
+def forward_pass(part, mid, begin, collective_id, chunks=4):
     rows, width = mid.shape
     return pl.pallas_call(
         functools.partial(forward_pass_kernel, chunks),
@@ -348,35 +386,257 @@
     )(part, mid, begin)
 
 
-def forward_last_kernel(chunks, part, mid, result, *bufs):
-    place = WtPlace(mid.shape[1])
-    greet_wt(place)
-    rows = mid.shape[0] // chunks
-    spans = [pl.ds(q * rows, rows) for q in range(chunks)]
-    sums = [Reduce(place, part, bufs, q, spans[q]) for q in range(chunks)]
-    for one in sums:
-        one.start()
-    for one in sums:
-        one.pass_on()
-    for q in range(chunks):
-        result[spans[q], :] = (mid[spans[q], :] + sums[q].total()).astype(bf16)
-    for one in sums:
-        one.finish()
-
-
-def forward_last(part, mid, collective_id, chunks=2):
-    rows, width = mid.shape
-    return pl.pallas_call(
-        functools.partial(forward_last_kernel, chunks),
-        out_shape=jax.ShapeDtypeStruct((rows, width), bf16),
-        in_specs=[pl.BlockSpec(memory_space=pltpu.VMEM)] * 2,
-        out_specs=pl.BlockSpec(memory_space=pltpu.VMEM),
-        scratch_shapes=reduce_scratch(chunks, rows // chunks, width),
-        compiler_params=pltpu.CompilerParams(
-            collective_id=collective_id, has_side_effects=True, vmem_limit_bytes=32 * MiB
-        ),
-        name="sum_last",
-    )(part, mid)
+def add_up(dst, sources, step=64):
+    def some(i, carry):
+        span = pl.ds(pl.multiple_of(i * step, step), step)
+        total = sources[0][span, :].astype(f32)
+        for source in sources[1:]:
+            total = total + source[span, :].astype(f32)
+        dst[span, :] = total.astype(dst.dtype)
+        return carry
+
+    lax.fori_loop(0, dst.shape[0] // step, some, 0)
+
+
+class CtxPlace:
+    def __init__(self):
+        self.me = lax.axis_index("ctx")
+        self.x = self.me // 2
+        self.y = self.me % 2
+
+    def at(self, k, y):
+        return lax.rem(self.x + k + 4, 4) * 2 + y
+
+    def x_peer(self, hop):
+        return {"ctx": self.at(hop, self.y)}
+
+    def y_peer(self):
+        return {"ctx": self.at(0, 1 - self.y)}
+
+    def near(self):
+        return [self.x_peer(1), self.x_peer(-1), self.y_peer()]
+
+    def all(self):
+        return [{"ctx": lax.rem(self.me + d, 8)} for d in range(1, 8)]
+
+
+class XRing:
+    def __init__(self, place, s, loaded, bufs, sems):
+        self.place, self.s, self.loaded = place, s, loaded
+        self.via, self.near, self.joined, self.summed = bufs
+        self.send, self.recv = sems
+        self.copies = {}
+
+    def go(self, i, src, dst, hop):
+        copy = remote(src, dst, self.send.at[i], self.recv.at[i], self.place.x_peer(hop))
+        copy.start()
+        self.copies[i] = copy
+
+    def start(self, k):
+        if k == 2:
+            self.go(0, self.loaded(2), self.via, self.s)
+        elif k == -self.s:
+            self.go(1, self.loaded(k), self.near, k)
+
+    def join(self):
+        self.copies[0].wait_recv()
+        add_up(self.summed, [self.loaded(self.s), self.via])
+        self.go(2, self.summed, self.joined, self.s)
+
+    def total(self, dst):
+        self.copies[1].wait_recv()
+        self.copies[2].wait_recv()
+        add_up(dst, [self.loaded(0), self.near, self.joined])
+
+    def finish(self):
+        for copy in self.copies.values():
+            copy.wait_send()
+
+
+def cut(array, dim, owner):
+    length = array.shape[dim] // 8
+    span = pl.ds(pl.multiple_of(owner * length, length), length)
+    return array.at[span] if dim == 0 else array.at[:, span]
+
+
+BLOCKS = (2, -1, 1, 0)
+
+
+class XFirst:
+    def __init__(self, place, array, dim, out, scratch):
+        self.place, self.array, self.dim, self.out = place, array, dim, out
+        (self.held, bufs, summed, self.swapped, self.lsem, sems, self.ssend, self.srecv) = scratch
+        held = self.held
+        self.rings = [
+            XRing(
+                place, way(y), lambda k, y=y: held.at[k % 4, y],
+                [bufs.at[y, j] for j in range(3)] + [summed.at[y]],
+                [sems.at[0, y], sems.at[1, y]],
+            )
+            for y in (0, 1)
+        ]
+
+    def start(self):
+        self.loads = {}
+        for k in BLOCKS:
+            for y in (0, 1):
+                copy = pltpu.make_async_copy(
+                    cut(self.array, self.dim, self.place.at(k, y)), self.held.at[k % 4, y],
+                    self.lsem.at[k % 4, y],
+                )
+                copy.start()
+                self.loads[k, y] = copy
+
+    def first(self):
+        for k in BLOCKS:
+            for y in (0, 1):
+                self.loads[k, y].wait()
+                self.rings[y].start(k)
+
+    def join(self):
+        for ring in self.rings:
+            ring.join()
+
+    def swap(self):
+        for y in (0, 1):
+            self.rings[y].total(self.swapped.at[1 + y])
+        self.across = remote(
+            self.swapped.at[1 + (1 - self.place.y)], self.swapped.at[0], self.ssend.at[0],
+            self.srecv.at[0], self.place.y_peer(),
+        )
+        self.across.start()
+
+    def total(self):
+        self.across.wait_recv()
+        add_up(self.out, [self.swapped.at[1 + self.place.y], self.swapped.at[0]])
+
+    def finish(self):
+        for ring in self.rings:
+            ring.finish()
+        self.across.wait_send()
+
+
+class YFirst:
+    def __init__(self, place, array, dim, out, scratch):
+        self.place, self.array, self.dim, self.out = place, array, dim, out
+        (self.held, bufs, summed, self.swapped, self.lsem, sems, self.ssend, self.srecv) = scratch
+        swapped = self.swapped
+        self.half = half = self.held.shape[1] // 2
+        self.rings = [
+            XRing(
+                place, way(h), lambda k, h=h: swapped.at[k % 4, pl.ds(h * half, half)],
+                [bufs.at[h, j] for j in range(3)] + [summed.at[h]],
+                [sems.at[0, h], sems.at[1, h]],
+            )
+            for h in (0, 1)
+        ]
+
+    def start(self):
+        self.swaps, self.loads = {}, {}
+        for k in BLOCKS:
+            copy = remote(
+                cut(self.array, self.dim, self.place.at(k, 1 - self.place.y)),
+                self.swapped.at[k % 4], self.ssend.at[k % 4], self.srecv.at[k % 4],
+                self.place.y_peer(),
+            )
+            copy.start()
+            self.swaps[k] = copy
+        for k in BLOCKS:
+            copy = pltpu.make_async_copy(
+                cut(self.array, self.dim, self.place.at(k, self.place.y)),
+                self.held.at[k % 4], self.lsem.at[k % 4],
+            )
+            copy.start()
+            self.loads[k] = copy
+
+    def first(self):
+        for k in BLOCKS:
+            self.loads[k].wait()
+            self.swaps[k].wait_recv()
+            block = self.swapped.at[k % 4]
+            add_up(block, [block, self.held.at[k % 4]])
+            for ring in self.rings:
+                ring.start(k)
+
+    def join(self):
+        for ring in self.rings:
+            ring.join()
+
+    def total(self):
+        for h, ring in enumerate(self.rings):
+            ring.total(self.out.at[pl.ds(h * self.half, self.half)])
+
+    def finish(self):
+        for ring in self.rings:
+            ring.finish()
+        for copy in self.swaps.values():
+            copy.wait_send()
+
+
+def ctx_scratch(shapes, dims, modes):
+    scratch = []
+    for shape, dim, mode in zip(shapes, dims, modes):
+        rows, width = owned(shape, dim)
+        if mode == "x":
+            held, ring = (4, 2, rows, width), (2, 3, rows, width)
+        else:
+            held, ring = (4, rows, width), (2, 3, rows // 2, width)
+        scratch += [
+            pltpu.VMEM(held, bf16),
+            pltpu.VMEM(ring, bf16),
+            pltpu.VMEM((2, *ring[2:]), bf16),
+            pltpu.VMEM((3 if mode == "x" else 4, rows, width), bf16),
+            pltpu.SemaphoreType.DMA((4, 2) if mode == "x" else (4,)),
+            pltpu.SemaphoreType.DMA((2, 2, 3)),
+            pltpu.SemaphoreType.DMA((4,)),
+            pltpu.SemaphoreType.DMA((4,)),
+        ]
+    return scratch
+
+
+def owned(shape, dim):
+    return tuple(n // 8 if i == dim else n for i, n in enumerate(shape))
+
+
+class CtxSums:
+    def __init__(self, place, arrays, dims, modes, outs, scratch):
+        sums = [
+            (XFirst if mode == "x" else YFirst)(
+                place, arrays[i], dims[i], outs[i], scratch[8 * i : 8 * i + 8]
+            )
+            for i, mode in enumerate(modes)
+        ]
+        self.xs = [one for one, mode in zip(sums, modes) if mode == "x"]
+        self.ys = [one for one, mode in zip(sums, modes) if mode == "y"]
+
+    def start(self):
+        for one in self.xs + self.ys:
+            one.start()
+
+    def first(self):
+        for one in self.xs:
+            one.first()
+
+    def middle(self):
+        for one in self.ys[:-1]:
+            one.first()
+            one.join()
+        for one in self.xs:
+            one.join()
+        for one in self.ys[-1:]:
+            one.first()
+
+    def later(self):
+        for one in self.xs:
+            one.swap()
+        for one in self.ys[-1:]:
+            one.join()
+
+    def end(self):
+        for one in self.ys[:-1] + self.xs + self.ys[-1:]:
+            one.total()
+        for one in self.xs + self.ys:
+            one.finish()
 
 
 def everyone(place):
@@ -407,22 +667,32 @@
             copy.wait_send()
 
 
-def backward_kernel(
-    mode, chunks, part, line, above, own, factor, gain, *rest
-):
+def backward_kernel(mode, chunks, dims, modes, part, line, above, own, factor, gain, *rest):
+    count = len(dims)
+    arrays, rest = rest[:count], rest[count:]
     if mode == "mid":
-        share, piece, whole, agsrc, *scratch = rest
+        share, piece, whole, *rest = rest
     elif mode == "pass":
-        begin, share, whole, agsrc, arrived, xsend, xrecv, *scratch = rest
+        begin, share, whole, *rest = rest
     else:
-        other, share, pieces, piece, gsend, grecv, *scratch = rest
-    slots, lsend, lrecv, *scratch = scratch
-    bufs, sems = scratch[:7], scratch[7:]
-    place = WtPlace(own.shape[1])
+        other, last_part, last_mid, share, result, gain_out, *rest = rest
+    outs, rest = rest[:count], rest[count:]
+    scratch, rest = rest[: 8 * count], rest[8 * count :]
+    if mode == "mid":
+        agsrc, *rest = rest
+    elif mode == "pass":
+        agsrc, arrived, xsend, xrecv, *rest = rest
+    else:
+        piece, pieces, gsend, grecv, gain_slots, osend, orecv, *rest = rest
+        last_bufs, rest = rest[:7], rest[7:]
+    slots, lsend, lrecv, *rest = rest
+    bufs, sems = rest[:7], rest[7:]
+    place, ctx = WtPlace(own.shape[1]), CtxPlace()
     section = lax.axis_index("section")
     greet(
         [{"wt": peer} for peer in everyone(place)]
         + ([{"section": 1 - section}] if mode == "pass" else [])
+        + (ctx.all() if mode == "last" else ctx.near() if count else [])
     )
     rows = own.shape[0] // chunks
     depth = 8 * own.shape[1]
@@ -431,11 +701,18 @@
     gathers = [Gather(place, whole, sems, q, spans[q]) for q in range(chunks)] if (
         mode != "last") else []
     lines = Lines(place, line, slots, lsend, lrecv)
+    beside = CtxSums(ctx, arrays, dims, modes, outs, scratch) if count else None
     lines.start()
     for one in sums:
         one.start()
+    if beside:
+        beside.start()
     for one in sums:
         one.pass_on()
+    if beside:
+        beside.first()
+    for one in sums:
+        one.pass_more()
     mean = column(lines.total(), own.shape[0] // 128) * (1.0 / depth)
     swaps = []
     terms = jnp.zeros((1, own.shape[1]), f32)
@@ -473,20 +750,43 @@
     if mode == "last":
         piece[0:8, :] = jnp.broadcast_to(terms, (8, own.shape[1]))
         piece[8:16, :] = other[...]
-        copies = [
+        piece_copies = [
             remote(
                 piece, pieces.at[place.me], gsend.at[d], grecv.at[d],
                 {"wt": lax.rem(place.me + d, 8)},
             )
             for d in range(1, 8)
         ]
-        for copy in copies:
+        for copy in piece_copies:
             copy.start()
+        last_sums = [Reduce(place, last_part, last_bufs, q, spans[q]) for q in range(chunks)]
+        for one in last_sums:
+            one.start()
+        for one in last_sums:
+            one.pass_on()
         pieces[place.me] = piece[...]
-        for copy in copies:
+        for copy in piece_copies:
             copy.wait()
+        owner_copies = []
+        for d in range(1, 8):
+            owner = lax.rem(ctx.me + d, 8)
+            copy = remote(
+                pieces.at[owner], gain_slots.at[d], osend.at[d], orecv.at[d], {"ctx": owner}
+            )
+            copy.start()
+            owner_copies.append(copy)
+        for one in last_sums:
+            one.pass_more()
+        for q in range(chunks):
+            span = spans[q]
+            result[span, :] = (last_mid[span, :] + last_sums[q].total()).astype(bf16)
+        sums = sums + last_sums
     for one in gathers:
         one.forward()
+    for one in gathers:
+        one.forward_more()
+    if beside:
+        beside.middle()
     for one in gathers:
         one.finish()
     for one in sums:
@@ -494,13 +794,30 @@
     for one in swaps:
         one.wait_send()
     lines.finish()
-
-
-def backward_sum(mode, part, line, above, own, factor, gain, extra, collective_id, chunks=2):
+    if beside:
+        beside.later()
+    if mode == "last":
+        total = pieces[ctx.me]
+        for d, copy in enumerate(owner_copies, start=1):
+            copy.wait_recv()
+            total = total + gain_slots[d]
+        gain_out[...] = total
+        for copy in owner_copies:
+            copy.wait_send()
+    if beside:
+        beside.end()
+
+
+def backward_sum(
+    mode, part, line, above, own, factor, gain, arrays, dims, modes, extra, collective_id,
+    chunks=4
+):
     rows, width = own.shape
     vmem = pl.BlockSpec(memory_space=pltpu.VMEM)
     hbm = pl.BlockSpec(memory_space=pl.ANY)
     whole = jax.ShapeDtypeStruct((rows, 8 * width), bf16)
+    one_sum = reduce_scratch(chunks, rows // chunks, width)
+    seven = [pltpu.SemaphoreType.DMA((8,)), pltpu.SemaphoreType.DMA((8,))]
     if mode == "mid":
         out_shape = (
             jax.ShapeDtypeStruct((rows, width), f32),
@@ -519,31 +836,27 @@
     else:
         out_shape = (
             jax.ShapeDtypeStruct((rows, width), bf16),
-            jax.ShapeDtypeStruct((8, 16, width), f32),
+            jax.ShapeDtypeStruct((rows, width), bf16),
+            jax.ShapeDtypeStruct((16, width), f32),
         )
-        out_specs = (vmem, vmem)
-        scratch = [
-            pltpu.VMEM((16, width), f32),
-            pltpu.SemaphoreType.DMA((8,)),
-            pltpu.SemaphoreType.DMA((8,)),
-        ]
-    scratch += [
-        pltpu.VMEM((8, 8, 128), f32),
-        pltpu.SemaphoreType.DMA((8,)),
-        pltpu.SemaphoreType.DMA((8,)),
-    ]
-    scratch += reduce_scratch(chunks, rows // chunks, width)
+        out_specs = (vmem, vmem, vmem)
+        scratch = [pltpu.VMEM((16, width), f32), pltpu.VMEM((8, 16, width), f32)]
+        scratch += seven + [pltpu.VMEM((8, 16, width), f32)] + seven + one_sum
+    scratch += [pltpu.VMEM((8, 8, 128), f32)] + seven + one_sum
     if mode != "last":
         scratch += gather_scratch(chunks)
-    operands = [part, line, above, own, factor, gain] + extra
+    operands = [part, line, above, own, factor, gain] + arrays + extra
+    shapes = [array.shape for array in arrays]
     return pl.pallas_call(
-        functools.partial(backward_kernel, mode, chunks),
-        out_shape=out_shape,
-        in_specs=[vmem] * len(operands),
-        out_specs=out_specs,
-        scratch_shapes=scratch,
+        functools.partial(backward_kernel, mode, chunks, dims, modes),
+        out_shape=out_shape
+        + tuple(jax.ShapeDtypeStruct(owned(*one), f32) for one in zip(shapes, dims)),
+        in_specs=[vmem] * 6 + [hbm] * len(arrays) + [vmem] * len(extra),
+        out_specs=out_specs + (vmem,) * len(arrays),
+        scratch_shapes=ctx_scratch(shapes, dims, modes) + scratch,
         compiler_params=pltpu.CompilerParams(
-            collective_id=collective_id, has_side_effects=True, vmem_limit_bytes=32 * MiB
+            collective_id=collective_id, has_side_effects=True,
+            vmem_limit_bytes=(56 if arrays else 32) * MiB,
         ),
         name="sum_back_" + mode,
     )(*operands)
@@ -849,63 +1162,6 @@
         compiler_params=pltpu.CompilerParams(vmem_limit_bytes=40 * MiB),
         name="attention_back",
     )(bounds, flat, cosine, sine, kv, logs, mixed, grad)
-
-
-def owners_kernel(n, dims, *refs):
-    count = len(dims)
-    arrays, outs = refs[:count], refs[count : 2 * count]
-    send, recv, local = refs[2 * count :]
-    me = lax.axis_index("ctx")
-    greet([{"ctx": lax.rem(me + d, n)} for d in range(1, n)])
-
-    def cut(array, dim, owner):
-        length = array.shape[dim] // n
-        span = pl.ds(pl.multiple_of(owner * length, length), length)
-        return array.at[span] if dim == 0 else array.at[:, span]
-
-    copies = []
-    for i in range(count):
-        for d in range(1, n):
-            owner = lax.rem(me + d, n)
-            copy = remote(
-                cut(arrays[i], dims[i], owner), outs[i].at[me], send.at[i, d], recv.at[i, d],
-                {"ctx": owner},
-            )
-            copy.start()
-            copies.append(copy)
-    for i in range(count):
-        own = pltpu.make_async_copy(
-            cut(arrays[i], dims[i], me), outs[i].at[me], local.at[i]
-        )
-        own.start()
-        copies.append(own)
-    for copy in copies:
-        copy.wait()
-
-
-def to_owners(arrays, dims, collective_id):
-    n = 8
-    shapes = []
-    for array, dim in zip(arrays, dims):
-        shape = list(array.shape)
-        shape[dim] //= n
-        shapes.append(jax.ShapeDtypeStruct((n, *shape), array.dtype))
-    hbm = pl.BlockSpec(memory_space=pl.ANY)
-    return pl.pallas_call(
-        functools.partial(owners_kernel, n, dims),
-        out_shape=tuple(shapes),
-        in_specs=[hbm] * len(arrays),
-        out_specs=(hbm,) * len(arrays),
-        scratch_shapes=[
-            pltpu.SemaphoreType.DMA((len(arrays), n)),
-            pltpu.SemaphoreType.DMA((len(arrays), n)),
-            pltpu.SemaphoreType.DMA((len(arrays),)),
-        ],
-        compiler_params=pltpu.CompilerParams(
-            collective_id=collective_id, has_side_effects=True
-        ),
-        name="grads_to_owners",
-    )(*arrays)
 
 
 def per_device(
@@ -962,7 +1218,7 @@
         mlp_in = (mid_wide * mid_factor * gain_mlp).astype(bf16)
         gate = jnp.dot(mlp_in, w_g, preferred_element_type=f32)
         up = jnp.dot(mlp_in, w_u, preferred_element_type=f32)
-        inner = (jax.nn.silu(gate) * up).astype(bf16)
+        inner = lax.optimization_barrier((jax.nn.silu(gate) * up).astype(bf16))
         part = jnp.dot(inner, w_d, preferred_element_type=f32).astype(bf16)
         saved = dict(
             whole=whole, share=share, factor=factor, attn_in=attn_in, q_pre=q_pre, kv=kv,
@@ -977,7 +1233,7 @@
             [dots.reshape(rows // 128, 128), jnp.zeros((8 - rows // 128, 128), f32)]
         )
 
-    def backward(grad, grad_share, saved):
+    def backward(grad, grad_share, saved, last):
         gate, up = saved["gate"], saved["up"]
         grad_inner = times_transposed(grad, w_d)
         sigmoid = jax.nn.sigmoid(gate)
@@ -985,9 +1241,17 @@
         grad_up = (grad_inner * gate * sigmoid).astype(bf16)
         part = times_transposed(grad_gate, w_g) + times_transposed(grad_up, w_u)
         line = line_of(part, saved["mid_whole"], saved["mid_factor"], gain_mlp)
-        grad_mid, piece, grad_attn = backward_sum(
+        arrays = []
+        if last:
+            half = saved["inner"].shape[1] // 2
+            arrays = [
+                contract_rows(saved["inner"][:, :half], grad).astype(bf16),
+                contract_rows(saved["inner"][:, half:], grad).astype(bf16),
+            ]
+        grad_mid, piece, grad_attn, *down = backward_sum(
             "mid", part.astype(bf16), line, grad_share, saved["mid"], saved["mid_factor"],
-            own_gain_mlp, [], 3,
+            own_gain_mlp, arrays, (1, 1)[: len(arrays)], ("x", "y")[: len(arrays)], [],
+            8 if last else 3,
         )
         grad_mix = times_transposed(grad_attn, w_o).astype(bf16)
         grad_query, terms = attention_back(
@@ -1004,31 +1268,30 @@
         )
         return operands, dict(
             grad_gate=grad_gate, grad_up=grad_up, grad_attn=grad_attn, grad_pre=grad_pre,
-            piece=piece,
+            piece=piece, down=down,
         )
 
-    whole_cot = wt_gather(cot, 5)
+    whole_cot = lax.all_gather(cot, "wt", axis=1, tiled=True)
     part, saved = forward(wt_gather(begin, 6), begin, 0)
     share, whole = forward_pass(part, saved["mid"], begin, 7)
     part, saved = forward(whole, share, 1)
-    result = forward_last(part, saved["mid"], 8)
-
-    operands, _ = backward(whole_cot, cot, saved)
+    last_part = part
+
+    operands, _ = backward(whole_cot, cot, saved, False)
     section = lax.axis_index("section")
-    grad_share, grad = backward_sum("pass", *operands, [cot], 9)
-    operands, kept = backward(grad, grad_share, saved)
-    first_grad, pieces = backward_sum("last", *operands, [kept["piece"]], 10)
-
-    arrays = (
-        contract_rows(saved["inner"], grad).astype(bf16),
+    grad_share, grad = backward_sum("pass", *operands, [], (), (), [cot], 9)
+    operands, kept = backward(grad, grad_share, saved, True)
+    arrays = [
+        contract_rows(saved["mlp_in"], kept["grad_up"]).astype(bf16),
+        contract_rows(saved["attn_in"], kept["grad_pre"]).astype(bf16),
+        contract_rows(saved["mix"], kept["grad_attn"]).astype(bf16),
         contract_rows(saved["mlp_in"], kept["grad_gate"]).astype(bf16),
-        contract_rows(saved["mlp_in"], kept["grad_up"]).astype(bf16),
-        contract_rows(saved["mix"], kept["grad_attn"]).astype(bf16),
-        contract_rows(saved["attn_in"], kept["grad_pre"]).astype(bf16),
-        pieces.reshape(8 * 16, share_width),
+    ]
+    first_grad, result, gains, up, pre, out, gate = backward_sum(
+        "last", *operands, arrays, (0, 0, 1, 0), ("x", "x", "y", "y"),
+        [kept["piece"], last_part, saved["mid"]], 10,
     )
-    sent = to_owners(arrays, (1, 0, 0, 1, 0, 0), 11)
-    down, gate, up, out, pre, gains = (jnp.sum(one.astype(f32), axis=0) for one in sent)
+    down = jnp.concatenate(kept["down"], axis=0)
     boundary = jnp.where(section == 0, first_grad, result)
     return (
         boundary.reshape(1, micro_count, block_rows, share_width),

time: 629 us -> 467 us (0.74)
  Pallas kernels: 534 us -> 355 us
  between operations: 1.63 us -> 15.3 us
  other arithmetic: 17.6 us -> 4.85 us
  local copies, waits for them, and re-layouts: 9.9 us -> 20.2 us
    pallas_call x6 -> x4, Pallas kernels: 337 us -> 182 us  [backward_sum(): pl.pallas_call(functools.partial(backward_kernel, mode, chunks, dims, mod...]
    pallas_call x2 -> x1, Pallas kernels: 31.1 us -> 16 us  [wt_gather(): pl.pallas_call(functools.partial(gather_kernel, chunks), out_shape=jax.Sh...]
    reduce_sum x6 -> x0, other arithmetic: 12.4 us -> none  [per_device(): jnp.sum(one.astype(f32), axis=0)]
    dot_general x5 -> x6, matrix products: 17.5 us -> 18.5 us  [contract_rows(): lax.dot_general(left, right, (((0,), (0,)), ((), ())), preferred_element_...]
  transfers between devices with their start and end apart: 0 -> 1, of which waited for: 0 -> 0; matrix products, arithmetic and copies ran while one was open for 0% -> 6% of each run, Pallas kernels for 0% -> 27%
where the time goes in v2:
time: 467 us; the launch traced here: 459 us
  Pallas kernels  355 us (76%)
  matrix products  63.1 us (14%)
  local copies, waits for them, and re-layouts  20.2 us (4%)
  between operations  15.3 us (3%)
  other arithmetic  4.85 us (1%)
    pallas_call x4, Pallas kernels, backward_sum(): pl.pallas_call(functools.partial(backward_kernel, mode, chunks, dims, mod...  182 us
    pallas_call x2, Pallas kernels, forward_mid(): pl.pallas_call(functools.partial(forward_mid_kernel, chunks), out_shape=(...  44.8 us
    pallas_call x2, Pallas kernels, kv_sum(): pl.pallas_call(functools.partial(kv_sum_kernel, n), out_shape=jax.ShapeDt...  40.4 us
    pallas_call x2, Pallas kernels, kv_gather(): pl.pallas_call(functools.partial(kv_gather_kernel, n), out_shape=jax.Shap...  31.4 us
    pallas_call x1, Pallas kernels, forward_pass(): pl.pallas_call(functools.partial(forward_pass_kernel, chunks), out_shape=...  28.2 us
    dot_general x10, matrix products, times_transposed(): lax.dot_general(left, right, (((1,), (1,)), ((), ())), preferred_element_...  22.4 us
    dot_general x6, matrix products, contract_rows(): lax.dot_general(left, right, (((0,), (0,)), ((), ())), preferred_element_...  18.5 us
    pallas_call x1, Pallas kernels, wt_gather(): pl.pallas_call(functools.partial(gather_kernel, chunks), out_shape=jax.Sh...  16 us
  transfers between devices with their start and end apart: 1, of which 0 were waited for; matrix products, arithmetic and copies ran while one was open for 6% of the time, Pallas kernels for 27%

profile of v2, /device:TPU:1, one launch (start us, length us, event | category | flops | bytes accessed | tf_op | source)
XLA Modules:
  0.0 459.2 jit_solution(13436004444187449940)
XLA Ops:
  8.9 16.0 %gather_wt.1 = bf16[384,2048]{1,0:T(8,128)(2,1)S(1)} custom-call(bf16[384,256]{1,0:T(8,128)(2,1)S(1)} %bitcast.95), custom_call_target="tpu_custom_call" | custom-call | tf_op jit(solution)/shard_map/gather_wt/pallas_call | solution.py:179
  25.4 1.2 copy.35
  26.6 2.1 copy.34
  28.8 2.6 fusion.56
  32.9 12.9 %gather_kv.2.kv = bf16[8,2,192,128]{3,2,1,0:T(8,128)(2,1)S(1)} custom-call(f32[384,128]{1,0:T(8,128)S(1)} %slice.53.kv, f32[384,128]{1,0:T(8,128)S(1)} %get-tuple-element.126.cosine, f32[384,128]{1,0:T(8,128)S(1)} %get-tuple-element.115.sine), custom_call_target="tpu_custom_call" | custom-call | tf_op jit(solution)/shard_map/gather_kv/pallas_call | solution.py:931
  45.8 3.3 attention.2
  50.0 22.2 %sum_mid_gather.2 = (f32[384,256]{1,0:T(8,128)S(1)}, bf16[384,2048]{1,0:T(8,128)(2,1)S(1)}) custom-call(bf16[384,2048]{1,0:T(8,128)(2,1)S(1)} %convolution_convert_fusion.6.part, bf16[384,256]{1,0:T(8,128)(2,1)S(1)} %bitcast.96), custom_call_target="tpu_custom_call" | custom-call | tf_op jit(solution)/shard_map/sum_mid_gather/pallas_call | solution.py:302
  72.7 1.8 fusion.22
  74.9 2.0 multiply_convert_fusion.5
  77.1 1.8 fusion.50.part
  78.9 28.2 %sum_pass_gather.1 = (bf16[384,256]{1,0:T(8,128)(2,1)S(1)}, bf16[384,2048]{1,0:T(8,128)(2,1)S(1)}) custom-call(bf16[384,2048]{1,0:T(8,128)(2,1)S(1)} %fusion.50.part, f32[384,256]{1,0:T(8,128)S(1)} %get-tuple-element.42.mid, bf16[384,256]{1,0:T(8,128)(2,1)S(1)} %bitcast.97), custom_call_target="tpu_custom_call" | custom-call | tf_op jit(solution)/shard_map/sum_pass_gather/pallas_call | solution.py:363
  107.6 1.0 fusion.70
  109.5 18.6 %gather_kv.3.kv = bf16[8,2,192,128]{3,2,1,0:T(8,128)(2,1)S(1)} custom-call(f32[384,128]{1,0:T(8,128)S(1)} %slice.55.kv, f32[384,128]{1,0:T(8,128)S(1)} %get-tuple-element.126.cosine, f32[384,128]{1,0:T(8,128)S(1)} %get-tuple-element.115.sine), custom_call_target="tpu_custom_call" | custom-call | tf_op jit(solution)/shard_map/gather_kv/pallas_call | solution.py:931
  128.2 2.3 attention.3
  131.1 22.6 %sum_mid_gather.3 = (f32[384,256]{1,0:T(8,128)S(1)}, bf16[384,2048]{1,0:T(8,128)(2,1)S(1)}) custom-call(bf16[384,2048]{1,0:T(8,128)(2,1)S(1)} %convolution_convert_fusion.5.part, bf16[384,256]{1,0:T(8,128)(2,1)S(1)} %copy-done.18), custom_call_target="tpu_custom_call" | custom-call | tf_op jit(solution)/shard_map/sum_mid_gather/pallas_call | solution.py:302
  154.5 1.2 copy-done.13
  156.8 5.8 %fusion.12 = f32[384,1024]{1,0:T(8,128)} fusion(bf16[1,2048,1024]{2,1,0:T(8,128)(2,1)} %param.22, bf16[384,2048]{1,0:T(8,128)(2,1)} %copy-done.13, f32[384]{0:T(512)S(1)} %add_rsqrt_fusion, f32[2048]{0:T(1024)S(1)} %bitcast.114), kind=kOutput, calls=%fused_computation.12 | convolution fusion | flops 1613758464 | bytes 7349760 | tf_op jit(solution)/shard_map/dot_general | solution.py:1220
  162.7 3.0 fusion.20
  165.7 4.6 %fusion.4 = f32[384,1024]{1,0:T(8,128)S(1)} fusion(bf16[384,2048]{1,0:T(8,128)(2,1)} %all-gather.2.cloned.1.call-done, bf16[1,1024,2048]{2,1,0:T(8,128)(2,1)} %param.23), kind=kOutput, calls=%fused_computation.4 | convolution fusion | flops 1610612736 | bytes 7340032 | tf_op jit(solution)/shard_map/dot_general | solution.py:44
  170.4 1.8 fusion.10
  173.5 2.6 fusion.42
  176.2 24.4 %sum_back_mid.2 = (f32[384,256]{1,0:T(8,128)S(1)}, f32[8,256]{1,0:T(8,128)}, bf16[384,2048]{1,0:T(8,128)(2,1)S(1)}) custom-call(bf16[384,2048]{1,0:T(8,128)(2,1)S(1)} %get-tuple-element.112.part, f32[8,128]{1,0:T(8,128)S(1)} %concatenate.49.line, bf16[384,256]{1,0:T(8,128)(2,1)S(1)} %bitcast.99, f32[384,256]{1,0:T(8,128)S(1)} %copy-done.3, ...), custom_call_target="tpu_custom_call" | custom-call | tf_op jit(solution)/shard_map/sum_back_mid/pallas_call | solution.py:850
  201.7 3.5 attention_back.2
  205.2 24.8 %sum_kv.2 = bf16[384,128]{1,0:T(8,128)(2,1)S(1)} custom-call(bf16[8,2,192,128]{3,2,1,0:T(8,128)(2,1)S(1)} %get-tuple-element.52.terms, f32[384,128]{1,0:T(8,128)S(1)} %get-tuple-element.126.cosine, f32[384,128]{1,0:T(8,128)S(1)} %get-tuple-element.115.sine), custom_call_target="tpu_custom_call" | custom-call | tf_op jit(solution)/shard_map/sum_kv/pallas_call | solution.py:995
  230.1 1.2 fusion.35
  231.3 29.2 %sum_back_pass.1 = (bf16[384,256]{1,0:T(8,128)(2,1)S(1)}, bf16[384,2048]{1,0:T(8,128)(2,1)S(1)}) custom-call(bf16[384,2048]{1,0:T(8,128)(2,1)S(1)} %get-tuple-element.110.part, f32[8,128]{1,0:T(8,128)S(1)} %concatenate.51.line, f32[384,256]{1,0:T(8,128)S(1)} %get-tuple-element.53.above, f32[384,256]{1,0:T(8,128)S(1)} %convert_element_type.131.own, ...), custom_call_target="tpu_custom_call" | custom-call | tf_op jit(solution)/shard_map/sum_back_pass/pallas_call | solution.py:850
  260.5 2.3 multiply_convert_fusion
  262.9 2.7 convolution_convert_fusion.3.rest_0_
  265.6 2.7 convolution_convert_fusion.2.rest_1_
  268.2 1.8 fusion.8
  270.1 4.5 convolution_convert_fusion.1.rest_0_
  274.5 3.1 fusion.43
  278.2 42.3 %sum_back_mid.3 = (f32[384,256]{1,0:T(8,128)}, f32[8,256]{1,0:T(8,128)}, bf16[384,2048]{1,0:T(8,128)(2,1)}, f32[512,256]{1,0:T(8,128)}, f32[512,256]{1,0:T(8,128)}) custom-call(bf16[384,2048]{1,0:T(8,128)(2,1)} %get-tuple-element.108.part, f32[8,128]{1,0:T(8,128)} %concatenate.52.line, bf16[384,256]{1,0:T(8,128)(2,1)} %copy-done.21, f32[384,256]{1,0:T(8,128)} %copy-done.2, ...), custom_call_target="tpu_custom_call" | custom-call | tf_op jit(solution)/shard_map/sum_back_mid/pallas_call | solution.py:850
  320.5 2.0 convolution_convert_fusion.8.grad
  322.5 3.4 attention_back.3
  325.9 15.6 %sum_kv.3 = bf16[384,128]{1,0:T(8,128)(2,1)S(1)} custom-call(bf16[8,2,192,128]{3,2,1,0:T(8,128)(2,1)S(1)} %get-tuple-element.58.terms, f32[384,128]{1,0:T(8,128)S(1)} %get-tuple-element.126.cosine, f32[384,128]{1,0:T(8,128)S(1)} %get-tuple-element.115.sine), custom_call_target="tpu_custom_call" | custom-call | tf_op jit(solution)/shard_map/sum_kv/pallas_call | solution.py:995
  341.5 2.2 fusion.36
  343.7 2.5 convolution_convert_fusion.4.rest_1_
  346.3 1.7 convolution_convert_fusion.7.rest_2_
  348.0 4.5 convolution_convert_fusion.rest_3_
  352.5 3.0 fusion.53.rest_5_
  356.1 85.8 %sum_back_last.1 = (bf16[384,256]{1,0:T(8,128)(2,1)}, bf16[384,256]{1,0:T(8,128)(2,1)}, f32[16,256]{1,0:T(8,128)}, f32[256,1024]{1,0:T(8,128)}, f32[256,384]{1,0...) custom-call(bf16[384,2048]{1,0:T(8,128)(2,1)} %get-tuple-element.103.part, f32[8,128]{1,0:T(8,128)} %concatenate.54.line, ...), custom_call_target="tpu_custom_call" | custom-call | tf_op jit(solution)/shard_map/sum_back_last/pallas_call | solution.py:850
  441.9 1.8 slice_bitcast_fusion
  443.7 1.1 slice_bitcast_fusion.1
  444.8 1.3 fusion.90
  447.6 1.0 maximum_bitcast_fusion
  450.0 1.0 copy.46
  451.0 1.0 copy.47
  (158 shorter events, 15.8 us)
Async XLA Ops:
  7.2 41.9 %copy-start = (bf16[1,256,2048]{2,1,0:T(8,128)(2,1)S(1)}, bf16[1,256,2048]{2,1,0:T(8,128)(2,1)}, u32[]{:S(2)}) copy-start(bf16[1,256,2048]{2,1,0:T(8,128)(2,1)} %param.19) | copy-start | bytes 3145732
  7.2 17.8 %copy-start.39 = (bf16[1,2048]{1,0:T(2,128)(2,1)S(1)}, bf16[1,2048]{1,0:T(2,128)(2,1)}, u32[]{:S(2)}) copy-start(bf16[1,2048]{1,0:T(2,128)(2,1)} %param.15) | copy-start | bytes 12292
  7.2 158.5 %all-gather.2.cloned.1.call-start = ((), (), s32[]{:S(2)}) async-start(), calls=%async_computation | async-start | bytes 1769472 | tf_op jit(solution)/shard_map/all_gather | solution.py:1274
  26.6 81.0 %copy-start.28 = (bf16[2048,64]{1,0:T(8,128)(2,1)}, bf16[2048,64]{1,0:T(8,128)(2,1)S(1)}, u32[]{:S(2)}) copy-start(bf16[2048,64]{1,0:T(8,128)(2,1)S(1)} %copy.35) | copy-start | bytes 786436
  28.8 2.6 copy-start.22
  49.1 23.6 %copy-start.43 = (bf16[1,2048,1024]{2,1,0:T(8,128)(2,1)S(1)}, bf16[1,2048,1024]{2,1,0:T(8,128)(2,1)}, u32[]{:S(2)}) copy-start(bf16[1,2048,1024]{2,1,0:T(8,128)(2,1)} %param.21) | copy-start | bytes 12582916
  50.0 22.2 %copy-start.40 = (bf16[1,2048]{1,0:T(2,128)(2,1)S(1)}, bf16[1,2048]{1,0:T(2,128)(2,1)}, u32[]{:S(2)}) copy-start(bf16[1,2048]{1,0:T(2,128)(2,1)} %param.20) | copy-start | bytes 12292
  72.7 2.2 copy-start.41
  74.9 2.2 copy-start.46
  78.9 28.7 %copy-start.31 = (bf16[2048,64]{1,0:T(8,128)(2,1)S(1)}, bf16[2048,64]{1,0:T(8,128)(2,1)}, u32[]{:S(2)}) copy-start(bf16[2048,64]{1,0:T(8,128)(2,1)} %copy.34) | copy-start | bytes 786436
  78.9 28.7 %copy-start.49 = (bf16[1,2048,256]{2,1,0:T(8,128)(2,1)S(1)}, bf16[1,2048,256]{2,1,0:T(8,128)(2,1)}, u32[]{:S(2)}) copy-start(bf16[1,2048,256]{2,1,0:T(8,128)(2,1)} %param.16) | copy-start | bytes 3145732
  108.7 19.4 %copy-start.18 = (bf16[384,256]{1,0:T(8,128)(2,1)S(1)}, bf16[384,256]{1,0:T(8,128)(2,1)}, u32[]{:S(2)}) copy-start(bf16[384,256]{1,0:T(8,128)(2,1)} %copy-done.17) | copy-start | bytes 589828
  128.2 103.1 %copy-start.1 = (f32[384,256]{1,0:T(8,128)}, f32[384,256]{1,0:T(8,128)S(1)}, u32[]{:S(2)}) copy-start(f32[384,256]{1,0:T(8,128)S(1)} %convert_element_type.131.own) | copy-start | bytes 1179652
  130.5 23.2 %copy-start.4 = (f32[2,128,768]{2,1,0:T(8,128)}, f32[2,128,768]{2,1,0:T(8,128)S(1)}, u32[]{:S(2)}) copy-start(f32[2,128,768]{2,1,0:T(8,128)S(1)} %get-tuple-element.45.mixed) | copy-start | bytes 2359300
  130.5 23.2 %copy-start.19 = (bf16[384,256]{1,0:T(8,128)(2,1)}, bf16[384,256]{1,0:T(8,128)(2,1)S(1)}, u32[]{:S(2)}) copy-start(bf16[384,256]{1,0:T(8,128)(2,1)S(1)} %get-tuple-element.46) | copy-start | bytes 589828
  156.8 19.3 %copy-start.24 = (f32[1,256]{1,0:T(1,128)}, f32[1,256]{1,0:T(1,128)S(1)}, u32[]{:S(2)}) copy-start(f32[1,256]{1,0:T(1,128)S(1)} %get-tuple-element.134.gain) | copy-start | bytes 3076
  156.8 74.5 %copy-start.23 = (f32[1,256]{1,0:T(1,128)}, f32[1,256]{1,0:T(1,128)S(1)}, u32[]{:S(2)}) copy-start(f32[1,256]{1,0:T(1,128)S(1)} %get-tuple-element.133.gain) | copy-start | bytes 3076
  156.8 5.8 %copy-start.14 = (bf16[384,2048]{1,0:T(8,128)(2,1)S(1)}, bf16[384,2048]{1,0:T(8,128)(2,1)}, u32[]{:S(2)}) copy-start(bf16[384,2048]{1,0:T(8,128)(2,1)} %copy-done.13) | copy-start | bytes 4718596
  156.8 5.8 %copy-start.44 = (bf16[1,2048,1024]{2,1,0:T(8,128)(2,1)S(1)}, bf16[1,2048,1024]{2,1,0:T(8,128)(2,1)}, u32[]{:S(2)}) copy-start(bf16[1,2048,1024]{2,1,0:T(8,128)(2,1)} %param.21) | copy-start | bytes 12582916
  165.7 4.6 %copy-start.42 = (bf16[1,2048,1024]{2,1,0:T(8,128)(2,1)S(1)}, bf16[1,2048,1024]{2,1,0:T(8,128)(2,1)}, u32[]{:S(2)}) copy-start(bf16[1,2048,1024]{2,1,0:T(8,128)(2,1)} %param.22) | copy-start | bytes 12582916
  165.7 4.7 %copy-start.57 = (f32[384,1024]{1,0:T(8,128)S(1)}, f32[384,1024]{1,0:T(8,128)}, u32[]{:S(2)}) copy-start(f32[384,1024]{1,0:T(8,128)} %fusion.20) | copy-start | bytes 4718596
  170.4 2.7 copy-start.45
  170.4 3.1 copy-start.56
  173.5 2.7 copy-start.3
  173.5 2.7 copy-start.7
  173.5 2.7 copy-start.10
  201.7 28.4 %copy-start.12 = (bf16[384,2048]{1,0:T(8,128)(2,1)S(1)}, bf16[384,2048]{1,0:T(8,128)(2,1)}, u32[]{:S(2)}) copy-start(bf16[384,2048]{1,0:T(8,128)(2,1)} %copy-done.11) | copy-start | bytes 4718596
  201.7 28.4 %copy-start.29 = (bf16[2048,64]{1,0:T(8,128)(2,1)S(1)}, bf16[2048,64]{1,0:T(8,128)(2,1)}, u32[]{:S(2)}) copy-start(bf16[2048,64]{1,0:T(8,128)(2,1)} %copy-done.28) | copy-start | bytes 786436
  201.7 28.4 %copy-start.32 = (bf16[2048,64]{1,0:T(8,128)(2,1)S(1)}, bf16[2048,64]{1,0:T(8,128)(2,1)}, u32[]{:S(2)}) copy-start(bf16[2048,64]{1,0:T(8,128)(2,1)} %copy.34) | copy-start | bytes 786436
  201.7 28.4 %copy-start.50 = (bf16[1,2048,256]{2,1,0:T(8,128)(2,1)S(1)}, bf16[1,2048,256]{2,1,0:T(8,128)(2,1)}, u32[]{:S(2)}) copy-start(bf16[1,2048,256]{2,1,0:T(8,128)(2,1)} %param.16) | copy-start | bytes 3145732
  230.1 30.4 %copy-start.47 = (bf16[1,1024,2048]{2,1,0:T(8,128)(2,1)S(1)}, bf16[1,1024,2048]{2,1,0:T(8,128)(2,1)}, u32[]{:S(2)}) copy-start(bf16[1,1024,2048]{2,1,0:T(8,128)(2,1)} %param.23) | copy-start | bytes 12582916
  260.5 2.4 copy-start.21
  262.9 2.7 copy-start.52
  262.9 11.6 %copy-start.54 = (bf16[384,1024]{1,0:T(8,128)(2,1)}, bf16[384,1024]{1,0:T(8,128)(2,1)S(1)}, u32[]{:S(2)}) copy-start(bf16[384,1024]{1,0:T(8,128)(2,1)S(1)} %get-tuple-element.105) | copy-start | bytes 2359300
  322.5 19.0 %copy-start.30 = (bf16[2048,64]{1,0:T(8,128)(2,1)S(1)}, bf16[2048,64]{1,0:T(8,128)(2,1)}, u32[]{:S(2)}) copy-start(bf16[2048,64]{1,0:T(8,128)(2,1)} %copy-done.28) | copy-start | bytes 786436
  322.5 19.0 %copy-start.33 = (bf16[2048,64]{1,0:T(8,128)(2,1)S(1)}, bf16[2048,64]{1,0:T(8,128)(2,1)}, u32[]{:S(2)}) copy-start(bf16[2048,64]{1,0:T(8,128)(2,1)} %copy.34) | copy-start | bytes 786436
  322.5 19.0 %copy-start.51 = (bf16[1,2048,256]{2,1,0:T(8,128)(2,1)S(1)}, bf16[1,2048,256]{2,1,0:T(8,128)(2,1)}, u32[]{:S(2)}) copy-start(bf16[1,2048,256]{2,1,0:T(8,128)(2,1)} %param.16) | copy-start | bytes 3145732
  343.7 2.5 copy-start.20
  343.7 2.5 copy-start.25
  348.0 4.5 copy-start.48
  348.0 4.5 copy-start.53
  441.9 5.7 %copy-start.34 = (f32[512,256]{1,0:T(8,128)S(1)}, f32[512,256]{1,0:T(8,128)}, u32[]{:S(2)}) copy-start(f32[512,256]{1,0:T(8,128)} %get-tuple-element.68) | copy-start | bytes 1572868
  441.9 5.7 %copy-start.35 = (f32[512,256]{1,0:T(8,128)S(1)}, f32[512,256]{1,0:T(8,128)}, u32[]{:S(2)}) copy-start(f32[512,256]{1,0:T(8,128)} %get-tuple-element.69) | copy-start | bytes 1572868
  443.7 4.9 %copy-start.37 = (bf16[384,256]{1,0:T(8,128)(2,1)S(1)}, bf16[384,256]{1,0:T(8,128)(2,1)}, u32[]{:S(2)}) copy-start(bf16[384,256]{1,0:T(8,128)(2,1)} %get-tuple-element.61) | copy-start | bytes 589828
  443.7 4.9 %copy-start.38 = (bf16[384,256]{1,0:T(8,128)(2,1)S(1)}, bf16[384,256]{1,0:T(8,128)(2,1)}, u32[]{:S(2)}) copy-start(bf16[384,256]{1,0:T(8,128)(2,1)} %get-tuple-element.62) | copy-start | bytes 589828
  444.8 4.5 copy-start.36
  447.6 2.5 copy-start.27
  448.6 2.4 copy-start.26
  (11 other events, 14.4 us)
Sparse Core Ops, SparseCore 0:
  9.7 28.9 all-gather.1

commit v3 on v2

--- a/solution.py
+++ b/solution.py
@@ -249,6 +249,17 @@
             copy.wait_send()
 
 
+def sum_in_turn(sums, use):
+    for one in sums:
+        one.start()
+    for one in sums:
+        one.pass_on()
+    for one in sums:
+        one.pass_more()
+    for q in range(len(sums)):
+        use(q)
+
+
 def reduce_scratch(chunks, rows, width):
     return [pltpu.VMEM((chunks, 4, rows, width), bf16) for _ in range(3)] + [
         pltpu.SemaphoreType.DMA((chunks, 4)) for _ in range(4)
@@ -281,17 +292,14 @@
     spans = [pl.ds(q * rows, rows) for q in range(chunks)]
     sums = [Reduce(place, part, bufs, q, spans[q]) for q in range(chunks)]
     gathers = [Gather(place, whole, sems, q, spans[q]) for q in range(chunks)]
-    for one in sums:
-        one.start()
-    for one in sums:
-        one.pass_on()
-    for one in sums:
-        one.pass_more()
-    for q in range(chunks):
+
+    def use(q):
         value = skip[spans[q], :].astype(f32) + sums[q].total()
         mid[spans[q], :] = value
         agsrc[spans[q], :] = value.astype(bf16)
         gathers[q].start(agsrc.at[spans[q]])
+
+    sum_in_turn(sums, use)
     gather_all(gathers)
     for one in sums:
         one.finish()
@@ -332,19 +340,16 @@
     sums = [Reduce(place, part, bufs, q, spans[q]) for q in range(chunks)]
     gathers = [Gather(place, whole, sems, q, spans[q]) for q in range(chunks)]
     swaps = []
-    for one in sums:
-        one.start()
-    for one in sums:
-        one.pass_on()
-    for one in sums:
-        one.pass_more()
-    for q in range(chunks):
+
+    def use(q):
         agsrc[spans[q], :] = (mid[spans[q], :] + sums[q].total()).astype(bf16)
         swap = swap_sections(
             agsrc.at[spans[q]], arrived.at[spans[q]], xsend.at[q], xrecv.at[q]
         )
         swap.start()
         swaps.append(swap)
+
+    sum_in_turn(sums, use)
     for q in range(chunks):
         swaps[q].wait_recv()
         share[spans[q], :] = jnp.where(
@@ -879,137 +884,6 @@
     return y * cosine + turned
 
 
-def kv_gather_kernel(n, kv, cosine, sine, out, mine, send, recv, local):
-    me = lax.axis_index("ctx")
-    barrier = pltpu.get_barrier_semaphore()
-    for d in range(1, n):
-
-        @pl.when(me - d >= 0)
-        def _():
-            pl.semaphore_signal(
-                barrier, inc=1, device_id={"ctx": me - d}, device_id_type=MESH
-            )
-
-    rows = kv.shape[0] // 2
-    turned = turn(kv[...], cosine[...], sine[...]).astype(bf16)
-    mine[0] = turned[:rows]
-    mine[1] = turned[rows:]
-    own = pltpu.make_async_copy(mine, out.at[me], local)
-    own.start()
-
-    @pl.when(me < n - 1)
-    def _():
-        pl.semaphore_wait(barrier, n - 1 - me)
-
-    def copy(d):
-        return remote(mine, out.at[me], send.at[d], recv.at[d], {"ctx": lax.rem(me + d, n)})
-
-    for d in range(1, n):
-
-        @pl.when(me + d < n)
-        def _():
-            copy(d).start()
-
-    for d in range(1, n):
-
-        @pl.when(me - d >= 0)
-        def _():
-            copy(d).wait_recv()
-
-    for d in range(1, n):
-
-        @pl.when(me + d < n)
-        def _():
-            copy(d).wait_send()
-
-    own.wait()
-
-
-def kv_gather(kv, cosine, sine, collective_id):
-    n = 8
-    rows = kv.shape[0] // 2
-    return pl.pallas_call(
-        functools.partial(kv_gather_kernel, n),
-        out_shape=jax.ShapeDtypeStruct((n, 2, rows, 128), bf16),
-        in_specs=[pl.BlockSpec(memory_space=pltpu.VMEM)] * 3,
-        out_specs=pl.BlockSpec(memory_space=pl.ANY),
-        scratch_shapes=[
-            pltpu.VMEM((2, rows, 128), bf16),
-            pltpu.SemaphoreType.DMA((n,)),
-            pltpu.SemaphoreType.DMA((n,)),
-            pltpu.SemaphoreType.DMA,
-        ],
-        compiler_params=pltpu.CompilerParams(
-            collective_id=collective_id, has_side_effects=True, vmem_limit_bytes=32 * MiB
-        ),
-        name="gather_kv",
-    )(kv, cosine, sine)
-
-
-def kv_sum_kernel(n, terms, cosine, sine, out, slots, total, send, recv):
-    me = lax.axis_index("ctx")
-    barrier = pltpu.get_barrier_semaphore()
-    for d in range(1, n):
-
-        @pl.when(me + d < n)
-        def _():
-            pl.semaphore_signal(
-                barrier, inc=1, device_id={"ctx": lax.rem(me + d, n)}, device_id_type=MESH
-            )
-
-    @pl.when(me > 0)
-    def _():
-        pl.semaphore_wait(barrier, me)
-
-    def copy(d):
-        back = lax.rem(me + n - d, n)
-        return remote(terms.at[back], slots.at[d], send.at[d], recv.at[d], {"ctx": back})
-
-    for d in range(1, n):
-
-        @pl.when(me - d >= 0)
-        def _():
-            copy(d).start()
-
-    total[...] = terms[me].astype(f32)
-    for d in range(1, n):
-
-        @pl.when(me + d < n)
-        def _():
-            copy(d).wait_recv()
-            total[...] += slots[d].astype(f32)
-
-    rows = terms.shape[2]
-    for b in range(2):
-        span = pl.ds(b * rows, rows)
-        out[span, :] = turn_back(total[b], cosine[span, :], sine[span, :]).astype(bf16)
-    for d in range(1, n):
-
-        @pl.when(me - d >= 0)
-        def _():
-            copy(d).wait_send()
-
-
-def kv_sum(terms, cosine, sine, collective_id):
-    n, two, rows, width = terms.shape
-    return pl.pallas_call(
-        functools.partial(kv_sum_kernel, n),
-        out_shape=jax.ShapeDtypeStruct((2 * rows, width), bf16),
-        in_specs=[pl.BlockSpec(memory_space=pltpu.VMEM)] * 3,
-        out_specs=pl.BlockSpec(memory_space=pltpu.VMEM),
-        scratch_shapes=[
-            pltpu.VMEM((n, 2, rows, width), bf16),
-            pltpu.VMEM((2, rows, width), f32),
-            pltpu.SemaphoreType.DMA((n,)),
-            pltpu.SemaphoreType.DMA((n,)),
-        ],
-        compiler_params=pltpu.CompilerParams(
-            collective_id=collective_id, has_side_effects=True, vmem_limit_bytes=32 * MiB
-        ),
-        name="sum_kv",
-    )(terms, cosine, sine)
-
-
 def visible_keys(bounds, b, key_block, me, rows, heads):
     row = lax.broadcasted_iota(jnp.int32, (1, heads * rows), 1)
     for head in range(1, heads):
@@ -1033,10 +907,58 @@
         stacked[b, pl.ds((2 * pair + 1) * rows, rows), :] = odd.astype(bf16)
 
 
-def attention_kernel(bounds, flat, cosine, sine, kv, mix, logs, mixed, stacked, acc):
+def later(me, d, n):
+    return me + d < n
+
+
+def earlier(me, d, n):
+    return me - d >= 0
+
+
+def greet_order(me, n, side, count):
+    barrier = pltpu.get_barrier_semaphore()
+    step = 1 if side is later else n - 1
+    for d in range(1, n):
+
+        @pl.when(side(me, d, n))
+        def _():
+            pl.semaphore_signal(
+                barrier, inc=1, device_id={"ctx": lax.rem(me + d * step, n)},
+                device_id_type=MESH,
+            )
+
+    def wait():
+        @pl.when(count > 0)
+        def _():
+            pl.semaphore_wait(barrier, count)
+
+    return wait
+
+
+def attention_kernel(
+    n, bounds, flat, kv_pre, cosine, sine, kv_cosine, kv_sine, mix, logs, mixed, kv,
+    stacked, acc, mine, send, recv
+):
     me = lax.axis_index("ctx")
     rows = kv.shape[2]
     heads = 4
+    wait = greet_order(me, n, earlier, n - 1 - me)
+    for b in range(2):
+        span = pl.ds(b * rows, rows)
+        turned = turn(kv_pre[span, :], kv_cosine[span, :], kv_sine[span, :]).astype(bf16)
+        mine[b] = turned
+        kv[me, b] = turned
+    wait()
+
+    def copy(d):
+        return remote(mine, kv.at[me], send.at[d], recv.at[d], {"ctx": lax.rem(me + d, n)})
+
+    for d in reversed(range(1, n)):
+
+        @pl.when(later(me, d, n))
+        def _():
+            copy(d).start()
+
     for b in range(2):
         stack_queries(flat, cosine, sine, b, rows, stacked)
     acc[...] = jnp.zeros_like(acc)
@@ -1056,8 +978,13 @@
             after += [new_peak, total]
         return tuple(after)
 
+    def arrived(d, carry):
+        copy(d).wait_recv()
+        return block(me - d, carry)
+
     zero = jnp.zeros((1, heads * rows), f32)
-    done = lax.fori_loop(0, me + 1, block, (zero + neg_big, zero) * 2)
+    done = block(me, (zero + neg_big, zero) * 2)
+    done = lax.fori_loop(1, me + 1, arrived, done)
     low = lanes((rows, 128)) < HD
     for b in range(2):
         peak, total = done[2 * b : 2 * b + 2]
@@ -1070,36 +997,50 @@
             odd = upright[(2 * pair + 1) * rows : (2 * pair + 2) * rows]
             both = jnp.where(low, pltpu.roll(even, HD, 1), odd)
             mix[pl.ds(b * rows, rows), 128 * pair : 128 * pair + 128] = both.astype(bf16)
-
-
-def attention(bounds, flat, cosine, sine, kv):
-    rows = kv.shape[2]
+    for d in range(1, n):
+
+        @pl.when(later(me, d, n))
+        def _():
+            copy(d).wait_send()
+
+
+def attention(bounds, flat, kv_pre, cosine, sine, kv_cosine, kv_sine, collective_id):
+    n = 8
+    rows = flat.shape[0] // 2
     vmem = pl.BlockSpec(memory_space=pltpu.VMEM)
     return pl.pallas_call(
-        attention_kernel,
+        functools.partial(attention_kernel, n),
         out_shape=(
             jax.ShapeDtypeStruct((2 * rows, 256), bf16),
             jax.ShapeDtypeStruct((2, 1, 4 * rows), f32),
             jax.ShapeDtypeStruct((2, 128, 4 * rows), f32),
+            jax.ShapeDtypeStruct((n, 2, rows, 128), bf16),
         ),
-        in_specs=[pl.BlockSpec(memory_space=pltpu.SMEM)] + [vmem] * 4,
-        out_specs=(vmem, vmem, vmem),
+        in_specs=[pl.BlockSpec(memory_space=pltpu.SMEM)] + [vmem] * 6,
+        out_specs=(vmem,) * 4,
         scratch_shapes=[
             pltpu.VMEM((2, 4 * rows, 128), bf16),
             pltpu.VMEM((2, 128, 4 * rows), f32),
+            pltpu.VMEM((2, rows, 128), bf16),
+            pltpu.SemaphoreType.DMA((n,)),
+            pltpu.SemaphoreType.DMA((n,)),
         ],
-        compiler_params=pltpu.CompilerParams(vmem_limit_bytes=40 * MiB),
+        compiler_params=pltpu.CompilerParams(
+            collective_id=collective_id, has_side_effects=True, vmem_limit_bytes=40 * MiB
+        ),
         name="attention",
-    )(bounds, flat, cosine, sine, kv)
+    )(bounds, flat, kv_pre, cosine, sine, kv_cosine, kv_sine)
 
 
 def attention_back_kernel(
-    bounds, flat, cosine, sine, kv, logs, mixed, grad, out, terms, stacked, grads, acc
+    n, bounds, flat, cosine, sine, kv_cosine, kv_sine, kv, logs, mixed, grad, out, grad_kv,
+    terms, slots, total, stacked, grads, acc, send, recv
 ):
     me = lax.axis_index("ctx")
     rows = kv.shape[2]
     heads = 4
     low = lanes((rows, 128)) < HD
+    wait = greet_order(me, n, later, me)
     deltas = []
     for b in range(2):
         stack_queries(flat, cosine, sine, b, rows, stacked)
@@ -1113,8 +1054,9 @@
             jnp.sum(mixed[b] * grads[b].astype(f32).T, axis=0, keepdims=True)
         )
     acc[...] = jnp.zeros_like(acc)
-
-    def block(j, carry):
+    wait()
+
+    def block(j):
         for b in range(2):
             keys = kv[j, b]
             scores = times_transposed(keys, stacked[b])
@@ -1128,9 +1070,18 @@
                 jnp.dot(grad_scores, stacked[b], preferred_element_type=f32)
                 + jnp.dot(probs.astype(bf16), grads[b], preferred_element_type=f32)
             ).astype(bf16)
+
+    def copy(d):
+        back = lax.rem(me + n - d, n)
+        return remote(terms.at[back], slots.at[d], send.at[d], recv.at[d], {"ctx": back})
+
+    def block_sent(j, carry):
+        block(j)
+        copy(me - j).start()
         return carry
 
-    lax.fori_loop(0, me + 1, block, 0)
+    lax.fori_loop(0, me, block_sent, 0)
+    block(me)
     for b in range(2):
         span = pl.ds(b * rows, rows)
         upright = acc[b].T * (HD**-0.5)
@@ -1141,27 +1092,55 @@
             out[span, 128 * pair : 128 * pair + 128] = turn_back(
                 both, cosine[span, :], sine[span, :]
             ).astype(bf16)
-
-
-def attention_back(bounds, flat, cosine, sine, kv, logs, mixed, grad):
-    rows = kv.shape[2]
+    for b in range(2):
+        total[b] = terms[me, b].astype(f32)
+    for d in range(1, n):
+
+        @pl.when(later(me, d, n))
+        def _():
+            copy(d).wait_recv()
+            total[...] += slots[d].astype(f32)
+
+    for b in range(2):
+        span = pl.ds(b * rows, rows)
+        grad_kv[span, :] = turn_back(
+            total[b], kv_cosine[span, :], kv_sine[span, :]
+        ).astype(bf16)
+    for d in range(1, n):
+
+        @pl.when(earlier(me, d, n))
+        def _():
+            copy(d).wait_send()
+
+
+def attention_back(
+    bounds, flat, cosine, sine, kv_cosine, kv_sine, kv, logs, mixed, grad, collective_id
+):
+    n, two, rows, width = kv.shape
     vmem = pl.BlockSpec(memory_space=pltpu.VMEM)
     return pl.pallas_call(
-        attention_back_kernel,
+        functools.partial(attention_back_kernel, n),
         out_shape=(
             jax.ShapeDtypeStruct((2 * rows, 256), bf16),
-            jax.ShapeDtypeStruct(kv.shape, bf16),
+            jax.ShapeDtypeStruct((2 * rows, 128), bf16),
         ),
-        in_specs=[pl.BlockSpec(memory_space=pltpu.SMEM)] + [vmem] * 7,
+        in_specs=[pl.BlockSpec(memory_space=pltpu.SMEM)] + [vmem] * 9,
         out_specs=(vmem, vmem),
         scratch_shapes=[
+            pltpu.VMEM(kv.shape, bf16),
+            pltpu.VMEM(kv.shape, bf16),
+            pltpu.VMEM((2, rows, width), f32),
             pltpu.VMEM((2, 4 * rows, 128), bf16),
             pltpu.VMEM((2, 4 * rows, 128), bf16),
             pltpu.VMEM((2, 128, 4 * rows), f32),
+            pltpu.SemaphoreType.DMA((n,)),
+            pltpu.SemaphoreType.DMA((n,)),
         ],
-        compiler_params=pltpu.CompilerParams(vmem_limit_bytes=40 * MiB),
+        compiler_params=pltpu.CompilerParams(
+            collective_id=collective_id, has_side_effects=True, vmem_limit_bytes=40 * MiB
+        ),
         name="attention_back",
-    )(bounds, flat, cosine, sine, kv, logs, mixed, grad)
+    )(bounds, flat, cosine, sine, kv_cosine, kv_sine, kv, logs, mixed, grad)
 
 
 def per_device(
@@ -1209,8 +1188,9 @@
         attn_in = (hidden * factor * gain_attn).astype(bf16)
         pre = jnp.dot(attn_in, w_qkv, preferred_element_type=f32)
         q_pre, kv_pre = pre[:, :256], pre[:, 256:]
-        kv = kv_gather(kv_pre, kv_cosine, kv_sine, 1)
-        mix, logs, mixed = attention(doc_bounds, q_pre, cosine, sine, kv)
+        mix, logs, mixed, kv = attention(
+            doc_bounds, q_pre, kv_pre, cosine, sine, kv_cosine, kv_sine, 1
+        )
         part = jnp.dot(mix, w_o, preferred_element_type=f32).astype(bf16)
         mid, mid_whole = forward_mid(part, share, 2)
         mid_wide = mid_whole.astype(f32)
@@ -1254,11 +1234,10 @@
             8 if last else 3,
         )
         grad_mix = times_transposed(grad_attn, w_o).astype(bf16)
-        grad_query, terms = attention_back(
-            doc_bounds, saved["q_pre"], cosine, sine, saved["kv"], saved["logs"],
-            saved["mixed"], grad_mix,
-        )
-        grad_kv = kv_sum(terms, kv_cosine, kv_sine, 4)
+        grad_query, grad_kv = attention_back(
+            doc_bounds, saved["q_pre"], cosine, sine, kv_cosine, kv_sine, saved["kv"],
+            saved["logs"], saved["mixed"], grad_mix, 4,
+        )
         grad_pre = jnp.concatenate([grad_query, grad_kv], axis=1)
         part = times_transposed(grad_pre, w_qkv)
         line = line_of(part, saved["whole"], saved["factor"], gain_attn)

time: 467 us -> 441 us (0.944)
  Pallas kernels: 355 us -> 332 us
    pallas_call x8 -> x4, Pallas kernels: 84.4 us -> 58.7 us  [the longest x2 30.6 us: attention(): pl.pallas_call(functools.partial(attention_kernel, n), out_shape=(jax.Sha...]
    unnamed x121 -> x122, local copies, waits for them, and re-layouts: 9.71 us -> 9.27 us
where the time goes in v3:
time: 441 us; the launch traced here: 434 us
  Pallas kernels  332 us (75%)
  matrix products  63.7 us (14%)
  local copies, waits for them, and re-layouts  17.4 us (4%)
  between operations  15.2 us (3%)
  other arithmetic  4.85 us (1%)
    pallas_call x4, Pallas kernels, backward_sum(): pl.pallas_call(functools.partial(backward_kernel, mode, chunks, dims, mod...  185 us
    pallas_call x2, Pallas kernels, forward_mid(): pl.pallas_call(functools.partial(forward_mid_kernel, chunks), out_shape=(...  44.6 us
    pallas_call x2, Pallas kernels, attention(): pl.pallas_call(functools.partial(attention_kernel, n), out_shape=(jax.Sha...  30.6 us
    pallas_call x1, Pallas kernels, forward_pass(): pl.pallas_call(functools.partial(forward_pass_kernel, chunks), out_shape=...  28.2 us
    pallas_call x2, Pallas kernels, attention_back(): pl.pallas_call(functools.partial(attention_back_kernel, n), out_shape=(ja...  28.1 us
    dot_general x10, matrix products, times_transposed(): lax.dot_general(left, right, (((1,), (1,)), ((), ())), preferred_element_...  23 us
    dot_general x6, matrix products, contract_rows(): lax.dot_general(left, right, (((0,), (0,)), ((), ())), preferred_element_...  18.5 us
    pallas_call x1, Pallas kernels, wt_gather(): pl.pallas_call(functools.partial(gather_kernel, chunks), out_shape=jax.Sh...  16.1 us
  transfers between devices with their start and end apart: 1, of which 0 were waited for; matrix products, arithmetic and copies ran while one was open for 6% of the time, Pallas kernels for 27%

profile of v3, /device:TPU:1, one launch (start us, length us, event | category | flops | bytes accessed | tf_op | source)
XLA Modules:
  0.0 434.2 jit_solution(16394594852143150518)
XLA Ops:
  7.9 0.9 copy-done.9
  8.9 16.1 %gather_wt.1 = bf16[384,2048]{1,0:T(8,128)(2,1)S(1)} custom-call(bf16[384,256]{1,0:T(8,128)(2,1)S(1)} %bitcast.97), custom_call_target="tpu_custom_call" | custom-call | tf_op jit(solution)/shard_map/gather_wt/pallas_call | solution.py:179
  25.7 2.1 copy.34
  27.8 2.4 fusion.56
  30.7 0.8 multiply_sine_fusion
  31.9 14.5 %attention.2 = (bf16[384,256]{1,0:T(8,128)(2,1)S(1)}, f32[2,1,768]{2,1,0:T(1,128)}, f32[2,128,768]{2,1,0:T(8,128)}, bf16[8,2,192,128]{3,2,1,0:T(8,128)(2,1)}) custom-call(s32[2,2]{1,0:T(2,128)S(1)} %copy-done.21, f32[384,256]{1,0:T(8,128)S(1)} %slice.52.flat, f32[384,128]{1,0:T(8,128)S(1)} %slice.53.kv_pre, f32[384,128]{1,0:T(8,128)S(1)} %get-tuple-element.127.cosine, ...), custom_call_target="tpu_custom_call" | custom-call | tf_op jit(solution)/shard_map/attention/pallas_call | solution.py:1011
  47.4 22.2 %sum_mid_gather.2 = (f32[384,256]{1,0:T(8,128)S(1)}, bf16[384,2048]{1,0:T(8,128)(2,1)S(1)}) custom-call(bf16[384,2048]{1,0:T(8,128)(2,1)S(1)} %convolution_convert_fusion.6.part, bf16[384,256]{1,0:T(8,128)(2,1)S(1)} %bitcast.98), custom_call_target="tpu_custom_call" | custom-call | tf_op jit(solution)/shard_map/sum_mid_gather/pallas_call | solution.py:310
  70.1 1.9 fusion.22
  72.2 2.0 multiply_convert_fusion.5
  74.4 1.8 fusion.50.part
  76.3 28.2 %sum_pass_gather.1 = (bf16[384,256]{1,0:T(8,128)(2,1)S(1)}, bf16[384,2048]{1,0:T(8,128)(2,1)S(1)}) custom-call(bf16[384,2048]{1,0:T(8,128)(2,1)S(1)} %fusion.50.part, f32[384,256]{1,0:T(8,128)S(1)} %get-tuple-element.43.mid, bf16[384,256]{1,0:T(8,128)(2,1)S(1)} %bitcast.99), custom_call_target="tpu_custom_call" | custom-call | tf_op jit(solution)/shard_map/sum_pass_gather/pallas_call | solution.py:368
  104.9 1.1 fusion.70
  106.2 16.0 %attention.3 = (bf16[384,256]{1,0:T(8,128)(2,1)S(1)}, f32[2,1,768]{2,1,0:T(1,128)S(1)}, f32[2,128,768]{2,1,0:T(8,128)S(1)}, bf16[8,2,192,128]{3,2,1,0:T(8,128)(2,1)S(1)}) custom-call(s32[2,2]{1,0:T(2,128)S(1)} %copy-done.21, f32[384,256]{1,0:T(8,128)S(1)} %slice.54.flat, f32[384,128]{1,0:T(8,128)S(1)} %slice.55.kv_pre, ...), custom_call_target="tpu_custom_call" | custom-call | tf_op jit(solution)/shard_map/attention/pallas_call | solution.py:1011
  123.5 22.3 %sum_mid_gather.3 = (f32[384,256]{1,0:T(8,128)S(1)}, bf16[384,2048]{1,0:T(8,128)(2,1)S(1)}) custom-call(bf16[384,2048]{1,0:T(8,128)(2,1)S(1)} %convolution_convert_fusion.5.part, bf16[384,256]{1,0:T(8,128)(2,1)S(1)} %get-tuple-element.49.skip), custom_call_target="tpu_custom_call" | custom-call | tf_op jit(solution)/shard_map/sum_mid_gather/pallas_call | solution.py:310
  146.3 0.8 copy-done.14
  147.2 5.8 %fusion.12 = f32[384,1024]{1,0:T(8,128)} fusion(bf16[1,2048,1024]{2,1,0:T(8,128)(2,1)} %param.22, bf16[384,2048]{1,0:T(8,128)(2,1)} %copy-done.14, f32[384]{0:T(512)S(1)} %add_rsqrt_fusion, f32[2048]{0:T(1024)S(1)} %bitcast.116), kind=kOutput, calls=%fused_computation.12 | convolution fusion | flops 1613758464 | bytes 7349760 | tf_op jit(solution)/shard_map/dot_general | solution.py:1200
  153.0 3.0 fusion.20
  156.1 4.6 %fusion.4 = f32[384,1024]{1,0:T(8,128)S(1)} fusion(bf16[384,2048]{1,0:T(8,128)(2,1)} %all-gather.2.cloned.1.call-done, bf16[1,1024,2048]{2,1,0:T(8,128)(2,1)} %param.23), kind=kOutput, calls=%fused_computation.4 | convolution fusion | flops 1610612736 | bytes 7340032 | tf_op jit(solution)/shard_map/dot_general | solution.py:44
  160.8 1.9 fusion.10
  162.7 0.7 copy-done.45
  163.9 2.7 fusion.42
  166.6 24.4 %sum_back_mid.2 = (f32[384,256]{1,0:T(8,128)S(1)}, f32[8,256]{1,0:T(8,128)}, bf16[384,2048]{1,0:T(8,128)(2,1)S(1)}) custom-call(bf16[384,2048]{1,0:T(8,128)(2,1)S(1)} %get-tuple-element.114.part, f32[8,128]{1,0:T(8,128)S(1)} %concatenate.49.line, bf16[384,256]{1,0:T(8,128)(2,1)S(1)} %bitcast.101, f32[384,256]{1,0:T(8,128)S(1)} %get-tuple-element.51.own.rest_6_, ...), custom_call_target="tpu_custom_call" | custom-call | tf_op jit(solution)/shard_map/sum_back_mid/pallas_call | solution.py:855
  192.4 17.8 %attention_back.2 = (bf16[384,256]{1,0:T(8,128)(2,1)S(1)}, bf16[384,128]{1,0:T(8,128)(2,1)S(1)}) custom-call(s32[2,2]{1,0:T(2,128)S(1)} %copy-done.21, f32[384,256]{1,0:T(8,128)S(1)} %slice.54.flat, f32[384,128]{1,0:T(8,128)S(1)} %get-tuple-element.127.cosine, f32[384,128]{1,0:T(8,128)S(1)} %get-tuple-element.118.sine, ...), custom_call_target="tpu_custom_call" | custom-call | tf_op jit(solution)/shard_map/attention_back/pallas_call | solution.py:1121
  210.3 1.3 fusion.35
  211.6 28.4 %sum_back_pass.1 = (bf16[384,256]{1,0:T(8,128)(2,1)S(1)}, bf16[384,2048]{1,0:T(8,128)(2,1)S(1)}) custom-call(bf16[384,2048]{1,0:T(8,128)(2,1)S(1)} %get-tuple-element.112.part, f32[8,128]{1,0:T(8,128)S(1)} %concatenate.51.line, f32[384,256]{1,0:T(8,128)S(1)} %get-tuple-element.55.above, f32[384,256]{1,0:T(8,128)S(1)} %convert_element_type.131.own, ...), custom_call_target="tpu_custom_call" | custom-call | tf_op jit(solution)/shard_map/sum_back_pass/pallas_call | solution.py:855
  240.0 2.4 multiply_convert_fusion
  242.5 2.7 convolution_convert_fusion.3.rest_0_
  245.2 2.7 convolution_convert_fusion.2.rest_1_
  247.8 1.8 fusion.8
  249.7 4.5 %convolution_convert_fusion.1.rest_0_ = bf16[2048,1024]{1,0:T(8,128)(2,1)} fusion(bf16[384,1024]{1,0:T(8,128)(2,1)S(1)} %get-tuple-element.108, bf16[384,2048]{1,0:T(8,128)(2,1)S(1)} %copy-done.16, f32[384]{0:T(512)S(1)} %add_rsqrt_fusion, f32[2048]{0:T(1024)S(1)} %bitcast.119), kind=kOutput, calls=%fused_computation.33 | convolution fusion | flops 1615855616 | bytes 6563328 | tf_op jit(solution)/shard_map/dot_general | solution.py:38
  254.1 3.3 fusion.43
  258.0 40.9 %sum_back_mid.3 = (f32[384,256]{1,0:T(8,128)}, f32[8,256]{1,0:T(8,128)}, bf16[384,2048]{1,0:T(8,128)(2,1)}, f32[512,256]{1,0:T(8,128)}, f32[512,256]{1,0:T(8,128)}) custom-call(bf16[384,2048]{1,0:T(8,128)(2,1)} %get-tuple-element.110.part, f32[8,128]{1,0:T(8,128)} %concatenate.52.line, bf16[384,256]{1,0:T(8,128)(2,1)} %copy-done.20, f32[384,256]{1,0:T(8,128)} %copy-done.2, ...), custom_call_target="tpu_custom_call" | custom-call | tf_op jit(solution)/shard_map/sum_back_mid/pallas_call | solution.py:855
  298.9 2.0 convolution_convert_fusion.8.grad
  300.9 10.3 %attention_back.3 = (bf16[384,256]{1,0:T(8,128)(2,1)S(1)}, bf16[384,128]{1,0:T(8,128)(2,1)S(1)}) custom-call(s32[2,2]{1,0:T(2,128)S(1)} %copy-done.21, f32[384,256]{1,0:T(8,128)S(1)} %slice.54.flat, f32[384,128]{1,0:T(8,128)S(1)} %get-tuple-element.127.cosine, f32[384,128]{1,0:T(8,128)S(1)} %get-tuple-element.118.sine, ...), custom_call_target="tpu_custom_call" | custom-call | tf_op jit(solution)/shard_map/attention_back/pallas_call | solution.py:1121
  311.3 2.3 fusion.36
  313.6 2.6 convolution_convert_fusion.4.rest_1_
  316.2 1.7 convolution_convert_fusion.7.rest_2_
  317.9 4.5 %convolution_convert_fusion.rest_3_ = bf16[2048,1024]{1,0:T(8,128)(2,1)} fusion(bf16[384,1024]{1,0:T(8,128)(2,1)S(1)} %copy-done.55, bf16[384,2048]{1,0:T(8,128)(2,1)S(1)} %copy-done.17, f32[384]{0:T(512)S(1)} %add_rsqrt_fusion, f32[2048]{0:T(1024)S(1)} %bitcast.121), kind=kOutput, calls=%fused_computation.32 | convolution fusion | flops 1615855616 | bytes 6563328 | tf_op jit(solution)/shard_map/dot_general | solution.py:38
  322.4 3.0 fusion.53.rest_5_
  326.0 91.1 %sum_back_last.1 = (bf16[384,256]{1,0:T(8,128)(2,1)}, bf16[384,256]{1,0:T(8,128)(2,1)}, f32[16,256]{1,0:T(8,128)}, f32[256,1024]{1,0:T(8,128)}, f32[256,384]{1,0...) custom-call(bf16[384,2048]{1,0:T(8,128)(2,1)} %get-tuple-element.105.part, f32[8,128]{1,0:T(8,128)} %concatenate.54.line, ...), custom_call_target="tpu_custom_call" | custom-call | tf_op jit(solution)/shard_map/sum_back_last/pallas_call | solution.py:855
  417.1 1.8 slice_bitcast_fusion
  418.9 1.1 slice_bitcast_fusion.1
  420.0 1.3 fusion.88
  421.3 0.7 copy.40
  422.0 0.7 copy.41
  422.7 1.0 maximum_bitcast_fusion
  425.2 1.0 copy.47
  426.2 1.0 copy.48
  (156 shorter events, 10.9 us)
Async XLA Ops:
  7.2 39.3 %copy-start = (bf16[1,256,2048]{2,1,0:T(8,128)(2,1)S(1)}, bf16[1,256,2048]{2,1,0:T(8,128)(2,1)}, u32[]{:S(2)}) copy-start(bf16[1,256,2048]{2,1,0:T(8,128)(2,1)} %param.19) | copy-start | bytes 3145732
  7.2 17.8 %copy-start.39 = (bf16[1,2048]{1,0:T(2,128)(2,1)S(1)}, bf16[1,2048]{1,0:T(2,128)(2,1)}, u32[]{:S(2)}) copy-start(bf16[1,2048]{1,0:T(2,128)(2,1)} %param.15) | copy-start | bytes 12292
  7.2 148.9 %all-gather.2.cloned.1.call-start = ((), (), s32[]{:S(2)}) async-start(), calls=%async_computation | async-start | bytes 1769472 | tf_op jit(solution)/shard_map/all_gather | solution.py:1253
  8.9 16.5 %copy-start.35 = (bf16[1,2048,64]{1,2,0:T(8,128)(2,1)S(1)}, bf16[1,2048,64]{1,2,0:T(8,128)(2,1)}, u32[]{:S(2)}) copy-start(bf16[1,2048,64]{1,2,0:T(8,128)(2,1)} %param.18) | copy-start | bytes 786436
  25.7 4.6 %copy-start.27 = (bf16[2048,64]{1,0:T(8,128)(2,1)}, bf16[2048,64]{1,0:T(8,128)(2,1)S(1)}, u32[]{:S(2)}) copy-start(bf16[2048,64]{1,0:T(8,128)(2,1)S(1)} %copy.35) | copy-start | bytes 786436
  27.8 2.6 copy-start.21
  46.5 23.6 %copy-start.43 = (bf16[1,2048,1024]{2,1,0:T(8,128)(2,1)S(1)}, bf16[1,2048,1024]{2,1,0:T(8,128)(2,1)}, u32[]{:S(2)}) copy-start(bf16[1,2048,1024]{2,1,0:T(8,128)(2,1)} %param.21) | copy-start | bytes 12582916
  47.4 22.3 %copy-start.40 = (bf16[1,2048]{1,0:T(2,128)(2,1)S(1)}, bf16[1,2048]{1,0:T(2,128)(2,1)}, u32[]{:S(2)}) copy-start(bf16[1,2048]{1,0:T(2,128)(2,1)} %param.20) | copy-start | bytes 12292
  70.0 2.2 copy-start.41
  76.3 28.6 %copy-start.28 = (bf16[2048,64]{1,0:T(8,128)(2,1)S(1)}, bf16[2048,64]{1,0:T(8,128)(2,1)}, u32[]{:S(2)}) copy-start(bf16[2048,64]{1,0:T(8,128)(2,1)} %copy-done.27) | copy-start | bytes 786436
  76.3 28.6 %copy-start.30 = (bf16[2048,64]{1,0:T(8,128)(2,1)S(1)}, bf16[2048,64]{1,0:T(8,128)(2,1)}, u32[]{:S(2)}) copy-start(bf16[2048,64]{1,0:T(8,128)(2,1)} %copy.34) | copy-start | bytes 786436
  76.3 28.6 %copy-start.49 = (bf16[1,2048,256]{2,1,0:T(8,128)(2,1)S(1)}, bf16[1,2048,256]{2,1,0:T(8,128)(2,1)}, u32[]{:S(2)}) copy-start(bf16[1,2048,256]{2,1,0:T(8,128)(2,1)} %param.16) | copy-start | bytes 3145732
  106.1 105.5 %copy-start.7 = (f32[384,1]{1,0:T(8,128)}, f32[384,1]{1,0:T(8,128)S(1)}, u32[]{:S(2)}) copy-start(f32[384,1]{1,0:T(8,128)S(1)} %rsqrt.33.factor) | copy-start | bytes 4612
  106.2 105.4 %copy-start.1 = (f32[384,256]{1,0:T(8,128)}, f32[384,256]{1,0:T(8,128)S(1)}, u32[]{:S(2)}) copy-start(f32[384,256]{1,0:T(8,128)S(1)} %convert_element_type.131.own) | copy-start | bytes 1179652
  122.2 23.6 %copy-start.3 = (f32[2,128,768]{2,1,0:T(8,128)}, f32[2,128,768]{2,1,0:T(8,128)S(1)}, u32[]{:S(2)}) copy-start(f32[2,128,768]{2,1,0:T(8,128)S(1)} %get-tuple-element.47.mixed) | copy-start | bytes 2359300
  122.2 23.6 %copy-start.5 = (bf16[8,2,192,128]{3,2,1,0:T(8,128)(2,1)}, bf16[8,2,192,128]{3,2,1,0:T(8,128)(2,1)S(1)}, u32[]{:S(2)}) copy-start(bf16[8,2,192,128]{3,2,1,0:T(8,128)(2,1)S(1)} %get-tuple-element.45.kv) | copy-start | bytes 2359300
  145.9 20.7 %copy-start.2 = (f32[384,256]{1,0:T(8,128)}, f32[384,256]{1,0:T(8,128)S(1)}, u32[]{:S(2)}) copy-start(f32[384,256]{1,0:T(8,128)S(1)} %get-tuple-element.51.own.rest_6_) | copy-start | bytes 1179652
  147.2 19.5 %copy-start.8 = (f32[384,1]{1,0:T(8,128)}, f32[384,1]{1,0:T(8,128)S(1)}, u32[]{:S(2)}) copy-start(f32[384,1]{1,0:T(8,128)S(1)} %rsqrt.32.factor) | copy-start | bytes 4612
  147.2 19.4 %copy-start.23 = (f32[1,256]{1,0:T(1,128)}, f32[1,256]{1,0:T(1,128)S(1)}, u32[]{:S(2)}) copy-start(f32[1,256]{1,0:T(1,128)S(1)} %get-tuple-element.136.gain) | copy-start | bytes 3076
  147.2 64.4 %copy-start.22 = (f32[1,256]{1,0:T(1,128)}, f32[1,256]{1,0:T(1,128)S(1)}, u32[]{:S(2)}) copy-start(f32[1,256]{1,0:T(1,128)S(1)} %get-tuple-element.135.gain) | copy-start | bytes 3076
  147.2 5.8 %copy-start.15 = (bf16[384,2048]{1,0:T(8,128)(2,1)S(1)}, bf16[384,2048]{1,0:T(8,128)(2,1)}, u32[]{:S(2)}) copy-start(bf16[384,2048]{1,0:T(8,128)(2,1)} %copy-done.14) | copy-start | bytes 4718596
  147.2 5.8 %copy-start.44 = (bf16[1,2048,1024]{2,1,0:T(8,128)(2,1)S(1)}, bf16[1,2048,1024]{2,1,0:T(8,128)(2,1)}, u32[]{:S(2)}) copy-start(bf16[1,2048,1024]{2,1,0:T(8,128)(2,1)} %param.21) | copy-start | bytes 12582916
  156.1 4.6 %copy-start.42 = (bf16[1,2048,1024]{2,1,0:T(8,128)(2,1)S(1)}, bf16[1,2048,1024]{2,1,0:T(8,128)(2,1)}, u32[]{:S(2)}) copy-start(bf16[1,2048,1024]{2,1,0:T(8,128)(2,1)} %param.22) | copy-start | bytes 12582916
  156.1 4.6 %copy-start.57 = (f32[384,1024]{1,0:T(8,128)S(1)}, f32[384,1024]{1,0:T(8,128)}, u32[]{:S(2)}) copy-start(f32[384,1024]{1,0:T(8,128)} %fusion.20) | copy-start | bytes 4718596
  160.7 2.7 copy-start.45
  160.8 3.1 copy-start.56
  163.9 2.8 copy-start.11
  191.1 19.2 %copy-start.50 = (bf16[1,2048,256]{2,1,0:T(8,128)(2,1)S(1)}, bf16[1,2048,256]{2,1,0:T(8,128)(2,1)}, u32[]{:S(2)}) copy-start(bf16[1,2048,256]{2,1,0:T(8,128)(2,1)} %param.16) | copy-start | bytes 3145732
  191.8 18.5 %copy-start.13 = (bf16[384,2048]{1,0:T(8,128)(2,1)S(1)}, bf16[384,2048]{1,0:T(8,128)(2,1)}, u32[]{:S(2)}) copy-start(bf16[384,2048]{1,0:T(8,128)(2,1)} %copy-done.12) | copy-start | bytes 4718596
  191.8 18.5 %copy-start.29 = (bf16[2048,64]{1,0:T(8,128)(2,1)S(1)}, bf16[2048,64]{1,0:T(8,128)(2,1)}, u32[]{:S(2)}) copy-start(bf16[2048,64]{1,0:T(8,128)(2,1)} %copy-done.27) | copy-start | bytes 786436
  191.8 18.5 %copy-start.31 = (bf16[2048,64]{1,0:T(8,128)(2,1)S(1)}, bf16[2048,64]{1,0:T(8,128)(2,1)}, u32[]{:S(2)}) copy-start(bf16[2048,64]{1,0:T(8,128)(2,1)} %copy.34) | copy-start | bytes 786436
  210.3 29.7 %copy-start.47 = (bf16[1,1024,2048]{2,1,0:T(8,128)(2,1)S(1)}, bf16[1,1024,2048]{2,1,0:T(8,128)(2,1)}, u32[]{:S(2)}) copy-start(bf16[1,1024,2048]{2,1,0:T(8,128)(2,1)} %param.23) | copy-start | bytes 12582916
  240.0 2.5 copy-start.20
  242.5 2.7 copy-start.52
  242.5 11.6 %copy-start.54 = (bf16[384,1024]{1,0:T(8,128)(2,1)}, bf16[384,1024]{1,0:T(8,128)(2,1)S(1)}, u32[]{:S(2)}) copy-start(bf16[384,1024]{1,0:T(8,128)(2,1)S(1)} %get-tuple-element.107) | copy-start | bytes 2359300
  300.9 10.4 %copy-start.32 = (bf16[2048,64]{1,0:T(8,128)(2,1)S(1)}, bf16[2048,64]{1,0:T(8,128)(2,1)}, u32[]{:S(2)}) copy-start(bf16[2048,64]{1,0:T(8,128)(2,1)} %copy.34) | copy-start | bytes 786436
  300.9 10.4 %copy-start.51 = (bf16[1,2048,256]{2,1,0:T(8,128)(2,1)S(1)}, bf16[1,2048,256]{2,1,0:T(8,128)(2,1)}, u32[]{:S(2)}) copy-start(bf16[1,2048,256]{2,1,0:T(8,128)(2,1)} %param.16) | copy-start | bytes 3145732
  313.6 2.6 copy-start.19
  313.6 2.6 copy-start.24
  317.9 4.5 %copy-start.48 = (bf16[1,1024,2048]{2,1,0:T(8,128)(2,1)S(1)}, bf16[1,1024,2048]{2,1,0:T(8,128)(2,1)}, u32[]{:S(2)}) copy-start(bf16[1,1024,2048]{2,1,0:T(8,128)(2,1)} %param.23) | copy-start | bytes 12582916
  317.9 4.5 %copy-start.53 = (bf16[384,1024]{1,0:T(8,128)(2,1)S(1)}, bf16[384,1024]{1,0:T(8,128)(2,1)}, u32[]{:S(2)}) copy-start(bf16[384,1024]{1,0:T(8,128)(2,1)} %copy-done.52) | copy-start | bytes 2359300
  417.1 5.7 %copy-start.33 = (f32[512,256]{1,0:T(8,128)S(1)}, f32[512,256]{1,0:T(8,128)}, u32[]{:S(2)}) copy-start(f32[512,256]{1,0:T(8,128)} %get-tuple-element.70) | copy-start | bytes 1572868
  417.1 5.7 %copy-start.34 = (f32[512,256]{1,0:T(8,128)S(1)}, f32[512,256]{1,0:T(8,128)}, u32[]{:S(2)}) copy-start(f32[512,256]{1,0:T(8,128)} %get-tuple-element.71) | copy-start | bytes 1572868
  418.9 4.9 %copy-start.37 = (bf16[384,256]{1,0:T(8,128)(2,1)S(1)}, bf16[384,256]{1,0:T(8,128)(2,1)}, u32[]{:S(2)}) copy-start(bf16[384,256]{1,0:T(8,128)(2,1)} %get-tuple-element.63) | copy-start | bytes 589828
  418.9 4.9 %copy-start.38 = (bf16[384,256]{1,0:T(8,128)(2,1)S(1)}, bf16[384,256]{1,0:T(8,128)(2,1)}, u32[]{:S(2)}) copy-start(bf16[384,256]{1,0:T(8,128)(2,1)} %get-tuple-element.64) | copy-start | bytes 589828
  420.0 4.5 %copy-start.36 = (f32[256,256]{1,0:T(8,128)S(1)}, f32[256,256]{1,0:T(8,128)}, u32[]{:S(2)}) copy-start(f32[256,256]{1,0:T(8,128)} %get-tuple-element.67) | copy-start | bytes 786436
  422.7 2.5 copy-start.26
  423.8 2.4 copy-start.25
  (11 other events, 15.2 us)
Sparse Core Ops, SparseCore 0:
  9.7 28.9 all-gather.1

commit v4 on v3

--- a/solution.py
+++ b/solution.py
@@ -469,12 +469,22 @@
 
 class XFirst:
     def __init__(self, place, array, dim, out, scratch):
-        self.place, self.array, self.dim, self.out = place, array, dim, out
-        (self.held, bufs, summed, self.swapped, self.lsem, sems, self.ssend, self.srecv) = scratch
-        held = self.held
+        self.place, self.out = place, out
+        bufs, summed, self.swapped, sems, self.ssend, self.srecv, *held = scratch
+        self.held, self.lsem = held if held else (None, None)
+
+        def block(k, y):
+            return cut(array, dim, place.at(k, y))
+
+        def loaded(k, y):
+            if held and k in (0, way(y)):
+                return self.held.at[abs(k), y]
+            return block(k, y)
+
+        self.block = block
         self.rings = [
             XRing(
-                place, way(y), lambda k, y=y: held.at[k % 4, y],
+                place, way(y), lambda k, y=y: loaded(k, y),
                 [bufs.at[y, j] for j in range(3)] + [summed.at[y]],
                 [sems.at[0, y], sems.at[1, y]],
             )
@@ -482,23 +492,22 @@
         ]
 
     def start(self):
-        self.loads = {}
-        for k in BLOCKS:
+        self.loads = []
+        for y, ring in enumerate(self.rings):
+            ring.start(2)
+            ring.start(-ring.s)
+        if self.held is not None:
             for y in (0, 1):
-                copy = pltpu.make_async_copy(
-                    cut(self.array, self.dim, self.place.at(k, y)), self.held.at[k % 4, y],
-                    self.lsem.at[k % 4, y],
-                )
-                copy.start()
-                self.loads[k, y] = copy
-
-    def first(self):
-        for k in BLOCKS:
-            for y in (0, 1):
-                self.loads[k, y].wait()
-                self.rings[y].start(k)
+                for k in (way(y), 0):
+                    copy = pltpu.make_async_copy(
+                        self.block(k, y), self.held.at[abs(k), y], self.lsem.at[abs(k), y]
+                    )
+                    copy.start()
+                    self.loads.append(copy)
 
     def join(self):
+        for copy in self.loads:
+            copy.wait()
         for ring in self.rings:
             ring.join()
 
@@ -524,7 +533,7 @@
 class YFirst:
     def __init__(self, place, array, dim, out, scratch):
         self.place, self.array, self.dim, self.out = place, array, dim, out
-        (self.held, bufs, summed, self.swapped, self.lsem, sems, self.ssend, self.srecv) = scratch
+        (bufs, summed, self.swapped, sems, self.ssend, self.srecv, self.held, self.lsem) = scratch
         swapped = self.swapped
         self.half = half = self.held.shape[1] // 2
         self.rings = [
@@ -578,70 +587,26 @@
             copy.wait_send()
 
 
-def ctx_scratch(shapes, dims, modes):
-    scratch = []
-    for shape, dim, mode in zip(shapes, dims, modes):
-        rows, width = owned(shape, dim)
-        if mode == "x":
-            held, ring = (4, 2, rows, width), (2, 3, rows, width)
-        else:
-            held, ring = (4, rows, width), (2, 3, rows // 2, width)
-        scratch += [
-            pltpu.VMEM(held, bf16),
-            pltpu.VMEM(ring, bf16),
-            pltpu.VMEM((2, *ring[2:]), bf16),
-            pltpu.VMEM((3 if mode == "x" else 4, rows, width), bf16),
-            pltpu.SemaphoreType.DMA((4, 2) if mode == "x" else (4,)),
-            pltpu.SemaphoreType.DMA((2, 2, 3)),
-            pltpu.SemaphoreType.DMA((4,)),
-            pltpu.SemaphoreType.DMA((4,)),
-        ]
-    return scratch
-
-
 def owned(shape, dim):
     return tuple(n // 8 if i == dim else n for i, n in enumerate(shape))
 
 
-class CtxSums:
-    def __init__(self, place, arrays, dims, modes, outs, scratch):
-        sums = [
-            (XFirst if mode == "x" else YFirst)(
-                place, arrays[i], dims[i], outs[i], scratch[8 * i : 8 * i + 8]
-            )
-            for i, mode in enumerate(modes)
-        ]
-        self.xs = [one for one, mode in zip(sums, modes) if mode == "x"]
-        self.ys = [one for one, mode in zip(sums, modes) if mode == "y"]
-
-    def start(self):
-        for one in self.xs + self.ys:
-            one.start()
-
-    def first(self):
-        for one in self.xs:
-            one.first()
-
-    def middle(self):
-        for one in self.ys[:-1]:
-            one.first()
-            one.join()
-        for one in self.xs:
-            one.join()
-        for one in self.ys[-1:]:
-            one.first()
-
-    def later(self):
-        for one in self.xs:
-            one.swap()
-        for one in self.ys[-1:]:
-            one.join()
-
-    def end(self):
-        for one in self.ys[:-1] + self.xs + self.ys[-1:]:
-            one.total()
-        for one in self.xs + self.ys:
-            one.finish()
+def ctx_scratch(shape, dim, mode):
+    rows, width = owned(shape, dim)
+    ring = (rows // 2 if mode == "y" else rows, width)
+    scratch = [
+        pltpu.VMEM((2, 3, *ring), bf16),
+        pltpu.VMEM((2, *ring), bf16),
+        pltpu.VMEM((4 if mode == "y" else 3, rows, width), bf16),
+        pltpu.SemaphoreType.DMA((2, 2, 3)),
+        pltpu.SemaphoreType.DMA((4,)),
+        pltpu.SemaphoreType.DMA((4,)),
+    ]
+    if mode == "y":
+        scratch += [pltpu.VMEM((4, rows, width), bf16), pltpu.SemaphoreType.DMA((4,))]
+    elif mode == "x":
+        scratch += [pltpu.VMEM((2, 2, rows, width), bf16), pltpu.SemaphoreType.DMA((2, 2))]
+    return scratch
 
 
 def everyone(place):
@@ -672,78 +637,54 @@
             copy.wait_send()
 
 
-def backward_kernel(mode, chunks, dims, modes, part, line, above, own, factor, gain, *rest):
-    count = len(dims)
-    arrays, rest = rest[:count], rest[count:]
+def norm_back(total, above, own, scale, gain, mean):
+    normed = own * scale
+    grad = above.astype(f32) + scale * (total * gain - normed * mean)
+    return grad, jnp.sum(total * normed, axis=0, keepdims=True)
+
+
+def backward_kernel(mode, chunks, part, line, above, own, factor, gain, *rest):
     if mode == "mid":
-        share, piece, whole, *rest = rest
-    elif mode == "pass":
-        begin, share, whole, *rest = rest
+        share, whole, agsrc, *rest = rest
     else:
-        other, last_part, last_mid, share, result, gain_out, *rest = rest
-    outs, rest = rest[:count], rest[count:]
-    scratch, rest = rest[: 8 * count], rest[8 * count :]
-    if mode == "mid":
-        agsrc, *rest = rest
-    elif mode == "pass":
-        agsrc, arrived, xsend, xrecv, *rest = rest
-    else:
-        piece, pieces, gsend, grecv, gain_slots, osend, orecv, *rest = rest
-        last_bufs, rest = rest[:7], rest[7:]
+        begin, share, whole, agsrc, arrived, xsend, xrecv, *rest = rest
     slots, lsend, lrecv, *rest = rest
     bufs, sems = rest[:7], rest[7:]
-    place, ctx = WtPlace(own.shape[1]), CtxPlace()
+    place = WtPlace(own.shape[1])
     section = lax.axis_index("section")
     greet(
         [{"wt": peer} for peer in everyone(place)]
         + ([{"section": 1 - section}] if mode == "pass" else [])
-        + (ctx.all() if mode == "last" else ctx.near() if count else [])
     )
     rows = own.shape[0] // chunks
     depth = 8 * own.shape[1]
     spans = [pl.ds(q * rows, rows) for q in range(chunks)]
     sums = [Reduce(place, part, bufs, q, spans[q]) for q in range(chunks)]
-    gathers = [Gather(place, whole, sems, q, spans[q]) for q in range(chunks)] if (
-        mode != "last") else []
+    gathers = [Gather(place, whole, sems, q, spans[q]) for q in range(chunks)]
     lines = Lines(place, line, slots, lsend, lrecv)
-    beside = CtxSums(ctx, arrays, dims, modes, outs, scratch) if count else None
     lines.start()
     for one in sums:
         one.start()
-    if beside:
-        beside.start()
     for one in sums:
         one.pass_on()
-    if beside:
-        beside.first()
     for one in sums:
         one.pass_more()
     mean = column(lines.total(), own.shape[0] // 128) * (1.0 / depth)
     swaps = []
-    terms = jnp.zeros((1, own.shape[1]), f32)
     for q in range(chunks):
         span = spans[q]
-        total = sums[q].total()
-        scale = factor[span, :]
-        normed = own[span, :] * scale
-        if mode != "pass":
-            terms = terms + jnp.sum(total * normed, axis=0, keepdims=True)
-        grad = above[span, :].astype(f32) + scale * (
-            total * gain[...] - normed * mean[q * rows : (q + 1) * rows]
-        )
+        grad, _ = norm_back(
+            sums[q].total(), above[span, :], own[span, :], factor[span, :], gain[...],
+            mean[q * rows : (q + 1) * rows],
+        )
+        agsrc[span, :] = grad.astype(bf16)
         if mode == "mid":
             share[span, :] = grad
-            agsrc[span, :] = grad.astype(bf16)
             gathers[q].start(agsrc.at[span])
-        elif mode == "pass":
-            agsrc[span, :] = grad.astype(bf16)
+        else:
             swap = swap_sections(agsrc.at[span], arrived.at[span], xsend.at[q], xrecv.at[q])
             swap.start()
             swaps.append(swap)
-        else:
-            share[span, :] = grad.astype(bf16)
-    if mode == "mid":
-        piece[...] = jnp.broadcast_to(terms, piece.shape)
     if mode == "pass":
         for q in range(chunks):
             span = spans[q]
@@ -752,116 +693,43 @@
                 section == 1, begin[span, :].astype(f32), arrived[span, :].astype(f32)
             ).astype(bf16)
             gathers[q].start(share.at[span])
-    if mode == "last":
-        piece[0:8, :] = jnp.broadcast_to(terms, (8, own.shape[1]))
-        piece[8:16, :] = other[...]
-        piece_copies = [
-            remote(
-                piece, pieces.at[place.me], gsend.at[d], grecv.at[d],
-                {"wt": lax.rem(place.me + d, 8)},
-            )
-            for d in range(1, 8)
-        ]
-        for copy in piece_copies:
-            copy.start()
-        last_sums = [Reduce(place, last_part, last_bufs, q, spans[q]) for q in range(chunks)]
-        for one in last_sums:
-            one.start()
-        for one in last_sums:
-            one.pass_on()
-        pieces[place.me] = piece[...]
-        for copy in piece_copies:
-            copy.wait()
-        owner_copies = []
-        for d in range(1, 8):
-            owner = lax.rem(ctx.me + d, 8)
-            copy = remote(
-                pieces.at[owner], gain_slots.at[d], osend.at[d], orecv.at[d], {"ctx": owner}
-            )
-            copy.start()
-            owner_copies.append(copy)
-        for one in last_sums:
-            one.pass_more()
-        for q in range(chunks):
-            span = spans[q]
-            result[span, :] = (last_mid[span, :] + last_sums[q].total()).astype(bf16)
-        sums = sums + last_sums
-    for one in gathers:
-        one.forward()
-    for one in gathers:
-        one.forward_more()
-    if beside:
-        beside.middle()
-    for one in gathers:
-        one.finish()
+    gather_all(gathers)
     for one in sums:
         one.finish()
     for one in swaps:
         one.wait_send()
     lines.finish()
-    if beside:
-        beside.later()
-    if mode == "last":
-        total = pieces[ctx.me]
-        for d, copy in enumerate(owner_copies, start=1):
-            copy.wait_recv()
-            total = total + gain_slots[d]
-        gain_out[...] = total
-        for copy in owner_copies:
-            copy.wait_send()
-    if beside:
-        beside.end()
-
-
-def backward_sum(
-    mode, part, line, above, own, factor, gain, arrays, dims, modes, extra, collective_id,
-    chunks=4
-):
+
+
+def seven():
+    return [pltpu.SemaphoreType.DMA((8,)), pltpu.SemaphoreType.DMA((8,))]
+
+
+def backward_sum(mode, part, line, above, own, factor, gain, extra, collective_id, chunks=4):
     rows, width = own.shape
     vmem = pl.BlockSpec(memory_space=pltpu.VMEM)
     hbm = pl.BlockSpec(memory_space=pl.ANY)
-    whole = jax.ShapeDtypeStruct((rows, 8 * width), bf16)
-    one_sum = reduce_scratch(chunks, rows // chunks, width)
-    seven = [pltpu.SemaphoreType.DMA((8,)), pltpu.SemaphoreType.DMA((8,))]
-    if mode == "mid":
-        out_shape = (
-            jax.ShapeDtypeStruct((rows, width), f32),
-            jax.ShapeDtypeStruct((8, width), f32),
-            whole,
-        )
-        out_specs = (vmem, vmem, hbm)
-        scratch = [pltpu.VMEM((rows, width), bf16)]
-    elif mode == "pass":
-        out_shape = (jax.ShapeDtypeStruct((rows, width), bf16), whole)
-        out_specs = (vmem, hbm)
-        scratch = [pltpu.VMEM((rows, width), bf16)] * 2 + [
+    scratch = [pltpu.VMEM((rows, width), bf16)]
+    if mode == "pass":
+        scratch += [
+            pltpu.VMEM((rows, width), bf16),
             pltpu.SemaphoreType.DMA((chunks,)),
             pltpu.SemaphoreType.DMA((chunks,)),
         ]
-    else:
-        out_shape = (
-            jax.ShapeDtypeStruct((rows, width), bf16),
-            jax.ShapeDtypeStruct((rows, width), bf16),
-            jax.ShapeDtypeStruct((16, width), f32),
-        )
-        out_specs = (vmem, vmem, vmem)
-        scratch = [pltpu.VMEM((16, width), f32), pltpu.VMEM((8, 16, width), f32)]
-        scratch += seven + [pltpu.VMEM((8, 16, width), f32)] + seven + one_sum
-    scratch += [pltpu.VMEM((8, 8, 128), f32)] + seven + one_sum
-    if mode != "last":
-        scratch += gather_scratch(chunks)
-    operands = [part, line, above, own, factor, gain] + arrays + extra
-    shapes = [array.shape for array in arrays]
+    scratch += [pltpu.VMEM((8, 8, 128), f32)] + seven()
+    scratch += reduce_scratch(chunks, rows // chunks, width) + gather_scratch(chunks)
+    operands = [part, line, above, own, factor, gain] + extra
     return pl.pallas_call(
-        functools.partial(backward_kernel, mode, chunks, dims, modes),
-        out_shape=out_shape
-        + tuple(jax.ShapeDtypeStruct(owned(*one), f32) for one in zip(shapes, dims)),
-        in_specs=[vmem] * 6 + [hbm] * len(arrays) + [vmem] * len(extra),
-        out_specs=out_specs + (vmem,) * len(arrays),
-        scratch_shapes=ctx_scratch(shapes, dims, modes) + scratch,
+        functools.partial(backward_kernel, mode, chunks),
+        out_shape=(
+            jax.ShapeDtypeStruct((rows, width), f32 if mode == "mid" else bf16),
+            jax.ShapeDtypeStruct((rows, 8 * width), bf16),
+        ),
+        in_specs=[vmem] * len(operands),
+        out_specs=(vmem, hbm),
+        scratch_shapes=scratch,
         compiler_params=pltpu.CompilerParams(
-            collective_id=collective_id, has_side_effects=True,
-            vmem_limit_bytes=(56 if arrays else 32) * MiB,
+            collective_id=collective_id, has_side_effects=True, vmem_limit_bytes=32 * MiB
         ),
         name="sum_back_" + mode,
     )(*operands)
@@ -1032,15 +900,18 @@
     )(bounds, flat, kv_pre, cosine, sine, kv_cosine, kv_sine)
 
 
-def attention_back_kernel(
-    n, bounds, flat, cosine, sine, kv_cosine, kv_sine, kv, logs, mixed, grad, out, grad_kv,
-    terms, slots, total, stacked, grads, acc, send, recv
+def attention_back_kernel(n, *refs):
+    me = lax.axis_index("ctx")
+    attention_back_steps(n, me, greet_order(me, n, later, me), *refs)
+
+
+def attention_back_steps(
+    n, me, wait, bounds, flat, cosine, sine, kv_cosine, kv_sine, kv, logs, mixed, grad, out,
+    grad_kv, terms, slots, total, stacked, grads, acc, send, recv
 ):
-    me = lax.axis_index("ctx")
     rows = kv.shape[2]
     heads = 4
     low = lanes((rows, 128)) < HD
-    wait = greet_order(me, n, later, me)
     deltas = []
     for b in range(2):
         stack_queries(flat, cosine, sine, b, rows, stacked)
@@ -1113,6 +984,20 @@
             copy(d).wait_send()
 
 
+def attention_back_scratch(shape):
+    n, two, rows, width = shape
+    return [
+        pltpu.VMEM(shape, bf16),
+        pltpu.VMEM(shape, bf16),
+        pltpu.VMEM((2, rows, width), f32),
+        pltpu.VMEM((2, 4 * rows, 128), bf16),
+        pltpu.VMEM((2, 4 * rows, 128), bf16),
+        pltpu.VMEM((2, 128, 4 * rows), f32),
+        pltpu.SemaphoreType.DMA((n,)),
+        pltpu.SemaphoreType.DMA((n,)),
+    ]
+
+
 def attention_back(
     bounds, flat, cosine, sine, kv_cosine, kv_sine, kv, logs, mixed, grad, collective_id
 ):
@@ -1126,21 +1011,246 @@
         ),
         in_specs=[pl.BlockSpec(memory_space=pltpu.SMEM)] + [vmem] * 9,
         out_specs=(vmem, vmem),
-        scratch_shapes=[
-            pltpu.VMEM(kv.shape, bf16),
-            pltpu.VMEM(kv.shape, bf16),
-            pltpu.VMEM((2, rows, width), f32),
-            pltpu.VMEM((2, 4 * rows, 128), bf16),
-            pltpu.VMEM((2, 4 * rows, 128), bf16),
-            pltpu.VMEM((2, 128, 4 * rows), f32),
-            pltpu.SemaphoreType.DMA((n,)),
-            pltpu.SemaphoreType.DMA((n,)),
-        ],
+        scratch_shapes=attention_back_scratch(kv.shape),
         compiler_params=pltpu.CompilerParams(
             collective_id=collective_id, has_side_effects=True, vmem_limit_bytes=40 * MiB
         ),
         name="attention_back",
     )(bounds, flat, cosine, sine, kv_cosine, kv_sine, kv, logs, mixed, grad)
+
+
+def as_line(column_values, line):
+    eye = lax.broadcasted_iota(jnp.int32, (128, 128), 0) == lax.broadcasted_iota(
+        jnp.int32, (128, 128), 1
+    )
+    line[...] = jnp.zeros_like(line)
+    for j in range(column_values.shape[0] // 128):
+        block = column_values[128 * j : 128 * j + 128]
+        line[j : j + 1, :] = jnp.sum(
+            jnp.where(eye, jnp.broadcast_to(block, (128, 128)), 0.0), axis=0, keepdims=True
+        )
+
+
+CTX_NAMES = ("down_a", "up", "down_b", "gate", "pre", "out")
+CTX_DIMS = dict(down_a=1, up=0, down_b=1, gate=0, pre=0, out=1)
+CTX_MODES = dict(down_a="x", up="x", down_b="y", gate="y", pre="local", out="local")
+
+
+def end_kernel(n, chunks, names, *refs):
+    r, at = {}, 0
+    for name, count in names:
+        r[name] = refs[at] if count == 1 else refs[at : at + count]
+        at += count
+    place, ctx = WtPlace(r["mid"].shape[1]), CtxPlace()
+    greet([{"wt": peer} for peer in everyone(place)] + ctx.all())
+    width = r["mid"].shape[1]
+    all_rows = r["mid"].shape[0]
+    rows = all_rows // chunks
+    depth = 8 * width
+    spans = [pl.ds(q * rows, rows) for q in range(chunks)]
+    blocks = [pl.ds(width * c, width) for c in range(8)]
+    inner_sums = {
+        name: (YFirst if CTX_MODES[name] == "y" else XFirst)(
+            ctx, r[name], CTX_DIMS[name], r["own_" + name], r["sum_" + name]
+        )
+        for name in CTX_NAMES
+    }
+    down_a, up, down_b, gate, pre, out = (inner_sums[name] for name in CTX_NAMES)
+
+    sums = [Reduce(place, r["part"], r["reduce"], q, spans[q]) for q in range(chunks)]
+    gathers = [Gather(place, r["whole"], r["gather"], q, spans[q]) for q in range(chunks)]
+    lines = Lines(place, r["line"], *r["slots"])
+    lines.start()
+    for one in sums:
+        one.start()
+    for one in (down_a, up, down_b, gate):
+        one.start()
+    for one in sums:
+        one.pass_on()
+    for one in sums:
+        one.pass_more()
+    mean = column(lines.total(), all_rows // 128) * (1.0 / depth)
+    terms = jnp.zeros((1, width), f32)
+    for q in range(chunks):
+        span = spans[q]
+        grad, term = norm_back(
+            sums[q].total(), r["above"][span, :], r["mid"][span, :], r["mid_factor"][span, :],
+            r["mid_gain"][...], mean[q * rows : (q + 1) * rows],
+        )
+        terms = terms + term
+        r["grad_mid"][span, :] = grad
+        r["agsrc"][span, :] = grad.astype(bf16)
+        gathers[q].start(r["agsrc"].at[span])
+    r["piece"][8:16, :] = jnp.broadcast_to(terms, (8, width))
+    for one in gathers:
+        one.forward()
+    for one in gathers:
+        one.forward_more()
+    down_a.join()
+    for one in gathers:
+        one.finish()
+    last_sums = [
+        Reduce(place, r["last_part"], r["last_reduce"], q, spans[q]) for q in range(chunks)
+    ]
+    for one in last_sums:
+        one.start()
+    r["grad_mix"][...] = times_transposed(r["whole"][...], r["w_out"][...]).astype(bf16)
+    for one in last_sums:
+        one.pass_on()
+    down_b.first()
+
+    grad_pre = r["grad_pre"]
+    attention_back_steps(
+        n, ctx.me, lambda: None, r["bounds"], r["flat"], r["cosine"], r["sine"],
+        r["kv_cosine"], r["kv_sine"], r["kv"], r["logs"], r["mixed"], r["grad_mix"],
+        grad_pre.at[:, pl.ds(0, 256)], grad_pre.at[:, pl.ds(256, 128)], *r["attention"]
+    )
+    up.join()
+    for one in last_sums:
+        one.pass_more()
+
+    dots = jnp.zeros((all_rows, 1), f32)
+    for block in blocks:
+        partial_sum = times_transposed(grad_pre[...], r["w_qkv"][block, :])
+        dots = dots + jnp.sum(
+            partial_sum * r["attn_in"][:, block].astype(f32), axis=1, keepdims=True
+        )
+        r["part_in"][:, block] = partial_sum.astype(bf16)
+    as_line(dots, r["line_in"])
+    lines_in = Lines(place, r["line_in"], *r["slots_in"])
+    lines_in.start()
+    sums_in = [Reduce(place, r["part_in"], r["reduce_in"], q, spans[q]) for q in range(chunks)]
+    for one in sums_in:
+        one.start()
+    for one in sums_in:
+        one.pass_on()
+    down_b.join()
+    for block in blocks:
+        r["pre"][block, :] = contract_rows(r["attn_in"][:, block], grad_pre[...]).astype(bf16)
+    pre.start()
+    for one in sums_in:
+        one.pass_more()
+    for block in blocks:
+        r["out"][:, block] = contract_rows(r["mix"][...], r["whole"][:, block]).astype(bf16)
+    out.start()
+    mean = column(lines_in.total(), all_rows // 128) * (1.0 / depth)
+    terms = jnp.zeros((1, width), f32)
+    for q in range(chunks):
+        span = spans[q]
+        grad, term = norm_back(
+            sums_in[q].total(), r["grad_mid"][span, :], r["hidden"][span, :],
+            r["factor"][span, :], r["gain"][...], mean[q * rows : (q + 1) * rows],
+        )
+        terms = terms + term
+        r["first_grad"][span, :] = grad.astype(bf16)
+    r["piece"][0:8, :] = jnp.broadcast_to(terms, (8, width))
+    piece, pieces = r["piece"], r["pieces"]
+    gsend, grecv = r["piece_sems"]
+    piece_copies = [
+        remote(
+            piece, pieces.at[place.me], gsend.at[d], grecv.at[d],
+            {"wt": lax.rem(place.me + d, 8)},
+        )
+        for d in range(1, 8)
+    ]
+    for copy in piece_copies:
+        copy.start()
+    pieces[place.me] = piece[...]
+    down_a.swap()
+    up.swap()
+    for q in range(chunks):
+        span = spans[q]
+        r["result"][span, :] = (r["last_mid"][span, :] + last_sums[q].total()).astype(bf16)
+    for copy in piece_copies:
+        copy.wait()
+    osend, orecv = r["owner_sems"]
+    owner_copies = []
+    for d in range(1, 8):
+        owner = lax.rem(ctx.me + d, 8)
+        copy = remote(
+            pieces.at[owner], r["gain_slots"].at[d], osend.at[d], orecv.at[d], {"ctx": owner}
+        )
+        copy.start()
+        owner_copies.append(copy)
+    pre.join()
+    out.join()
+    down_b.total()
+    gate.first()
+    pre.swap()
+    out.swap()
+    gate.join()
+    down_a.total()
+    up.total()
+    total = pieces[ctx.me]
+    for d, copy in enumerate(owner_copies, start=1):
+        copy.wait_recv()
+        total = total + r["gain_slots"][d]
+    r["gains"][...] = total
+    pre.total()
+    out.total()
+    gate.total()
+    for one in sums + sums_in + last_sums + list(inner_sums.values()):
+        one.finish()
+    for copy in owner_copies:
+        copy.wait_send()
+    lines.finish()
+    lines_in.finish()
+
+
+def end_of_backward(operands, hbm_names, out_shapes, collective_id, chunks=4):
+    n = 8
+    rows, width = operands["mid"].shape
+    vmem = pl.BlockSpec(memory_space=pltpu.VMEM)
+    kinds = {name: pl.BlockSpec(memory_space=pl.ANY) for name in hbm_names}
+    kinds["bounds"] = pl.BlockSpec(memory_space=pltpu.SMEM)
+    shapes = {name: operands[name].shape for name in hbm_names}
+    shapes |= dict(pre=(8 * width, 384), out=(width, 8 * width))
+    outs = dict(out_shapes)
+    for name in CTX_NAMES:
+        outs["own_" + name] = (owned(shapes[name], CTX_DIMS[name]), bf16)
+    reduce = reduce_scratch(chunks, rows // chunks, width)
+    slots = [pltpu.VMEM((8, 8, 128), f32)] + seven()
+    scratch = dict(
+        whole=[pltpu.VMEM((rows, 8 * width), bf16)],
+        part_in=[pltpu.VMEM((rows, 8 * width), bf16)],
+        pre=[pltpu.VMEM(shapes["pre"], bf16)],
+        out=[pltpu.VMEM(shapes["out"], bf16)],
+        grad_mid=[pltpu.VMEM((rows, width), f32)],
+        agsrc=[pltpu.VMEM((rows, width), bf16)],
+        grad_mix=[pltpu.VMEM((rows, width), bf16)],
+        grad_pre=[pltpu.VMEM((rows, 384), bf16)],
+        line_in=[pltpu.VMEM((8, 128), f32)],
+        piece=[pltpu.VMEM((16, width), f32)],
+        pieces=[pltpu.VMEM((8, 16, width), f32)],
+        gain_slots=[pltpu.VMEM((8, 16, width), f32)],
+        piece_sems=seven(),
+        owner_sems=seven(),
+        slots=slots,
+        slots_in=slots,
+        reduce=reduce,
+        reduce_in=reduce,
+        last_reduce=reduce,
+        gather=gather_scratch(chunks),
+        attention=attention_back_scratch(operands["kv"].shape),
+    )
+    for name in CTX_NAMES:
+        scratch["sum_" + name] = ctx_scratch(shapes[name], CTX_DIMS[name], CTX_MODES[name])
+    names = (
+        [(name, 1) for name in operands] + [(name, 1) for name in outs]
+        + [(name, len(specs)) for name, specs in scratch.items()]
+    )
+    results = pl.pallas_call(
+        functools.partial(end_kernel, n, chunks, names),
+        out_shape=tuple(jax.ShapeDtypeStruct(*one) for one in outs.values()),
+        in_specs=[kinds.get(name, vmem) for name in operands],
+        out_specs=(vmem,) * len(outs),
+        scratch_shapes=[spec for specs in scratch.values() for spec in specs],
+        compiler_params=pltpu.CompilerParams(
+            collective_id=collective_id, has_side_effects=True, vmem_limit_bytes=60 * MiB
+        ),
+        name="end_of_backward",
+    )(*operands.values())
+    return dict(zip(outs, results))
 
 
 def per_device(
@@ -1213,7 +1323,7 @@
             [dots.reshape(rows // 128, 128), jnp.zeros((8 - rows // 128, 128), f32)]
         )
 
-    def backward(grad, grad_share, saved, last):
+    def behind_mlp(grad, saved):
         gate, up = saved["gate"], saved["up"]
         grad_inner = times_transposed(grad, w_d)
         sigmoid = jax.nn.sigmoid(gate)
@@ -1221,17 +1331,13 @@
         grad_up = (grad_inner * gate * sigmoid).astype(bf16)
         part = times_transposed(grad_gate, w_g) + times_transposed(grad_up, w_u)
         line = line_of(part, saved["mid_whole"], saved["mid_factor"], gain_mlp)
-        arrays = []
-        if last:
-            half = saved["inner"].shape[1] // 2
-            arrays = [
-                contract_rows(saved["inner"][:, :half], grad).astype(bf16),
-                contract_rows(saved["inner"][:, half:], grad).astype(bf16),
-            ]
-        grad_mid, piece, grad_attn, *down = backward_sum(
-            "mid", part.astype(bf16), line, grad_share, saved["mid"], saved["mid_factor"],
-            own_gain_mlp, arrays, (1, 1)[: len(arrays)], ("x", "y")[: len(arrays)], [],
-            8 if last else 3,
+        return part.astype(bf16), line, grad_gate, grad_up
+
+    def backward(grad, grad_share, saved):
+        part, line, _, _ = behind_mlp(grad, saved)
+        grad_mid, grad_attn = backward_sum(
+            "mid", part, line, grad_share, saved["mid"], saved["mid_factor"], own_gain_mlp,
+            [], 3,
         )
         grad_mix = times_transposed(grad_attn, w_o).astype(bf16)
         grad_query, grad_kv = attention_back(
@@ -1241,13 +1347,9 @@
         grad_pre = jnp.concatenate([grad_query, grad_kv], axis=1)
         part = times_transposed(grad_pre, w_qkv)
         line = line_of(part, saved["whole"], saved["factor"], gain_attn)
-        operands = (
+        return (
             part.astype(bf16), line, grad_mid, saved["share"].astype(f32), saved["factor"],
             own_gain_attn,
-        )
-        return operands, dict(
-            grad_gate=grad_gate, grad_up=grad_up, grad_attn=grad_attn, grad_pre=grad_pre,
-            piece=piece, down=down,
         )
 
     whole_cot = lax.all_gather(cot, "wt", axis=1, tiled=True)
@@ -1256,21 +1358,32 @@
     part, saved = forward(whole, share, 1)
     last_part = part
 
-    operands, _ = backward(whole_cot, cot, saved, False)
+    operands = backward(whole_cot, cot, saved)
     section = lax.axis_index("section")
-    grad_share, grad = backward_sum("pass", *operands, [], (), (), [cot], 9)
-    operands, kept = backward(grad, grad_share, saved, True)
-    arrays = [
-        contract_rows(saved["mlp_in"], kept["grad_up"]).astype(bf16),
-        contract_rows(saved["attn_in"], kept["grad_pre"]).astype(bf16),
-        contract_rows(saved["mix"], kept["grad_attn"]).astype(bf16),
-        contract_rows(saved["mlp_in"], kept["grad_gate"]).astype(bf16),
-    ]
-    first_grad, result, gains, up, pre, out, gate = backward_sum(
-        "last", *operands, arrays, (0, 0, 1, 0), ("x", "x", "y", "y"),
-        [kept["piece"], last_part, saved["mid"]], 10,
+    grad_share, grad = backward_sum("pass", *operands, [cot], 9)
+    part, line, grad_gate, grad_up = behind_mlp(grad, saved)
+    half = saved["inner"].shape[1] // 2
+    operands = dict(
+        bounds=doc_bounds, part=part, line=line, above=grad_share, mid=saved["mid"],
+        mid_factor=saved["mid_factor"], mid_gain=own_gain_mlp, flat=saved["q_pre"],
+        cosine=cosine, sine=sine, kv_cosine=kv_cosine, kv_sine=kv_sine, kv=saved["kv"],
+        logs=saved["logs"], mixed=saved["mixed"], w_out=w_o, w_qkv=w_qkv,
+        attn_in=saved["attn_in"], mix=saved["mix"], hidden=saved["share"].astype(f32),
+        factor=saved["factor"], gain=own_gain_attn, last_part=last_part,
+        last_mid=saved["mid"],
+        down_a=contract_rows(saved["inner"][:, :half], grad).astype(bf16),
+        up=contract_rows(saved["mlp_in"], grad_up).astype(bf16),
+        down_b=contract_rows(saved["inner"][:, half:], grad).astype(bf16),
+        gate=contract_rows(saved["mlp_in"], grad_gate).astype(bf16),
     )
-    down = jnp.concatenate(kept["down"], axis=0)
+    out_shapes = dict(
+        first_grad=((rows, share_width), bf16), result=((rows, share_width), bf16),
+        gains=((16, share_width), f32),
+    )
+    ends = end_of_backward(operands, ("down_a", "up", "down_b", "gate"), out_shapes, 10)
+    first_grad, result, gains = ends["first_grad"], ends["result"], ends["gains"]
+    up, gate, pre, out = (ends["own_" + name].astype(f32) for name in ("up", "gate", "pre", "out"))
+    down = jnp.concatenate([ends["own_down_a"], ends["own_down_b"]], axis=0).astype(f32)
     boundary = jnp.where(section == 0, first_grad, result)
     return (
         boundary.reshape(1, micro_count, block_rows, share_width),

time: 441 us -> 449 us (1.018)
  other arithmetic: 4.85 us -> 11.8 us
  Pallas kernels: 332 us -> 338 us
    pallas_call x4 -> x3, Pallas kernels: 185 us -> 199 us  [the longest x1 147 us: end_of_backward(): pl.pallas_call(functools.partial(end_kernel, n, chunks, names), out_shape...]
    pallas_call x2 -> x1, Pallas kernels: 28.1 us -> 18.1 us  [attention_back(): pl.pallas_call(functools.partial(attention_back_kernel, n), out_shape=(ja...]
    dot_general x10 -> x8, matrix products: 23 us -> 21.2 us  [times_transposed(): lax.dot_general(left, right, (((1,), (1,)), ((), ())), preferred_element_...]
    dot_general x6 -> x4, matrix products: 18.5 us -> 17.3 us  [contract_rows(): lax.dot_general(left, right, (((0,), (0,)), ((), ())), preferred_element_...]
    unnamed x122 -> x118, local copies, waits for them, and re-layouts: 9.27 us -> 9.41 us
  transfers between devices with their start and end apart: 1 -> 1, of which waited for: 0 -> 0; matrix products, arithmetic and copies ran while one was open for 6% -> 7% of each run, Pallas kernels for 27% -> 27%
where the time goes in v4:
time: 449 us; the launch traced here: 443 us
  Pallas kernels  338 us (75%)
  matrix products  62 us (14%)
  between operations  15.2 us (3%)
  local copies, waits for them, and re-layouts  15.1 us (3%)
  other arithmetic  11.8 us (3%)
    pallas_call x1, Pallas kernels, end_of_backward(): pl.pallas_call(functools.partial(end_kernel, n, chunks, names), out_shape...  147 us
    pallas_call x2, Pallas kernels, backward_sum(): pl.pallas_call(functools.partial(backward_kernel, mode, chunks), out_shap...  52.3 us
    pallas_call x2, Pallas kernels, forward_mid(): pl.pallas_call(functools.partial(forward_mid_kernel, chunks), out_shape=(...  45.7 us
    pallas_call x2, Pallas kernels, attention(): pl.pallas_call(functools.partial(attention_kernel, n), out_shape=(jax.Sha...  30.4 us
    pallas_call x1, Pallas kernels, forward_pass(): pl.pallas_call(functools.partial(forward_pass_kernel, chunks), out_shape=...  28.5 us
    dot_general x8, matrix products, times_transposed(): lax.dot_general(left, right, (((1,), (1,)), ((), ())), preferred_element_...  21.2 us
    pallas_call x1, Pallas kernels, attention_back(): pl.pallas_call(functools.partial(attention_back_kernel, n), out_shape=(ja...  18.1 us
    dot_general x4, matrix products, contract_rows(): lax.dot_general(left, right, (((0,), (0,)), ((), ())), preferred_element_...  17.3 us
  transfers between devices with their start and end apart: 1, of which 0 were waited for; matrix products, arithmetic and copies ran while one was open for 7% of the time, Pallas kernels for 27%

profile of v4, /device:TPU:1, one launch (start us, length us, event | category | flops | bytes accessed | tf_op | source)
XLA Modules:
  0.0 442.7 jit_solution(12987508212171366981)
XLA Ops:
  8.0 0.7 convert_element_type.115
  8.7 1.2 copy.34
  9.9 1.2 copy.35
  11.2 16.1 %gather_wt.1 = bf16[384,2048]{1,0:T(8,128)(2,1)S(1)} custom-call(bf16[384,256]{1,0:T(8,128)(2,1)S(1)} %bitcast.99), custom_call_target="tpu_custom_call" | custom-call | tf_op jit(solution)/shard_map/gather_wt/pallas_call | solution.py:179
  28.0 1.1 copy-done.25
  29.2 1.0 fusion.54
  30.6 0.8 multiply_sine_fusion
  31.8 14.6 %attention.2 = (bf16[384,256]{1,0:T(8,128)(2,1)S(1)}, f32[2,1,768]{2,1,0:T(1,128)}, f32[2,128,768]{2,1,0:T(8,128)}, bf16[8,2,192,128]{3,2,1,0:T(8,128)(2,1)}) custom-call(s32[2,2]{1,0:T(2,128)S(1)} %copy-done.19, f32[384,256]{1,0:T(8,128)S(1)} %slice.52.flat, f32[384,128]{1,0:T(8,128)S(1)} %slice.53.kv_pre, ...), custom_call_target="tpu_custom_call" | custom-call | tf_op jit(solution)/shard_map/attention/pallas_call | solution.py:879
  46.4 2.0 convolution_convert_fusion.5.part
  48.4 22.8 %sum_mid_gather.2 = (f32[384,256]{1,0:T(8,128)S(1)}, bf16[384,2048]{1,0:T(8,128)(2,1)S(1)}) custom-call(bf16[384,2048]{1,0:T(8,128)(2,1)S(1)} %convolution_convert_fusion.5.part, bf16[384,256]{1,0:T(8,128)(2,1)S(1)} %bitcast.100), custom_call_target="tpu_custom_call" | custom-call | tf_op jit(solution)/shard_map/sum_mid_gather/pallas_call | solution.py:310
  71.6 1.8 fusion.22
  73.8 2.0 multiply_convert_fusion.5
  76.0 1.8 fusion.48.part
  77.8 28.5 %sum_pass_gather.1 = (bf16[384,256]{1,0:T(8,128)(2,1)S(1)}, bf16[384,2048]{1,0:T(8,128)(2,1)S(1)}) custom-call(bf16[384,2048]{1,0:T(8,128)(2,1)S(1)} %fusion.48.part, f32[384,256]{1,0:T(8,128)S(1)} %get-tuple-element.38.mid, bf16[384,256]{1,0:T(8,128)(2,1)S(1)} %bitcast.101), custom_call_target="tpu_custom_call" | custom-call | tf_op jit(solution)/shard_map/sum_pass_gather/pallas_call | solution.py:368
  106.8 0.8 rsqrt.33.factor.refs_20_
  108.0 1.0 copy-done.26
  109.0 1.0 fusion.82
  110.3 15.8 %attention.3 = (bf16[384,256]{1,0:T(8,128)(2,1)S(1)}, f32[2,1,768]{2,1,0:T(1,128)S(1)}, f32[2,128,768]{2,1,0:T(8,128)S(1)}, bf16[8,2,192,128]{3,2,1,0:T(8,128)(2,1)S(1)}) custom-call(s32[2,2]{1,0:T(2,128)S(1)} %copy-done.19, f32[384,256]{1,0:T(8,128)S(1)} %slice.54.flat.refs_1_.refs_7_, f32[384,128]{1,0:T(8,128)S(1)} %slice.55.kv_pre, ...), custom_call_target="tpu_custom_call" | custom-call | tf_op jit(solution)/shard_map/attention/pallas_call | solution.py:879
  127.2 22.9 %sum_mid_gather.3 = (f32[384,256]{1,0:T(8,128)S(1)}, bf16[384,2048]{1,0:T(8,128)(2,1)}) custom-call(bf16[384,2048]{1,0:T(8,128)(2,1)S(1)} %convolution_convert_fusion.4.part, bf16[384,256]{1,0:T(8,128)(2,1)S(1)} %copy-done.17), custom_call_target="tpu_custom_call" | custom-call | tf_op jit(solution)/shard_map/sum_mid_gather/pallas_call | solution.py:310
  150.2 1.9 fusion.35
  152.7 0.8 rsqrt.32.factor.refs_5_
  153.5 1.3 constant_dynamic-slice_fusion
  154.8 5.8 %fusion.20 = f32[384,1024]{1,0:T(8,128)} fusion(bf16[1,2048,1024]{2,1,0:T(8,128)(2,1)} %param.21, bf16[384,2048]{1,0:T(8,128)(2,1)} %get-tuple-element.45, f32[384]{0:T(512)} %copy-done.44, f32[2048]{0:T(1024)} %bitcast.117), kind=kOutput, calls=%fused_computation.20 | convolution fusion | flops 1613758464 | bytes 7349760 | tf_op jit(solution)/shard_map/dot_general | solution.py:1309
  160.6 4.5 %fusion.12 = f32[384,1024]{1,0:T(8,128)} fusion(bf16[1,2048,1024]{2,1,0:T(8,128)(2,1)S(1)} %copy-done.51, bf16[384,2048]{1,0:T(8,128)(2,1)} %get-tuple-element.45, f32[384]{0:T(512)S(1)} %copy-done.45, f32[2048]{0:T(1024)S(1)} %bitcast.118), kind=kOutput, calls=%fused_computation.12 | convolution fusion | flops 1613758464 | bytes 7349760 | tf_op jit(solution)/shard_map/dot_general | solution.py:1310
  165.1 4.6 %fusion.4 = f32[384,1024]{1,0:T(8,128)S(1)} fusion(bf16[384,2048]{1,0:T(8,128)(2,1)} %all-gather.2.cloned.1.call-done, bf16[1,1024,2048]{2,1,0:T(8,128)(2,1)} %param.23), kind=kOutput, calls=%fused_computation.4 | convolution fusion | flops 1610612736 | bytes 7340032 | tf_op jit(solution)/shard_map/dot_general | solution.py:44
  169.8 1.9 fusion.10
  172.5 4.1 fusion.40
  176.6 23.8 %sum_back_mid.1 = (f32[384,256]{1,0:T(8,128)S(1)}, bf16[384,2048]{1,0:T(8,128)(2,1)S(1)}) custom-call(bf16[384,2048]{1,0:T(8,128)(2,1)S(1)} %get-tuple-element.102.part, f32[8,128]{1,0:T(8,128)S(1)} %concatenate.54.line, bf16[384,256]{1,0:T(8,128)(2,1)S(1)} %bitcast.103, f32[384,256]{1,0:T(8,128)S(1)} %get-tuple-element.46.own.refs_4_.refs_23_, ...), custom_call_target="tpu_custom_call" | custom-call | tf_op jit(solution)/shard_map/sum_back_mid/pallas_call | solution.py:722
  201.8 18.1 %attention_back.1 = (bf16[384,256]{1,0:T(8,128)(2,1)S(1)}, bf16[384,128]{1,0:T(8,128)(2,1)S(1)}) custom-call(s32[2,2]{1,0:T(2,128)S(1)} %copy-done.19, f32[384,256]{1,0:T(8,128)S(1)} %slice.54.flat.refs_1_.refs_7_, f32[384,128]{1,0:T(8,128)S(1)} %get-tuple-element.115.cosine.refs_2_.refs_8_, f32[384,128]{1,0:T(8,128)S(1)} %get-tuple-element.106.sine.refs_3_.refs_9_, ...), custom_call_target="tpu_custom_call" | custom-call | tf_op jit(solution)/shard_map/attention_back/pallas_call | solution.py:1006
  220.0 1.2 fusion.34
  221.2 28.5 %sum_back_pass.1 = (bf16[384,256]{1,0:T(8,128)(2,1)S(1)}, bf16[384,2048]{1,0:T(8,128)(2,1)S(1)}) custom-call(bf16[384,2048]{1,0:T(8,128)(2,1)S(1)} %get-tuple-element.100.part, f32[8,128]{1,0:T(8,128)S(1)} %concatenate.56.line, f32[384,256]{1,0:T(8,128)S(1)} %get-tuple-element.50.above, f32[384,256]{1,0:T(8,128)S(1)} %convert_element_type.134.own.refs_19_, ...), custom_call_target="tpu_custom_call" | custom-call | tf_op jit(solution)/shard_map/sum_back_pass/pallas_call | solution.py:722
  249.7 2.4 multiply_convert_fusion
  252.1 3.0 fusion.51.refs_22_
  255.1 2.7 convolution_convert_fusion.2.refs_26_
  257.8 2.6 convolution_convert_fusion.3.refs_24_
  260.4 1.9 fusion.8
  262.3 5.9 %convolution_convert_fusion.1.refs_25_ = bf16[2048,1024]{1,0:T(8,128)(2,1)} fusion(bf16[384,1024]{1,0:T(8,128)(2,1)S(1)} %get-tuple-element.96, bf16[384,2048]{1,0:T(8,128)(2,1)} %get-tuple-element.45, f32[384]{0:T(512)S(1)} %copy-done.46, f32[2048]{0:T(1024)S(1)} %bitcast.120), kind=kOutput, calls=%fused_computation.33 | convolution fusion | flops 1615855616 | bytes 6563328 | tf_op jit(solution)/shard_map/dot_general | solution.py:38
  268.1 6.1 %convolution_convert_fusion.refs_27_ = bf16[2048,1024]{1,0:T(8,128)(2,1)} fusion(bf16[384,1024]{1,0:T(8,128)(2,1)S(1)} %get-tuple-element.95, bf16[384,2048]{1,0:T(8,128)(2,1)} %get-tuple-element.45, f32[384]{0:T(512)S(1)} %copy-done.46, f32[2048]{0:T(1024)S(1)} %bitcast.121), kind=kOutput, calls=%fused_computation.32 | convolution fusion | flops 1615855616 | bytes 6563328 | tf_op jit(solution)/shard_map/dot_general | solution.py:38
  274.3 4.6 %fusion.41 = (f32[384]{0:T(512)S(1)}, bf16[384,2048]{1,0:T(8,128)(2,1)}) fusion(bf16[384,2048]{1,0:T(8,128)(2,1)} %get-tuple-element.45, f32[384]{0:T(512)S(1)} %copy-done.46, f32[2048]{0:T(1024)S(1)} %bitcast.122, f32[384,2048]{1,0:T(8,128)S(1)} %fusion.8, bf16[384,1024]{1,0:T(8,128)(2,1)S(1)} %get-tuple-element.95, bf16[1,2048,1024]{2,1,0:T(8,128)(2,1)S(1)} %copy-done.54), kind=kOutput, calls=%fused_computation.51 | convolution fusion | flops 1616117376 | bytes 11283456 | tf_op jit(solution)/shard_map/dot_general | solution.py:44
  279.5 146.8 %end_of_backward.1 = (bf16[384,256]{1,0:T(8,128)(2,1)}, bf16[384,256]{1,0:T(8,128)(2,1)}, f32[16,256]{1,0:T(8,128)}, bf16[512,256]{1,0:T(8,128)(2,1)}, bf16[256,...) custom-call(s32[2,2]{1,0:T(2,128)} %refs_0_.3, ...), custom_call_target="tpu_custom_call" | custom-call | tf_op jit(solution)/shard_map/end_of_backward/pallas_call | solution.py:1242
  426.3 1.0 convert_element_type.144
  427.4 0.7 slice_bitcast_fusion
  428.2 1.3 fusion.81
  429.5 0.7 bitcast_convert_fusion.2
  430.2 0.7 copy.41
  431.7 1.1 bitcast_convert_fusion.1
  432.8 1.1 bitcast_convert_fusion
  433.9 1.0 maximum_convert_fusion
  (148 shorter events, 10.3 us)
Async XLA Ops:
  7.2 4.0 copy-start.13
  7.2 157.9 %all-gather.2.cloned.1.call-start = ((), (), s32[]{:S(2)}) async-start(), calls=%async_computation | async-start | bytes 1769472 | tf_op jit(solution)/shard_map/all_gather | solution.py:1355
  8.7 98.9 %copy-start.37 = (f32[1,2048]{1,0:T(1,128)}, f32[1,2048]{1,0:T(1,128)S(1)}, u32[]{:S(2)}) copy-start(f32[1,2048]{1,0:T(1,128)S(1)} %convert_element_type.115) | copy-start | bytes 24580
  11.2 16.5 %copy-start.29 = (bf16[1,2048,256]{2,1,0:T(8,128)(2,1)S(1)}, bf16[1,2048,256]{2,1,0:T(8,128)(2,1)}, u32[]{:S(2)}) copy-start(bf16[1,2048,256]{2,1,0:T(8,128)(2,1)} %param.16) | copy-start | bytes 3145732
  30.4 43.0 %copy-start.41 = (f32[1,2048]{1,0:T(1,128)}, f32[1,2048]{1,0:T(1,128)S(1)}, u32[]{:S(2)}) copy-start(f32[1,2048]{1,0:T(1,128)S(1)} %convert_element_type.120) | copy-start | bytes 24580
  31.8 169.3 %copy-start.1 = (f32[384,128]{1,0:T(8,128)}, f32[384,128]{1,0:T(8,128)S(1)}, u32[]{:S(2)}) copy-start(f32[384,128]{1,0:T(8,128)S(1)} %get-tuple-element.105.kv_sine.refs_5_.refs_11_) | copy-start | bytes 589828
  31.8 169.3 %copy-start.2 = (f32[384,128]{1,0:T(8,128)}, f32[384,128]{1,0:T(8,128)S(1)}, u32[]{:S(2)}) copy-start(f32[384,128]{1,0:T(8,128)S(1)} %get-tuple-element.106.sine.refs_3_.refs_9_) | copy-start | bytes 589828
  31.8 169.3 %copy-start.3 = (f32[384,128]{1,0:T(8,128)}, f32[384,128]{1,0:T(8,128)S(1)}, u32[]{:S(2)}) copy-start(f32[384,128]{1,0:T(8,128)S(1)} %get-tuple-element.115.cosine.refs_2_.refs_8_) | copy-start | bytes 589828
  31.8 169.3 %copy-start.4 = (f32[384,128]{1,0:T(8,128)}, f32[384,128]{1,0:T(8,128)S(1)}, u32[]{:S(2)}) copy-start(f32[384,128]{1,0:T(8,128)S(1)} %get-tuple-element.116.kv_cosine.refs_4_.refs_10_) | copy-start | bytes 589828
  46.4 25.2 %copy-start.53 = (bf16[1,2048,1024]{2,1,0:T(8,128)(2,1)S(1)}, bf16[1,2048,1024]{2,1,0:T(8,128)(2,1)}, u32[]{:S(2)}) copy-start(bf16[1,2048,1024]{2,1,0:T(8,128)(2,1)} %param.21) | copy-start | bytes 12582916
  71.6 2.2 copy-start.50
  73.8 2.2 copy-start.48
  106.3 3.9 copy-start.16
  107.6 1.4 copy-start.26
  110.2 91.0 %copy-start = (f32[384,256]{1,0:T(8,128)}, f32[384,256]{1,0:T(8,128)S(1)}, u32[]{:S(2)}) copy-start(f32[384,256]{1,0:T(8,128)S(1)} %slice.54.flat.refs_1_.refs_7_) | copy-start | bytes 1179652
  110.2 15.9 %copy-start.23 = (bf16[1,256,2048]{2,1,0:T(8,128)(2,1)S(1)}, bf16[1,256,2048]{2,1,0:T(8,128)(2,1)}, u32[]{:S(2)}) copy-start(bf16[1,256,2048]{2,1,0:T(8,128)(2,1)} %param.19) | copy-start | bytes 3145732
  110.2 110.9 %copy-start.5 = (f32[384,256]{1,0:T(8,128)}, f32[384,256]{1,0:T(8,128)S(1)}, u32[]{:S(2)}) copy-start(f32[384,256]{1,0:T(8,128)S(1)} %convert_element_type.134.own.refs_19_) | copy-start | bytes 1179652
  126.0 24.1 %copy-start.7 = (f32[2,128,768]{2,1,0:T(8,128)}, f32[2,128,768]{2,1,0:T(8,128)S(1)}, u32[]{:S(2)}) copy-start(f32[2,128,768]{2,1,0:T(8,128)S(1)} %get-tuple-element.42.refs_8_.refs_14_) | copy-start | bytes 2359300
  126.0 24.1 %copy-start.9 = (bf16[8,2,192,128]{3,2,1,0:T(8,128)(2,1)}, bf16[8,2,192,128]{3,2,1,0:T(8,128)(2,1)S(1)}, u32[]{:S(2)}) copy-start(bf16[8,2,192,128]{3,2,1,0:T(8,128)(2,1)S(1)} %get-tuple-element.40.refs_6_.refs_12_) | copy-start | bytes 2359300
  126.1 24.1 %copy-start.15 = (bf16[384,256]{1,0:T(8,128)(2,1)}, bf16[384,256]{1,0:T(8,128)(2,1)S(1)}, u32[]{:S(2)}) copy-start(bf16[384,256]{1,0:T(8,128)(2,1)S(1)} %get-tuple-element.43.refs_18_) | copy-start | bytes 589828
  126.1 75.1 %copy-start.20 = (f32[2,1,768]{2,1,0:T(1,128)}, f32[2,1,768]{2,1,0:T(1,128)S(1)}, u32[]{:S(2)}) copy-start(f32[2,1,768]{2,1,0:T(1,128)S(1)} %get-tuple-element.41.refs_7_.refs_13_) | copy-start | bytes 18436
  150.2 26.4 %copy-start.6 = (f32[384,256]{1,0:T(8,128)}, f32[384,256]{1,0:T(8,128)S(1)}, u32[]{:S(2)}) copy-start(f32[384,256]{1,0:T(8,128)S(1)} %get-tuple-element.46.own.refs_4_.refs_23_) | copy-start | bytes 1179652
  154.8 66.4 %copy-start.21 = (f32[1,256]{1,0:T(1,128)}, f32[1,256]{1,0:T(1,128)S(1)}, u32[]{:S(2)}) copy-start(f32[1,256]{1,0:T(1,128)S(1)} %get-tuple-element.122.gain.refs_21_) | copy-start | bytes 3076
  154.8 5.8 %copy-start.42 = (f32[1,2048]{1,0:T(1,128)S(1)}, f32[1,2048]{1,0:T(1,128)}, u32[]{:S(2)}) copy-start(f32[1,2048]{1,0:T(1,128)} %copy-done.41) | copy-start | bytes 24580
  154.8 5.8 %copy-start.45 = (f32[384]{0:T(512)S(1)}, f32[384]{0:T(512)}, u32[]{:S(2)}) copy-start(f32[384]{0:T(512)} %copy-done.44) | copy-start | bytes 4612
  154.8 5.8 %copy-start.51 = (bf16[1,2048,1024]{2,1,0:T(8,128)(2,1)S(1)}, bf16[1,2048,1024]{2,1,0:T(8,128)(2,1)}, u32[]{:S(2)}) copy-start(bf16[1,2048,1024]{2,1,0:T(8,128)(2,1)} %param.22) | copy-start | bytes 12582916
  165.1 4.6 %copy-start.52 = (bf16[1,2048,1024]{2,1,0:T(8,128)(2,1)S(1)}, bf16[1,2048,1024]{2,1,0:T(8,128)(2,1)}, u32[]{:S(2)}) copy-start(bf16[1,2048,1024]{2,1,0:T(8,128)(2,1)} %param.22) | copy-start | bytes 12582916
  165.1 4.7 %copy-start.55 = (f32[384,1024]{1,0:T(8,128)S(1)}, f32[384,1024]{1,0:T(8,128)}, u32[]{:S(2)}) copy-start(f32[384,1024]{1,0:T(8,128)} %fusion.20) | copy-start | bytes 4718596
  169.7 1.9 copy-start.43
  169.7 1.9 copy-start.46
  169.8 2.2 copy-start.54
  169.8 2.7 copy-start.56
  172.4 4.1 copy-start.12
  172.4 4.1 copy-start.14
  172.5 4.2 copy-start.22
  176.5 23.9 %copy-start.24 = (bf16[1,256,2048]{2,1,0:T(8,128)(2,1)S(1)}, bf16[1,256,2048]{2,1,0:T(8,128)(2,1)}, u32[]{:S(2)}) copy-start(bf16[1,256,2048]{2,1,0:T(8,128)(2,1)} %param.19) | copy-start | bytes 3145732
  201.1 18.9 %copy-start.27 = (bf16[2048,384]{1,0:T(8,128)(2,1)S(1)}, bf16[2048,384]{1,0:T(8,128)(2,1)}, u32[]{:S(2)}) copy-start(bf16[2048,384]{1,0:T(8,128)(2,1)} %copy-done.25) | copy-start | bytes 4718596
  201.1 18.9 %copy-start.38 = (f32[1,2048]{1,0:T(1,128)S(1)}, f32[1,2048]{1,0:T(1,128)}, u32[]{:S(2)}) copy-start(f32[1,2048]{1,0:T(1,128)} %copy-done.37) | copy-start | bytes 24580
  201.1 18.9 %copy-start.40 = (f32[384]{0:T(512)S(1)}, f32[384]{0:T(512)}, u32[]{:S(2)}) copy-start(f32[384]{0:T(512)} %copy-done.39) | copy-start | bytes 4612
  220.0 29.7 %copy-start.49 = (bf16[1,1024,2048]{2,1,0:T(8,128)(2,1)S(1)}, bf16[1,1024,2048]{2,1,0:T(8,128)(2,1)}, u32[]{:S(2)}) copy-start(bf16[1,1024,2048]{2,1,0:T(8,128)(2,1)} %param.23) | copy-start | bytes 12582916
  249.7 2.5 copy-start.18
  426.3 3.2 copy-start.36
  426.3 5.3 %copy-start.31 = (bf16[256,1024]{1,0:T(8,128)(2,1)S(1)}, bf16[256,1024]{1,0:T(8,128)(2,1)}, u32[]{:S(2)}) copy-start(bf16[256,1024]{1,0:T(8,128)(2,1)} %get-tuple-element.58) | copy-start | bytes 1572868
  428.1 4.7 %copy-start.30 = (bf16[256,1024]{1,0:T(8,128)(2,1)S(1)}, bf16[256,1024]{1,0:T(8,128)(2,1)}, u32[]{:S(2)}) copy-start(bf16[256,1024]{1,0:T(8,128)(2,1)} %get-tuple-element.59) | copy-start | bytes 1572868
  431.7 2.2 copy-start.32
  431.7 2.2 copy-start.33
  432.8 2.1 copy-start.34
  432.8 2.1 copy-start.35
  (10 other events, 11.4 us)
Sparse Core Ops, SparseCore 0:
  9.7 28.9 all-gather.1

commit v5 on v4

--- a/solution.py
+++ b/solution.py
@@ -1,4 +1,5 @@
 import functools
+from types import SimpleNamespace
 
 import jax
 import jax.numpy as jnp
@@ -183,7 +184,7 @@
         out_specs=pl.BlockSpec(memory_space=pl.ANY),
         scratch_shapes=gather_scratch(chunks),
         compiler_params=pltpu.CompilerParams(
-            collective_id=collective_id, has_side_effects=True, vmem_limit_bytes=32 * MiB
+            collective_id=collective_id, has_side_effects=True, vmem_limit_bytes=4 * MiB
         ),
         name="gather_wt",
     )(x)
@@ -322,7 +323,7 @@
         + reduce_scratch(chunks, rows // chunks, width)
         + gather_scratch(chunks),
         compiler_params=pltpu.CompilerParams(
-            collective_id=collective_id, has_side_effects=True, vmem_limit_bytes=32 * MiB
+            collective_id=collective_id, has_side_effects=True, vmem_limit_bytes=10 * MiB
         ),
         name="sum_mid_gather",
     )(part, skip)
@@ -385,7 +386,7 @@
         + reduce_scratch(chunks, rows // chunks, width)
         + gather_scratch(chunks),
         compiler_params=pltpu.CompilerParams(
-            collective_id=collective_id, has_side_effects=True, vmem_limit_bytes=32 * MiB
+            collective_id=collective_id, has_side_effects=True, vmem_limit_bytes=10 * MiB
         ),
         name="sum_pass_gather",
     )(part, mid, begin)
@@ -729,7 +730,7 @@
         out_specs=(vmem, hbm),
         scratch_shapes=scratch,
         compiler_params=pltpu.CompilerParams(
-            collective_id=collective_id, has_side_effects=True, vmem_limit_bytes=32 * MiB
+            collective_id=collective_id, has_side_effects=True, vmem_limit_bytes=12 * MiB
         ),
         name="sum_back_" + mode,
     )(*operands)
@@ -894,7 +895,7 @@
             pltpu.SemaphoreType.DMA((n,)),
         ],
         compiler_params=pltpu.CompilerParams(
-            collective_id=collective_id, has_side_effects=True, vmem_limit_bytes=40 * MiB
+            collective_id=collective_id, has_side_effects=True, vmem_limit_bytes=20 * MiB
         ),
         name="attention",
     )(bounds, flat, kv_pre, cosine, sine, kv_cosine, kv_sine)
@@ -1013,7 +1014,7 @@
         out_specs=(vmem, vmem),
         scratch_shapes=attention_back_scratch(kv.shape),
         compiler_params=pltpu.CompilerParams(
-            collective_id=collective_id, has_side_effects=True, vmem_limit_bytes=40 * MiB
+            collective_id=collective_id, has_side_effects=True, vmem_limit_bytes=24 * MiB
         ),
         name="attention_back",
     )(bounds, flat, cosine, sine, kv_cosine, kv_sine, kv, logs, mixed, grad)
@@ -1031,57 +1032,74 @@
         )
 
 
-CTX_NAMES = ("down_a", "up", "down_b", "gate", "pre", "out")
 CTX_DIMS = dict(down_a=1, up=0, down_b=1, gate=0, pre=0, out=1)
 CTX_MODES = dict(down_a="x", up="x", down_b="y", gate="y", pre="local", out="local")
 
 
-def end_kernel(n, chunks, names, *refs):
-    r, at = {}, 0
-    for name, count in names:
-        r[name] = refs[at] if count == 1 else refs[at : at + count]
-        at += count
-    place, ctx = WtPlace(r["mid"].shape[1]), CtxPlace()
-    greet([{"wt": peer} for peer in everyone(place)] + ctx.all())
-    width = r["mid"].shape[1]
-    all_rows = r["mid"].shape[0]
-    rows = all_rows // chunks
-    depth = 8 * width
-    spans = [pl.ds(q * rows, rows) for q in range(chunks)]
-    blocks = [pl.ds(width * c, width) for c in range(8)]
-    inner_sums = {
-        name: (YFirst if CTX_MODES[name] == "y" else XFirst)(
-            ctx, r[name], CTX_DIMS[name], r["own_" + name], r["sum_" + name]
-        )
-        for name in CTX_NAMES
-    }
-    down_a, up, down_b, gate, pre, out = (inner_sums[name] for name in CTX_NAMES)
-
-    sums = [Reduce(place, r["part"], r["reduce"], q, spans[q]) for q in range(chunks)]
-    gathers = [Gather(place, r["whole"], r["gather"], q, spans[q]) for q in range(chunks)]
-    lines = Lines(place, r["line"], *r["slots"])
+class Call:
+    def __init__(self, chunks, names, ctx_names, refs):
+        given, at = {}, 0
+        for name, count in names:
+            given[name] = refs[at] if count == 1 else refs[at : at + count]
+            at += count
+        self.r = SimpleNamespace(**given)
+        self.place, self.ctx = WtPlace(given["gain"].shape[1]), CtxPlace()
+        greet([{"wt": peer} for peer in everyone(self.place)] + self.ctx.all())
+        self.width = self.place.width
+        self.all_rows = given["factor"].shape[0]
+        self.rows = self.all_rows // chunks
+        self.spans = [pl.ds(q * self.rows, self.rows) for q in range(chunks)]
+        self.blocks = [pl.ds(self.width * c, self.width) for c in range(8)]
+        self.beside = [
+            (YFirst if CTX_MODES[name] == "y" else XFirst)(
+                self.ctx, given[name], CTX_DIMS[name], given["own_" + name],
+                given["sum_" + name],
+            )
+            for name in ctx_names
+        ]
+
+    def sums(self, part, bufs):
+        return [Reduce(self.place, part, bufs, q, span) for q, span in enumerate(self.spans)]
+
+    def behind_norm(self, sums, lines, above, own, use):
+        r = self.r
+        mean = column(lines.total(), self.all_rows // 128) * (1.0 / (8 * self.width))
+        terms = jnp.zeros((1, self.width), f32)
+        for q, span in enumerate(self.spans):
+            grad, term = norm_back(
+                sums[q].total(), above[span, :], own[span, :], r.factor[span, :], r.gain[...],
+                mean[q * self.rows : (q + 1) * self.rows],
+            )
+            terms = terms + term
+            use(q, span, grad)
+        return jnp.broadcast_to(terms, (8, self.width))
+
+
+def middle_kernel(n, chunks, names, ctx_names, *refs):
+    call = Call(chunks, names, ctx_names, refs)
+    r, place, ctx = call.r, call.place, call.ctx
+    down_a, down_b = call.beside
+    sums = call.sums(r.part, r.reduce)
+    gathers = [
+        Gather(place, r.whole, r.gather, q, span) for q, span in enumerate(call.spans)
+    ]
+    lines = Lines(place, r.line, *r.slots)
     lines.start()
     for one in sums:
         one.start()
-    for one in (down_a, up, down_b, gate):
+    for one in call.beside:
         one.start()
     for one in sums:
         one.pass_on()
     for one in sums:
         one.pass_more()
-    mean = column(lines.total(), all_rows // 128) * (1.0 / depth)
-    terms = jnp.zeros((1, width), f32)
-    for q in range(chunks):
-        span = spans[q]
-        grad, term = norm_back(
-            sums[q].total(), r["above"][span, :], r["mid"][span, :], r["mid_factor"][span, :],
-            r["mid_gain"][...], mean[q * rows : (q + 1) * rows],
-        )
-        terms = terms + term
-        r["grad_mid"][span, :] = grad
-        r["agsrc"][span, :] = grad.astype(bf16)
-        gathers[q].start(r["agsrc"].at[span])
-    r["piece"][8:16, :] = jnp.broadcast_to(terms, (8, width))
+
+    def use(q, span, grad):
+        r.grad_mid[span, :] = grad
+        r.agsrc[span, :] = grad.astype(bf16)
+        gathers[q].start(r.agsrc.at[span])
+
+    r.piece[...] = call.behind_norm(sums, lines, r.above, r.mid, use)
     for one in gathers:
         one.forward()
     for one in gathers:
@@ -1089,63 +1107,65 @@
     down_a.join()
     for one in gathers:
         one.finish()
-    last_sums = [
-        Reduce(place, r["last_part"], r["last_reduce"], q, spans[q]) for q in range(chunks)
-    ]
+    r.grad_mix[...] = times_transposed(r.whole[...], r.w_out[...]).astype(bf16)
+    down_b.first()
+    attention_back_steps(
+        n, ctx.me, lambda: None, r.bounds, r.flat, r.cosine, r.sine, r.kv_cosine, r.kv_sine,
+        r.kv, r.logs, r.mixed, r.grad_mix, r.grad_pre.at[:, pl.ds(0, 256)],
+        r.grad_pre.at[:, pl.ds(256, 128)], *r.attention
+    )
+    down_b.join()
+    down_a.swap()
+    down_b.total()
+    down_a.total()
+    for one in sums + call.beside:
+        one.finish()
+    lines.finish()
+
+
+def last_kernel(n, chunks, names, ctx_names, *refs):
+    call = Call(chunks, names, ctx_names, refs)
+    r, place, ctx = call.r, call.place, call.ctx
+    up, gate, pre, out = call.beside
+    grad_pre = r.grad_pre
+    up.start()
+    gate.start()
+    dots = jnp.zeros((call.all_rows, 1), f32)
+    for block in call.blocks:
+        partial_sum = times_transposed(grad_pre[...], r.w_qkv[block, :])
+        dots = dots + jnp.sum(
+            partial_sum * r.attn_in[:, block].astype(f32), axis=1, keepdims=True
+        )
+        r.part[:, block] = partial_sum.astype(bf16)
+    as_line(dots, r.line)
+    lines = Lines(place, r.line, *r.slots)
+    lines.start()
+    sums = call.sums(r.part, r.reduce)
+    last_sums = call.sums(r.last_part, r.last_reduce)
+    for one in sums:
+        one.start()
+    for one in sums:
+        one.pass_on()
+    for block in call.blocks:
+        r.pre[block, :] = contract_rows(r.attn_in[:, block], grad_pre[...]).astype(bf16)
+    pre.start()
+    for one in sums:
+        one.pass_more()
     for one in last_sums:
         one.start()
-    r["grad_mix"][...] = times_transposed(r["whole"][...], r["w_out"][...]).astype(bf16)
+    for block in call.blocks:
+        r.out[:, block] = contract_rows(r.mix[...], r.whole[:, block]).astype(bf16)
+    out.start()
     for one in last_sums:
         one.pass_on()
-    down_b.first()
-
-    grad_pre = r["grad_pre"]
-    attention_back_steps(
-        n, ctx.me, lambda: None, r["bounds"], r["flat"], r["cosine"], r["sine"],
-        r["kv_cosine"], r["kv_sine"], r["kv"], r["logs"], r["mixed"], r["grad_mix"],
-        grad_pre.at[:, pl.ds(0, 256)], grad_pre.at[:, pl.ds(256, 128)], *r["attention"]
-    )
-    up.join()
-    for one in last_sums:
-        one.pass_more()
-
-    dots = jnp.zeros((all_rows, 1), f32)
-    for block in blocks:
-        partial_sum = times_transposed(grad_pre[...], r["w_qkv"][block, :])
-        dots = dots + jnp.sum(
-            partial_sum * r["attn_in"][:, block].astype(f32), axis=1, keepdims=True
-        )
-        r["part_in"][:, block] = partial_sum.astype(bf16)
-    as_line(dots, r["line_in"])
-    lines_in = Lines(place, r["line_in"], *r["slots_in"])
-    lines_in.start()
-    sums_in = [Reduce(place, r["part_in"], r["reduce_in"], q, spans[q]) for q in range(chunks)]
-    for one in sums_in:
-        one.start()
-    for one in sums_in:
-        one.pass_on()
-    down_b.join()
-    for block in blocks:
-        r["pre"][block, :] = contract_rows(r["attn_in"][:, block], grad_pre[...]).astype(bf16)
-    pre.start()
-    for one in sums_in:
-        one.pass_more()
-    for block in blocks:
-        r["out"][:, block] = contract_rows(r["mix"][...], r["whole"][:, block]).astype(bf16)
-    out.start()
-    mean = column(lines_in.total(), all_rows // 128) * (1.0 / depth)
-    terms = jnp.zeros((1, width), f32)
-    for q in range(chunks):
-        span = spans[q]
-        grad, term = norm_back(
-            sums_in[q].total(), r["grad_mid"][span, :], r["hidden"][span, :],
-            r["factor"][span, :], r["gain"][...], mean[q * rows : (q + 1) * rows],
-        )
-        terms = terms + term
-        r["first_grad"][span, :] = grad.astype(bf16)
-    r["piece"][0:8, :] = jnp.broadcast_to(terms, (8, width))
-    piece, pieces = r["piece"], r["pieces"]
-    gsend, grecv = r["piece_sems"]
+
+    def use(q, span, grad):
+        r.first_grad[span, :] = grad.astype(bf16)
+
+    r.both_pieces[0:8, :] = call.behind_norm(sums, lines, r.grad_mid, r.hidden, use)
+    r.both_pieces[8:16, :] = r.piece[...]
+    piece, pieces = r.both_pieces, r.pieces
+    gsend, grecv = r.piece_sems
     piece_copies = [
         remote(
             piece, pieces.at[place.me], gsend.at[d], grecv.at[d],
@@ -1155,102 +1175,126 @@
     ]
     for copy in piece_copies:
         copy.start()
+    for one in last_sums:
+        one.pass_more()
     pieces[place.me] = piece[...]
-    down_a.swap()
-    up.swap()
-    for q in range(chunks):
-        span = spans[q]
-        r["result"][span, :] = (r["last_mid"][span, :] + last_sums[q].total()).astype(bf16)
     for copy in piece_copies:
         copy.wait()
-    osend, orecv = r["owner_sems"]
+    osend, orecv = r.owner_sems
     owner_copies = []
     for d in range(1, 8):
         owner = lax.rem(ctx.me + d, 8)
         copy = remote(
-            pieces.at[owner], r["gain_slots"].at[d], osend.at[d], orecv.at[d], {"ctx": owner}
+            pieces.at[owner], r.gain_slots.at[d], osend.at[d], orecv.at[d], {"ctx": owner}
         )
         copy.start()
         owner_copies.append(copy)
+    up.join()
     pre.join()
     out.join()
-    down_b.total()
+    for q, span in enumerate(call.spans):
+        r.result[span, :] = (r.last_mid[span, :] + last_sums[q].total()).astype(bf16)
+    total = pieces[ctx.me]
+    for d, copy in enumerate(owner_copies, start=1):
+        copy.wait_recv()
+        total = total + r.gain_slots[d]
+    r.gains[...] = total
+    up.swap()
     gate.first()
     pre.swap()
     out.swap()
     gate.join()
-    down_a.total()
     up.total()
-    total = pieces[ctx.me]
-    for d, copy in enumerate(owner_copies, start=1):
-        copy.wait_recv()
-        total = total + r["gain_slots"][d]
-    r["gains"][...] = total
     pre.total()
     out.total()
     gate.total()
-    for one in sums + sums_in + last_sums + list(inner_sums.values()):
+    for one in sums + last_sums + call.beside:
         one.finish()
     for copy in owner_copies:
         copy.wait_send()
     lines.finish()
-    lines_in.finish()
-
-
-def end_of_backward(operands, hbm_names, out_shapes, collective_id, chunks=4):
-    n = 8
-    rows, width = operands["mid"].shape
+
+
+def call_with_ctx(
+    kernel, operands, outs, scratch, ctx_shapes, hbm_names, collective_id, vmem_mib, name,
+    chunks=4
+):
     vmem = pl.BlockSpec(memory_space=pltpu.VMEM)
-    kinds = {name: pl.BlockSpec(memory_space=pl.ANY) for name in hbm_names}
+    kinds = {one: pl.BlockSpec(memory_space=pl.ANY) for one in hbm_names}
     kinds["bounds"] = pl.BlockSpec(memory_space=pltpu.SMEM)
-    shapes = {name: operands[name].shape for name in hbm_names}
-    shapes |= dict(pre=(8 * width, 384), out=(width, 8 * width))
-    outs = dict(out_shapes)
-    for name in CTX_NAMES:
-        outs["own_" + name] = (owned(shapes[name], CTX_DIMS[name]), bf16)
-    reduce = reduce_scratch(chunks, rows // chunks, width)
-    slots = [pltpu.VMEM((8, 8, 128), f32)] + seven()
-    scratch = dict(
-        whole=[pltpu.VMEM((rows, 8 * width), bf16)],
-        part_in=[pltpu.VMEM((rows, 8 * width), bf16)],
-        pre=[pltpu.VMEM(shapes["pre"], bf16)],
-        out=[pltpu.VMEM(shapes["out"], bf16)],
-        grad_mid=[pltpu.VMEM((rows, width), f32)],
-        agsrc=[pltpu.VMEM((rows, width), bf16)],
-        grad_mix=[pltpu.VMEM((rows, width), bf16)],
-        grad_pre=[pltpu.VMEM((rows, 384), bf16)],
-        line_in=[pltpu.VMEM((8, 128), f32)],
-        piece=[pltpu.VMEM((16, width), f32)],
-        pieces=[pltpu.VMEM((8, 16, width), f32)],
-        gain_slots=[pltpu.VMEM((8, 16, width), f32)],
-        piece_sems=seven(),
-        owner_sems=seven(),
-        slots=slots,
-        slots_in=slots,
-        reduce=reduce,
-        reduce_in=reduce,
-        last_reduce=reduce,
-        gather=gather_scratch(chunks),
-        attention=attention_back_scratch(operands["kv"].shape),
-    )
-    for name in CTX_NAMES:
-        scratch["sum_" + name] = ctx_scratch(shapes[name], CTX_DIMS[name], CTX_MODES[name])
+    outs, scratch = dict(outs), dict(scratch)
+    for one, shape in ctx_shapes.items():
+        outs["own_" + one] = (owned(shape, CTX_DIMS[one]), bf16)
+        scratch["sum_" + one] = ctx_scratch(shape, CTX_DIMS[one], CTX_MODES[one])
     names = (
-        [(name, 1) for name in operands] + [(name, 1) for name in outs]
-        + [(name, len(specs)) for name, specs in scratch.items()]
+        [(one, 1) for one in operands] + [(one, 1) for one in outs]
+        + [(one, len(specs)) for one, specs in scratch.items()]
     )
     results = pl.pallas_call(
-        functools.partial(end_kernel, n, chunks, names),
+        functools.partial(kernel, 8, chunks, names, tuple(ctx_shapes)),
         out_shape=tuple(jax.ShapeDtypeStruct(*one) for one in outs.values()),
-        in_specs=[kinds.get(name, vmem) for name in operands],
+        in_specs=[kinds.get(one, vmem) for one in operands],
         out_specs=(vmem,) * len(outs),
         scratch_shapes=[spec for specs in scratch.values() for spec in specs],
         compiler_params=pltpu.CompilerParams(
-            collective_id=collective_id, has_side_effects=True, vmem_limit_bytes=60 * MiB
-        ),
-        name="end_of_backward",
+            collective_id=collective_id, has_side_effects=True,
+            vmem_limit_bytes=vmem_mib * MiB,
+        ),
+        name=name,
     )(*operands.values())
-    return dict(zip(outs, results))
+    return SimpleNamespace(**dict(zip(outs, results)))
+
+
+def middle_of_backward(operands, collective_id, chunks=4):
+    rows, width = operands["mid"].shape
+    shape = operands["down_a"].shape
+    return call_with_ctx(
+        middle_kernel, operands,
+        dict(
+            grad_mid=((rows, width), f32), piece=((8, width), f32),
+            whole=((rows, 8 * width), bf16), grad_pre=((rows, 384), bf16),
+        ),
+        dict(
+            agsrc=[pltpu.VMEM((rows, width), bf16)],
+            grad_mix=[pltpu.VMEM((rows, width), bf16)],
+            slots=[pltpu.VMEM((8, 8, 128), f32)] + seven(),
+            reduce=reduce_scratch(chunks, rows // chunks, width),
+            gather=gather_scratch(chunks),
+            attention=attention_back_scratch(operands["kv"].shape),
+        ),
+        dict(down_a=shape, down_b=shape), ("down_a", "down_b"), collective_id, 30,
+        "middle_of_backward", chunks,
+    )
+
+
+def end_of_backward(operands, collective_id, chunks=4):
+    rows, width = operands["grad_mid"].shape
+    wide = operands["up"].shape
+    pre, out = (8 * width, 384), (width, 8 * width)
+    reduce = reduce_scratch(chunks, rows // chunks, width)
+    return call_with_ctx(
+        last_kernel, operands,
+        dict(
+            first_grad=((rows, width), bf16), result=((rows, width), bf16),
+            gains=((16, width), f32),
+        ),
+        dict(
+            part=[pltpu.VMEM((rows, 8 * width), bf16)],
+            pre=[pltpu.VMEM(pre, bf16)],
+            out=[pltpu.VMEM(out, bf16)],
+            line=[pltpu.VMEM((8, 128), f32)],
+            both_pieces=[pltpu.VMEM((16, width), f32)],
+            pieces=[pltpu.VMEM((8, 16, width), f32)],
+            gain_slots=[pltpu.VMEM((8, 16, width), f32)],
+            piece_sems=seven(),
+            owner_sems=seven(),
+            slots=[pltpu.VMEM((8, 8, 128), f32)] + seven(),
+            reduce=reduce,
+            last_reduce=reduce,
+        ),
+        dict(up=wide, gate=wide, pre=pre, out=out), ("up", "gate"), collective_id, 48,
+        "end_of_backward", chunks,
+    )
 
 
 def per_device(
@@ -1310,7 +1354,7 @@
         up = jnp.dot(mlp_in, w_u, preferred_element_type=f32)
         inner = lax.optimization_barrier((jax.nn.silu(gate) * up).astype(bf16))
         part = jnp.dot(inner, w_d, preferred_element_type=f32).astype(bf16)
-        saved = dict(
+        saved = SimpleNamespace(
             whole=whole, share=share, factor=factor, attn_in=attn_in, q_pre=q_pre, kv=kv,
             mix=mix, logs=logs, mixed=mixed, mid=mid, mid_whole=mid_whole,
             mid_factor=mid_factor, mlp_in=mlp_in, gate=gate, up=up, inner=inner,
@@ -1324,37 +1368,37 @@
         )
 
     def behind_mlp(grad, saved):
-        gate, up = saved["gate"], saved["up"]
+        gate, up = saved.gate, saved.up
         grad_inner = times_transposed(grad, w_d)
         sigmoid = jax.nn.sigmoid(gate)
         grad_gate = (grad_inner * up * sigmoid * (1.0 + gate * (1.0 - sigmoid))).astype(bf16)
         grad_up = (grad_inner * gate * sigmoid).astype(bf16)
         part = times_transposed(grad_gate, w_g) + times_transposed(grad_up, w_u)
-        line = line_of(part, saved["mid_whole"], saved["mid_factor"], gain_mlp)
+        line = line_of(part, saved.mid_whole, saved.mid_factor, gain_mlp)
         return part.astype(bf16), line, grad_gate, grad_up
 
     def backward(grad, grad_share, saved):
         part, line, _, _ = behind_mlp(grad, saved)
         grad_mid, grad_attn = backward_sum(
-            "mid", part, line, grad_share, saved["mid"], saved["mid_factor"], own_gain_mlp,
+            "mid", part, line, grad_share, saved.mid, saved.mid_factor, own_gain_mlp,
             [], 3,
         )
         grad_mix = times_transposed(grad_attn, w_o).astype(bf16)
         grad_query, grad_kv = attention_back(
-            doc_bounds, saved["q_pre"], cosine, sine, kv_cosine, kv_sine, saved["kv"],
-            saved["logs"], saved["mixed"], grad_mix, 4,
+            doc_bounds, saved.q_pre, cosine, sine, kv_cosine, kv_sine, saved.kv,
+            saved.logs, saved.mixed, grad_mix, 4,
         )
         grad_pre = jnp.concatenate([grad_query, grad_kv], axis=1)
         part = times_transposed(grad_pre, w_qkv)
-        line = line_of(part, saved["whole"], saved["factor"], gain_attn)
+        line = line_of(part, saved.whole, saved.factor, gain_attn)
         return (
-            part.astype(bf16), line, grad_mid, saved["share"].astype(f32), saved["factor"],
+            part.astype(bf16), line, grad_mid, saved.share.astype(f32), saved.factor,
             own_gain_attn,
         )
 
     whole_cot = lax.all_gather(cot, "wt", axis=1, tiled=True)
     part, saved = forward(wt_gather(begin, 6), begin, 0)
-    share, whole = forward_pass(part, saved["mid"], begin, 7)
+    share, whole = forward_pass(part, saved.mid, begin, 7)
     part, saved = forward(whole, share, 1)
     last_part = part
 
@@ -1362,28 +1406,34 @@
     section = lax.axis_index("section")
     grad_share, grad = backward_sum("pass", *operands, [cot], 9)
     part, line, grad_gate, grad_up = behind_mlp(grad, saved)
-    half = saved["inner"].shape[1] // 2
-    operands = dict(
-        bounds=doc_bounds, part=part, line=line, above=grad_share, mid=saved["mid"],
-        mid_factor=saved["mid_factor"], mid_gain=own_gain_mlp, flat=saved["q_pre"],
-        cosine=cosine, sine=sine, kv_cosine=kv_cosine, kv_sine=kv_sine, kv=saved["kv"],
-        logs=saved["logs"], mixed=saved["mixed"], w_out=w_o, w_qkv=w_qkv,
-        attn_in=saved["attn_in"], mix=saved["mix"], hidden=saved["share"].astype(f32),
-        factor=saved["factor"], gain=own_gain_attn, last_part=last_part,
-        last_mid=saved["mid"],
-        down_a=contract_rows(saved["inner"][:, :half], grad).astype(bf16),
-        up=contract_rows(saved["mlp_in"], grad_up).astype(bf16),
-        down_b=contract_rows(saved["inner"][:, half:], grad).astype(bf16),
-        gate=contract_rows(saved["mlp_in"], grad_gate).astype(bf16),
-    )
-    out_shapes = dict(
-        first_grad=((rows, share_width), bf16), result=((rows, share_width), bf16),
-        gains=((16, share_width), f32),
-    )
-    ends = end_of_backward(operands, ("down_a", "up", "down_b", "gate"), out_shapes, 10)
-    first_grad, result, gains = ends["first_grad"], ends["result"], ends["gains"]
-    up, gate, pre, out = (ends["own_" + name].astype(f32) for name in ("up", "gate", "pre", "out"))
-    down = jnp.concatenate([ends["own_down_a"], ends["own_down_b"]], axis=0).astype(f32)
+    half = saved.inner.shape[1] // 2
+    mids = middle_of_backward(
+        dict(
+            bounds=doc_bounds, part=part, line=line, above=grad_share, mid=saved.mid,
+            factor=saved.mid_factor, gain=own_gain_mlp, flat=saved.q_pre, cosine=cosine,
+            sine=sine, kv_cosine=kv_cosine, kv_sine=kv_sine, kv=saved.kv, logs=saved.logs,
+            mixed=saved.mixed, w_out=w_o,
+            down_a=contract_rows(saved.inner[:, :half], grad).astype(bf16),
+            down_b=contract_rows(saved.inner[:, half:], grad).astype(bf16),
+        ),
+        8,
+    )
+    ends = end_of_backward(
+        dict(
+            grad_pre=mids.grad_pre, w_qkv=w_qkv, attn_in=saved.attn_in, mix=saved.mix,
+            whole=mids.whole, grad_mid=mids.grad_mid, hidden=saved.share.astype(f32),
+            factor=saved.factor, gain=own_gain_attn, piece=mids.piece, last_part=last_part,
+            last_mid=saved.mid,
+            up=contract_rows(saved.mlp_in, grad_up).astype(bf16),
+            gate=contract_rows(saved.mlp_in, grad_gate).astype(bf16),
+        ),
+        10,
+    )
+    first_grad, result, gains = ends.first_grad, ends.result, ends.gains
+    up, gate, pre, out = (
+        one.astype(f32) for one in (ends.own_up, ends.own_gate, ends.own_pre, ends.own_out)
+    )
+    down = jnp.concatenate([mids.own_down_a, mids.own_down_b], axis=0).astype(f32)
     boundary = jnp.where(section == 0, first_grad, result)
     return (
         boundary.reshape(1, micro_count, block_rows, share_width),

time: 449 us -> 426 us (0.949)
  matrix products: 62 us -> 49.9 us
  Pallas kernels: 338 us -> 327 us
    pallas_call x1 -> x2, Pallas kernels: 147 us -> 138 us  [call_with_ctx(): pl.pallas_call(functools.partial(kernel, 8, chunks, names, tuple(ctx_shap...]
    dot_general x4, matrix products: 17.3 us -> 11.8 us  [contract_rows(): lax.dot_general(left, right, (((0,), (0,)), ((), ())), preferred_element_...]
    unnamed x118 -> x92, local copies, waits for them, and re-layouts: 9.41 us -> 14.3 us
  transfers between devices with their start and end apart: 1 -> 1, of which waited for: 0 -> 0; matrix products, arithmetic and copies ran while one was open for 7% -> 7% of each run, Pallas kernels for 27% -> 28%
where the time goes in v5:
time: 426 us; the launch traced here: 421 us
  Pallas kernels  327 us (77%)
  matrix products  49.9 us (12%)
  local copies, waits for them, and re-layouts  18.1 us (4%)
  between operations  15.1 us (4%)
  other arithmetic  10.3 us (2%)
    pallas_call x2, Pallas kernels, call_with_ctx(): pl.pallas_call(functools.partial(kernel, 8, chunks, names, tuple(ctx_shap...  138 us
    pallas_call x2, Pallas kernels, backward_sum(): pl.pallas_call(functools.partial(backward_kernel, mode, chunks), out_shap...  52.3 us
    pallas_call x2, Pallas kernels, forward_mid(): pl.pallas_call(functools.partial(forward_mid_kernel, chunks), out_shape=(...  44.5 us
    pallas_call x2, Pallas kernels, attention(): pl.pallas_call(functools.partial(attention_kernel, n), out_shape=(jax.Sha...  30.4 us
    pallas_call x1, Pallas kernels, forward_pass(): pl.pallas_call(functools.partial(forward_pass_kernel, chunks), out_shape=...  28.2 us
    pallas_call x1, Pallas kernels, attention_back(): pl.pallas_call(functools.partial(attention_back_kernel, n), out_shape=(ja...  17.9 us
    dot_general x8, matrix products, times_transposed(): lax.dot_general(left, right, (((1,), (1,)), ((), ())), preferred_element_...  17.2 us
    pallas_call x1, Pallas kernels, wt_gather(): pl.pallas_call(functools.partial(gather_kernel, chunks), out_shape=jax.Sh...  16.1 us
  transfers between devices with their start and end apart: 1, of which 0 were waited for; matrix products, arithmetic and copies ran while one was open for 7% of the time, Pallas kernels for 28%

profile of v5, /device:TPU:1, one launch (start us, length us, event | category | flops | bytes accessed | tf_op | source)
XLA Modules:
  0.0 421.3 jit_solution(8712508754021618415)
XLA Ops:
  7.9 1.2 copy.35
  9.2 1.2 copy.34
  10.5 16.1 %gather_wt.1 = bf16[384,2048]{1,0:T(8,128)(2,1)S(1)} custom-call(bf16[384,256]{1,0:T(8,128)(2,1)S(1)} %bitcast.100), custom_call_target="tpu_custom_call" | custom-call | tf_op jit(solution)/shard_map/gather_wt/pallas_call | solution.py:180
  27.3 1.0 fusion.54
  29.0 0.8 multiply_sine_fusion
  30.1 14.6 %attention.2 = (bf16[384,256]{1,0:T(8,128)(2,1)S(1)}, f32[2,1,768]{2,1,0:T(1,128)}, f32[2,128,768]{2,1,0:T(8,128)}, bf16[8,2,192,128]{3,2,1,0:T(8,128)(2,1)}) custom-call(s32[2,2]{1,0:T(2,128)S(1)} %copy-done.30, f32[384,256]{1,0:T(8,128)S(1)} %slice.52.flat, f32[384,128]{1,0:T(8,128)S(1)} %slice.53.kv_pre, ...), custom_call_target="tpu_custom_call" | custom-call | tf_op jit(solution)/shard_map/attention/pallas_call | solution.py:880
  45.4 22.4 %sum_mid_gather.2 = (f32[384,256]{1,0:T(8,128)S(1)}, bf16[384,2048]{1,0:T(8,128)(2,1)S(1)}) custom-call(bf16[384,2048]{1,0:T(8,128)(2,1)S(1)} %convolution_convert_fusion.5.part, bf16[384,256]{1,0:T(8,128)(2,1)S(1)} %bitcast.101), custom_call_target="tpu_custom_call" | custom-call | tf_op jit(solution)/shard_map/sum_mid_gather/pallas_call | solution.py:311
  68.2 1.9 fusion.22
  70.3 2.0 multiply_convert_fusion.5
  72.5 1.8 fusion.48.part
  74.4 28.2 %sum_pass_gather.1 = (bf16[384,256]{1,0:T(8,128)(2,1)S(1)}, bf16[384,2048]{1,0:T(8,128)(2,1)S(1)}) custom-call(bf16[384,2048]{1,0:T(8,128)(2,1)S(1)} %fusion.48.part, f32[384,256]{1,0:T(8,128)S(1)} %get-tuple-element.42.mid, bf16[384,256]{1,0:T(8,128)(2,1)S(1)} %bitcast.102), custom_call_target="tpu_custom_call" | custom-call | tf_op jit(solution)/shard_map/sum_pass_gather/pallas_call | solution.py:369
  103.4 1.0 copy-done.2
  104.4 1.0 fusion.82
  106.3 0.8 rsqrt.33.factor.refs_7_
  107.1 1.7 convert_element_type.134.own.refs_6_
  108.8 0.9 copy-done.5
  109.7 0.9 copy-done.8
  110.7 0.9 copy-done.27
  111.6 15.8 %attention.3 = (bf16[384,256]{1,0:T(8,128)(2,1)S(1)}, f32[2,1,768]{2,1,0:T(1,128)S(1)}, f32[2,128,768]{2,1,0:T(8,128)S(1)}, bf16[8,2,192,128]{3,2,1,0:T(8,128)(2,1)S(1)}) custom-call(s32[2,2]{1,0:T(2,128)S(1)} %copy-done.30, f32[384,256]{1,0:T(8,128)S(1)} %slice.54.flat.refs_1_.refs_7_, f32[384,128]{1,0:T(8,128)S(1)} %copy-done.27, ...), custom_call_target="tpu_custom_call" | custom-call | tf_op jit(solution)/shard_map/attention/pallas_call | solution.py:880
  128.7 22.2 %sum_mid_gather.3 = (f32[384,256]{1,0:T(8,128)S(1)}, bf16[384,2048]{1,0:T(8,128)(2,1)S(1)}) custom-call(bf16[384,2048]{1,0:T(8,128)(2,1)S(1)} %convolution_convert_fusion.4.part, bf16[384,256]{1,0:T(8,128)(2,1)S(1)} %copy-done.29), custom_call_target="tpu_custom_call" | custom-call | tf_op jit(solution)/shard_map/sum_mid_gather/pallas_call | solution.py:311
  151.0 0.7 copy-done.10
  151.7 1.1 copy-done.21
  153.2 0.8 rsqrt.32.factor.refs_5_
  154.0 5.8 %fusion.12 = f32[384,1024]{1,0:T(8,128)} fusion(bf16[1,2048,1024]{2,1,0:T(8,128)(2,1)} %param.22, bf16[384,2048]{1,0:T(8,128)(2,1)} %copy-done.21, f32[384]{0:T(512)S(1)} %add_rsqrt_fusion, f32[2048]{0:T(1024)S(1)} %bitcast.117), kind=kOutput, calls=%fused_computation.12 | convolution fusion | flops 1613758464 | bytes 7349760 | tf_op jit(solution)/shard_map/dot_general | solution.py:1354
  159.9 3.0 fusion.20
  162.9 4.6 %fusion.4 = f32[384,1024]{1,0:T(8,128)S(1)} fusion(bf16[384,2048]{1,0:T(8,128)(2,1)} %all-gather.2.cloned.1.call-done, bf16[1,1024,2048]{2,1,0:T(8,128)(2,1)} %param.23), kind=kOutput, calls=%fused_computation.4 | convolution fusion | flops 1610612736 | bytes 7340032 | tf_op jit(solution)/shard_map/dot_general | solution.py:45
  167.6 1.9 fusion.10
  169.5 0.8 copy-done.41
  170.7 2.7 fusion.40
  173.4 23.8 %sum_back_mid.1 = (f32[384,256]{1,0:T(8,128)S(1)}, bf16[384,2048]{1,0:T(8,128)(2,1)S(1)}) custom-call(bf16[384,2048]{1,0:T(8,128)(2,1)S(1)} %get-tuple-element.110.part, f32[8,128]{1,0:T(8,128)S(1)} %concatenate.54.line, bf16[384,256]{1,0:T(8,128)(2,1)S(1)} %bitcast.104, f32[384,256]{1,0:T(8,128)S(1)} %copy-done.11, f32[384,1]{1,0:T(8,128)S(1)} %copy-done.20, ...), custom_call_target="tpu_custom_call" | custom-call | tf_op jit(solution)/shard_map/sum_back_mid/pallas_call | solution.py:723
  198.8 17.9 %attention_back.1 = (bf16[384,256]{1,0:T(8,128)(2,1)S(1)}, bf16[384,128]{1,0:T(8,128)(2,1)S(1)}) custom-call(s32[2,2]{1,0:T(2,128)S(1)} %copy-done.30, f32[384,256]{1,0:T(8,128)S(1)} %slice.54.flat.refs_1_.refs_7_, f32[384,128]{1,0:T(8,128)S(1)} %copy-done.6, f32[384,128]{1,0:T(8,128)S(1)} %get-tuple-element.114.sine.refs_3_.refs_9_, ...), custom_call_target="tpu_custom_call" | custom-call | tf_op jit(solution)/shard_map/attention_back/pallas_call | solution.py:1007
  216.8 1.2 fusion.34
  218.0 28.4 %sum_back_pass.1 = (bf16[384,256]{1,0:T(8,128)(2,1)S(1)}, bf16[384,2048]{1,0:T(8,128)(2,1)S(1)}) custom-call(bf16[384,2048]{1,0:T(8,128)(2,1)S(1)} %get-tuple-element.108.part, f32[8,128]{1,0:T(8,128)S(1)} %concatenate.56.line, f32[384,256]{1,0:T(8,128)S(1)} %get-tuple-element.54.above, f32[384,256]{1,0:T(8,128)S(1)} %copy-done.12, f32[384,1]{1,0:T(8,128)S(1)} %copy-done.17, ...), custom_call_target="tpu_custom_call" | custom-call | tf_op jit(solution)/shard_map/sum_back_pass/pallas_call | solution.py:723
  246.4 2.4 multiply_convert_fusion
  248.8 1.3 convolution_convert_fusion.3.refs_16_
  250.1 1.3 convolution_convert_fusion.2.refs_17_
  251.4 3.1 fusion.51.refs_10_
  254.5 1.8 fusion.8
  256.3 4.5 %convolution_convert_fusion.1.refs_12_ = bf16[2048,1024]{1,0:T(8,128)(2,1)} fusion(bf16[384,1024]{1,0:T(8,128)(2,1)S(1)} %get-tuple-element.104, bf16[384,2048]{1,0:T(8,128)(2,1)S(1)} %copy-done.23, f32[384]{0:T(512)S(1)} %add_rsqrt_fusion, f32[2048]{0:T(1024)S(1)} %bitcast.120), kind=kOutput, calls=%fused_computation.33 | convolution fusion | flops 1615855616 | bytes 6563328 | tf_op jit(solution)/shard_map/dot_general | solution.py:39
  260.8 4.7 %convolution_convert_fusion.refs_13_ = bf16[2048,1024]{1,0:T(8,128)(2,1)} fusion(bf16[384,1024]{1,0:T(8,128)(2,1)S(1)} %get-tuple-element.103, bf16[384,2048]{1,0:T(8,128)(2,1)S(1)} %copy-done.23, f32[384]{0:T(512)S(1)} %add_rsqrt_fusion, f32[2048]{0:T(1024)S(1)} %bitcast.121), kind=kOutput, calls=%fused_computation.32 | convolution fusion | flops 1615855616 | bytes 6563328 | tf_op jit(solution)/shard_map/dot_general | solution.py:39
  265.5 2.1 fusion.41
  267.6 52.3 %middle_of_backward.1 = (f32[384,256]{1,0:T(8,128)S(1)}, f32[8,256]{1,0:T(8,128)S(1)}, bf16[384,2048]{1,0:T(8,128)(2,1)S(1)}, bf16[384,384]{1,0:T(8,128)(2,1)S(1...) custom-call(s32[2,2]{1,0:T(2,128)S(1)} %copy-done.30, bf16[384,2048]{1,0:T(8,128)(2,1)S(1)} %get-tuple-element.106.refs_1_, ...), custom_call_target="tpu_custom_call" | custom-call | tf_op jit(solution)/shard_map/middle_of_backward/pallas_call | solution.py:1233
  320.0 1.1 copy-done.24
  321.1 85.6 %end_of_backward.1 = (bf16[384,256]{1,0:T(8,128)(2,1)S(1)}, bf16[384,256]{1,0:T(8,128)(2,1)S(1)}, f32[16,256]{1,0:T(8,128)S(1)}, bf16[256,1024]{1,0:T(8,128)(2,1...) custom-call(bf16[384,384]{1,0:T(8,128)(2,1)S(1)} %get-tuple-element.57.refs_0_, ...), custom_call_target="tpu_custom_call" | custom-call | tf_op jit(solution)/shard_map/end_of_backward/pallas_call | solution.py:1233
  406.7 0.7 slice_bitcast_fusion
  410.3 1.1 bitcast_convert_fusion.1
  411.4 1.1 bitcast_convert_fusion
  412.4 1.0 maximum_convert_fusion
  (123 shorter events, 12.8 us)
Async XLA Ops:
  7.2 3.3 copy-start.18
  7.2 155.7 %all-gather.2.cloned.1.call-start = ((), (), s32[]{:S(2)}) async-start(), calls=%async_computation | async-start | bytes 1769472 | tf_op jit(solution)/shard_map/all_gather | solution.py:1399
  7.9 18.6 %copy-start.33 = (bf16[1,2048]{1,0:T(2,128)(2,1)S(1)}, bf16[1,2048]{1,0:T(2,128)(2,1)}, u32[]{:S(2)}) copy-start(bf16[1,2048]{1,0:T(2,128)(2,1)} %param.15) | copy-start | bytes 12292
  10.4 16.5 %copy-start.32 = (bf16[1,2048,256]{2,1,0:T(8,128)(2,1)S(1)}, bf16[1,2048,256]{2,1,0:T(8,128)(2,1)}, u32[]{:S(2)}) copy-start(bf16[1,2048,256]{2,1,0:T(8,128)(2,1)} %param.16) | copy-start | bytes 3145732
  27.3 1.2 copy-start.1
  27.3 1.3 copy-start.30
  28.6 16.2 %copy-start = (bf16[1,256,2048]{2,1,0:T(8,128)(2,1)S(1)}, bf16[1,256,2048]{2,1,0:T(8,128)(2,1)}, u32[]{:S(2)}) copy-start(bf16[1,256,2048]{2,1,0:T(8,128)(2,1)} %param.19) | copy-start | bytes 3145732
  30.1 15.2 %copy-start.4 = (f32[384,128]{1,0:T(8,128)}, f32[384,128]{1,0:T(8,128)S(1)}, u32[]{:S(2)}) copy-start(f32[384,128]{1,0:T(8,128)S(1)} %get-tuple-element.123.cosine.refs_2_.refs_8_) | copy-start | bytes 589828
  30.1 15.2 %copy-start.7 = (f32[384,128]{1,0:T(8,128)}, f32[384,128]{1,0:T(8,128)S(1)}, u32[]{:S(2)}) copy-start(f32[384,128]{1,0:T(8,128)S(1)} %get-tuple-element.124.kv_cosine.refs_4_.refs_10_) | copy-start | bytes 589828
  44.7 23.4 %copy-start.39 = (bf16[1,2048,1024]{2,1,0:T(8,128)(2,1)S(1)}, bf16[1,2048,1024]{2,1,0:T(8,128)(2,1)}, u32[]{:S(2)}) copy-start(bf16[1,2048,1024]{2,1,0:T(8,128)(2,1)} %param.21) | copy-start | bytes 12582916
  45.3 22.4 %copy-start.34 = (bf16[1,2048]{1,0:T(2,128)(2,1)S(1)}, bf16[1,2048]{1,0:T(2,128)(2,1)}, u32[]{:S(2)}) copy-start(bf16[1,2048]{1,0:T(2,128)(2,1)} %param.20) | copy-start | bytes 12292
  68.2 2.2 copy-start.37
  70.3 2.2 copy-start.35
  102.6 0.8 copy-start.28
  103.0 1.4 copy-start.2
  104.4 1.1 copy-start.31
  108.8 0.9 copy-start.5
  109.7 0.9 copy-start.8
  110.7 0.9 copy-start.27
  127.4 23.5 %copy-start.13 = (f32[2,128,768]{2,1,0:T(8,128)}, f32[2,128,768]{2,1,0:T(8,128)S(1)}, u32[]{:S(2)}) copy-start(f32[2,128,768]{2,1,0:T(8,128)S(1)} %get-tuple-element.46.refs_8_.refs_14_) | copy-start | bytes 2359300
  127.5 23.5 %copy-start.15 = (bf16[8,2,192,128]{3,2,1,0:T(8,128)(2,1)}, bf16[8,2,192,128]{3,2,1,0:T(8,128)(2,1)S(1)}, u32[]{:S(2)}) copy-start(bf16[8,2,192,128]{3,2,1,0:T(8,128)(2,1)S(1)} %get-tuple-element.44.refs_6_.refs_12_) | copy-start | bytes 2359300
  127.5 1.3 copy-start.29
  128.1 0.7 copy-start.25
  150.9 0.7 copy-start.10
  151.7 1.1 copy-start.21
  154.0 5.9 %copy-start.22 = (bf16[384,2048]{1,0:T(8,128)(2,1)S(1)}, bf16[384,2048]{1,0:T(8,128)(2,1)}, u32[]{:S(2)}) copy-start(bf16[384,2048]{1,0:T(8,128)(2,1)} %copy-done.21) | copy-start | bytes 4718596
  154.0 5.9 %copy-start.40 = (bf16[1,2048,1024]{2,1,0:T(8,128)(2,1)S(1)}, bf16[1,2048,1024]{2,1,0:T(8,128)(2,1)}, u32[]{:S(2)}) copy-start(bf16[1,2048,1024]{2,1,0:T(8,128)(2,1)} %param.21) | copy-start | bytes 12582916
  162.9 4.6 %copy-start.38 = (bf16[1,2048,1024]{2,1,0:T(8,128)(2,1)S(1)}, bf16[1,2048,1024]{2,1,0:T(8,128)(2,1)}, u32[]{:S(2)}) copy-start(bf16[1,2048,1024]{2,1,0:T(8,128)(2,1)} %param.22) | copy-start | bytes 12582916
  162.9 4.6 %copy-start.43 = (f32[384,1024]{1,0:T(8,128)S(1)}, f32[384,1024]{1,0:T(8,128)}, u32[]{:S(2)}) copy-start(f32[384,1024]{1,0:T(8,128)} %fusion.20) | copy-start | bytes 4718596
  167.6 1.9 copy-start.23
  167.6 2.7 copy-start.41
  167.6 3.1 copy-start.42
  170.7 2.7 copy-start.11
  170.7 2.7 copy-start.19
  170.7 2.7 copy-start.20
  197.2 0.9 copy-start.6
  197.3 1.0 copy-start.9
  197.3 1.3 copy-start.14
  197.3 1.5 copy-start.16
  197.9 18.8 %copy-start.3 = (bf16[2048,384]{1,0:T(8,128)(2,1)S(1)}, bf16[2048,384]{1,0:T(8,128)(2,1)}, u32[]{:S(2)}) copy-start(bf16[2048,384]{1,0:T(8,128)(2,1)} %copy-done.1) | copy-start | bytes 4718596
  216.7 1.2 copy-start.12
  216.7 1.2 copy-start.17
  216.8 29.7 %copy-start.36 = (bf16[1,1024,2048]{2,1,0:T(8,128)(2,1)S(1)}, bf16[1,1024,2048]{2,1,0:T(8,128)(2,1)}, u32[]{:S(2)}) copy-start(bf16[1,1024,2048]{2,1,0:T(8,128)(2,1)} %param.23) | copy-start | bytes 12582916
  267.6 53.5 %copy-start.26 = (bf16[384,256]{1,0:T(8,128)(2,1)S(1)}, bf16[384,256]{1,0:T(8,128)(2,1)}, u32[]{:S(2)}) copy-start(bf16[384,256]{1,0:T(8,128)(2,1)} %copy-done.25) | copy-start | bytes 589828
  319.9 1.2 copy-start.24
Sparse Core Ops, SparseCore 0:
  9.7 29.0 all-gather.1

commit v6 on v5

--- a/solution.py
+++ b/solution.py
@@ -639,7 +639,7 @@
 
 
 def norm_back(total, above, own, scale, gain, mean):
-    normed = own * scale
+    normed = own.astype(f32) * scale
     grad = above.astype(f32) + scale * (total * gain - normed * mean)
     return grad, jnp.sum(total * normed, axis=0, keepdims=True)
 
@@ -1109,15 +1109,15 @@
         one.finish()
     r.grad_mix[...] = times_transposed(r.whole[...], r.w_out[...]).astype(bf16)
     down_b.first()
+    down_a.swap()
     attention_back_steps(
         n, ctx.me, lambda: None, r.bounds, r.flat, r.cosine, r.sine, r.kv_cosine, r.kv_sine,
         r.kv, r.logs, r.mixed, r.grad_mix, r.grad_pre.at[:, pl.ds(0, 256)],
         r.grad_pre.at[:, pl.ds(256, 128)], *r.attention
     )
     down_b.join()
-    down_a.swap()
+    down_a.total()
     down_b.total()
-    down_a.total()
     for one in sums + call.beside:
         one.finish()
     lines.finish()
@@ -1392,7 +1392,7 @@
         part = times_transposed(grad_pre, w_qkv)
         line = line_of(part, saved.whole, saved.factor, gain_attn)
         return (
-            part.astype(bf16), line, grad_mid, saved.share.astype(f32), saved.factor,
+            part.astype(bf16), line, grad_mid, saved.share, saved.factor,
             own_gain_attn,
         )
 
@@ -1421,7 +1421,7 @@
     ends = end_of_backward(
         dict(
             grad_pre=mids.grad_pre, w_qkv=w_qkv, attn_in=saved.attn_in, mix=saved.mix,
-            whole=mids.whole, grad_mid=mids.grad_mid, hidden=saved.share.astype(f32),
+            whole=mids.whole, grad_mid=mids.grad_mid, hidden=saved.share,
             factor=saved.factor, gain=own_gain_attn, piece=mids.piece, last_part=last_part,
             last_mid=saved.mid,
             up=contract_rows(saved.mlp_in, grad_up).astype(bf16),

time: 426 us -> 424 us (level)
  transfers between devices with their start and end apart: 1 -> 1, of which waited for: 0 -> 0; matrix products, arithmetic and copies ran while one was open for 7% -> 6% of each run, Pallas kernels for 28% -> 28%
where the time goes in v6:
time: 424 us; the launch traced here: 419 us
  Pallas kernels  327 us (77%)
  matrix products  49.9 us (12%)
  local copies, waits for them, and re-layouts  18 us (4%)
  between operations  15.1 us (4%)
  other arithmetic  8.52 us (2%)
    pallas_call x2, Pallas kernels, call_with_ctx(): pl.pallas_call(functools.partial(kernel, 8, chunks, names, tuple(ctx_shap...  137 us
    pallas_call x2, Pallas kernels, backward_sum(): pl.pallas_call(functools.partial(backward_kernel, mode, chunks), out_shap...  52.3 us
    pallas_call x2, Pallas kernels, forward_mid(): pl.pallas_call(functools.partial(forward_mid_kernel, chunks), out_shape=(...  44.5 us
    pallas_call x2, Pallas kernels, attention(): pl.pallas_call(functools.partial(attention_kernel, n), out_shape=(jax.Sha...  30.4 us
    pallas_call x1, Pallas kernels, forward_pass(): pl.pallas_call(functools.partial(forward_pass_kernel, chunks), out_shape=...  28.2 us
    pallas_call x1, Pallas kernels, attention_back(): pl.pallas_call(functools.partial(attention_back_kernel, n), out_shape=(ja...  17.9 us
    dot_general x8, matrix products, times_transposed(): lax.dot_general(left, right, (((1,), (1,)), ((), ())), preferred_element_...  17.4 us
    pallas_call x1, Pallas kernels, wt_gather(): pl.pallas_call(functools.partial(gather_kernel, chunks), out_shape=jax.Sh...  16.1 us
  transfers between devices with their start and end apart: 1, of which 0 were waited for; matrix products, arithmetic and copies ran while one was open for 6% of the time, Pallas kernels for 28%

profile of v6, /device:TPU:1, one launch (start us, length us, event | category | flops | bytes accessed | tf_op | source)
XLA Modules:
  0.0 418.9 jit_solution(13184312534839104233)
XLA Ops:
  7.9 1.2 copy.35
  9.2 1.2 copy.34
  10.5 16.1 %gather_wt.1 = bf16[384,2048]{1,0:T(8,128)(2,1)S(1)} custom-call(bf16[384,256]{1,0:T(8,128)(2,1)S(1)} %bitcast.100), custom_call_target="tpu_custom_call" | custom-call | tf_op jit(solution)/shard_map/gather_wt/pallas_call | solution.py:180
  27.3 1.0 fusion.54
  29.0 0.8 multiply_sine_fusion
  30.1 14.6 %attention.2 = (bf16[384,256]{1,0:T(8,128)(2,1)S(1)}, f32[2,1,768]{2,1,0:T(1,128)}, f32[2,128,768]{2,1,0:T(8,128)}, bf16[8,2,192,128]{3,2,1,0:T(8,128)(2,1)}) custom-call(s32[2,2]{1,0:T(2,128)S(1)} %copy-done.30, f32[384,256]{1,0:T(8,128)S(1)} %slice.52.flat, f32[384,128]{1,0:T(8,128)S(1)} %slice.53.kv_pre, ...), custom_call_target="tpu_custom_call" | custom-call | tf_op jit(solution)/shard_map/attention/pallas_call | solution.py:880
  45.4 22.4 %sum_mid_gather.2 = (f32[384,256]{1,0:T(8,128)S(1)}, bf16[384,2048]{1,0:T(8,128)(2,1)S(1)}) custom-call(bf16[384,2048]{1,0:T(8,128)(2,1)S(1)} %convolution_convert_fusion.5.part, bf16[384,256]{1,0:T(8,128)(2,1)S(1)} %bitcast.101), custom_call_target="tpu_custom_call" | custom-call | tf_op jit(solution)/shard_map/sum_mid_gather/pallas_call | solution.py:311
  68.2 1.9 fusion.22
  70.3 2.0 multiply_convert_fusion.5
  72.5 1.8 fusion.48.part
  74.4 28.2 %sum_pass_gather.1 = (bf16[384,256]{1,0:T(8,128)(2,1)S(1)}, bf16[384,2048]{1,0:T(8,128)(2,1)S(1)}) custom-call(bf16[384,2048]{1,0:T(8,128)(2,1)S(1)} %fusion.48.part, f32[384,256]{1,0:T(8,128)S(1)} %get-tuple-element.42.mid, bf16[384,256]{1,0:T(8,128)(2,1)S(1)} %bitcast.102), custom_call_target="tpu_custom_call" | custom-call | tf_op jit(solution)/shard_map/sum_pass_gather/pallas_call | solution.py:369
  103.4 1.0 copy-done.2
  104.4 1.0 fusion.82
  106.3 0.8 rsqrt.33.factor.refs_7_
  107.1 0.9 copy-done.5
  108.0 0.9 copy-done.8
  108.9 0.9 copy-done.29
  109.8 15.9 %attention.3 = (bf16[384,256]{1,0:T(8,128)(2,1)S(1)}, f32[2,1,768]{2,1,0:T(1,128)S(1)}, f32[2,128,768]{2,1,0:T(8,128)S(1)}, bf16[8,2,192,128]{3,2,1,0:T(8,128)(2,1)S(1)}) custom-call(s32[2,2]{1,0:T(2,128)S(1)} %copy-done.30, f32[384,256]{1,0:T(8,128)S(1)} %slice.54.flat.refs_1_.refs_7_, f32[384,128]{1,0:T(8,128)S(1)} %copy-done.29, ...), custom_call_target="tpu_custom_call" | custom-call | tf_op jit(solution)/shard_map/attention/pallas_call | solution.py:880
  126.9 22.2 %sum_mid_gather.3 = (f32[384,256]{1,0:T(8,128)S(1)}, bf16[384,2048]{1,0:T(8,128)(2,1)S(1)}) custom-call(bf16[384,2048]{1,0:T(8,128)(2,1)S(1)} %convolution_convert_fusion.4.part, bf16[384,256]{1,0:T(8,128)(2,1)S(1)} %copy-done.17), custom_call_target="tpu_custom_call" | custom-call | tf_op jit(solution)/shard_map/sum_mid_gather/pallas_call | solution.py:311
  149.1 0.7 copy-done.10
  149.9 1.1 copy-done.23
  151.4 0.8 rsqrt.32.factor.refs_5_
  152.2 5.8 %fusion.12 = f32[384,1024]{1,0:T(8,128)} fusion(bf16[1,2048,1024]{2,1,0:T(8,128)(2,1)} %param.22, bf16[384,2048]{1,0:T(8,128)(2,1)} %copy-done.23, f32[384]{0:T(512)S(1)} %add_rsqrt_fusion, f32[2048]{0:T(1024)S(1)} %bitcast.117), kind=kOutput, calls=%fused_computation.12 | convolution fusion | flops 1613758464 | bytes 7349760 | tf_op jit(solution)/shard_map/dot_general | solution.py:1354
  158.1 3.0 fusion.20
  161.1 4.6 %fusion.4 = f32[384,1024]{1,0:T(8,128)S(1)} fusion(bf16[384,2048]{1,0:T(8,128)(2,1)} %all-gather.2.cloned.1.call-done, bf16[1,1024,2048]{2,1,0:T(8,128)(2,1)} %param.23), kind=kOutput, calls=%fused_computation.4 | convolution fusion | flops 1610612736 | bytes 7340032 | tf_op jit(solution)/shard_map/dot_general | solution.py:45
  165.8 1.9 fusion.10
  167.7 0.7 copy-done.41
  168.9 2.7 fusion.40
  171.6 23.8 %sum_back_mid.1 = (f32[384,256]{1,0:T(8,128)S(1)}, bf16[384,2048]{1,0:T(8,128)(2,1)S(1)}) custom-call(bf16[384,2048]{1,0:T(8,128)(2,1)S(1)} %get-tuple-element.110.part, f32[8,128]{1,0:T(8,128)S(1)} %concatenate.54.line, bf16[384,256]{1,0:T(8,128)(2,1)S(1)} %bitcast.104, f32[384,256]{1,0:T(8,128)S(1)} %copy-done.11, f32[384,1]{1,0:T(8,128)S(1)} %copy-done.22, ...), custom_call_target="tpu_custom_call" | custom-call | tf_op jit(solution)/shard_map/sum_back_mid/pallas_call | solution.py:723
  197.0 17.9 %attention_back.1 = (bf16[384,256]{1,0:T(8,128)(2,1)S(1)}, bf16[384,128]{1,0:T(8,128)(2,1)S(1)}) custom-call(s32[2,2]{1,0:T(2,128)S(1)} %copy-done.30, f32[384,256]{1,0:T(8,128)S(1)} %slice.54.flat.refs_1_.refs_7_, f32[384,128]{1,0:T(8,128)S(1)} %copy-done.6, f32[384,128]{1,0:T(8,128)S(1)} %get-tuple-element.114.sine.refs_3_.refs_9_, ...), custom_call_target="tpu_custom_call" | custom-call | tf_op jit(solution)/shard_map/attention_back/pallas_call | solution.py:1007
  214.9 1.2 fusion.34
  216.1 28.5 %sum_back_pass.1 = (bf16[384,256]{1,0:T(8,128)(2,1)S(1)}, bf16[384,2048]{1,0:T(8,128)(2,1)S(1)}) custom-call(bf16[384,2048]{1,0:T(8,128)(2,1)S(1)} %get-tuple-element.108.part, f32[8,128]{1,0:T(8,128)S(1)} %concatenate.56.line, f32[384,256]{1,0:T(8,128)S(1)} %get-tuple-element.54.above, bf16[384,256]{1,0:T(8,128)(2,1)S(1)} %copy-done.18, ...), custom_call_target="tpu_custom_call" | custom-call | tf_op jit(solution)/shard_map/sum_back_pass/pallas_call | solution.py:723
  244.6 2.4 multiply_convert_fusion
  247.0 1.3 convolution_convert_fusion.3.refs_16_
  248.3 1.3 convolution_convert_fusion.2.refs_17_
  249.6 3.0 fusion.51.refs_10_
  252.6 1.8 fusion.8
  254.5 4.5 %convolution_convert_fusion.1.refs_12_ = bf16[2048,1024]{1,0:T(8,128)(2,1)} fusion(bf16[384,1024]{1,0:T(8,128)(2,1)S(1)} %get-tuple-element.104, bf16[384,2048]{1,0:T(8,128)(2,1)S(1)} %copy-done.25, f32[384]{0:T(512)S(1)} %add_rsqrt_fusion, f32[2048]{0:T(1024)S(1)} %bitcast.120), kind=kOutput, calls=%fused_computation.33 | convolution fusion | flops 1615855616 | bytes 6563328 | tf_op jit(solution)/shard_map/dot_general | solution.py:39
  259.0 4.7 %convolution_convert_fusion.refs_13_ = bf16[2048,1024]{1,0:T(8,128)(2,1)} fusion(bf16[384,1024]{1,0:T(8,128)(2,1)S(1)} %get-tuple-element.103, bf16[384,2048]{1,0:T(8,128)(2,1)S(1)} %copy-done.25, f32[384]{0:T(512)S(1)} %add_rsqrt_fusion, f32[2048]{0:T(1024)S(1)} %bitcast.121), kind=kOutput, calls=%fused_computation.32 | convolution fusion | flops 1615855616 | bytes 6563328 | tf_op jit(solution)/shard_map/dot_general | solution.py:39
  263.7 2.2 fusion.41
  265.9 49.3 %middle_of_backward.1 = (f32[384,256]{1,0:T(8,128)S(1)}, f32[8,256]{1,0:T(8,128)S(1)}, bf16[384,2048]{1,0:T(8,128)(2,1)S(1)}, bf16[384,384]{1,0:T(8,128)(2,1)S(1...) custom-call(s32[2,2]{1,0:T(2,128)S(1)} %copy-done.30, bf16[384,2048]{1,0:T(8,128)(2,1)S(1)} %get-tuple-element.106.refs_1_, ...), custom_call_target="tpu_custom_call" | custom-call | tf_op jit(solution)/shard_map/middle_of_backward/pallas_call | solution.py:1233
  315.2 1.1 copy-done.26
  316.4 87.9 %end_of_backward.1 = (bf16[384,256]{1,0:T(8,128)(2,1)S(1)}, bf16[384,256]{1,0:T(8,128)(2,1)S(1)}, f32[16,256]{1,0:T(8,128)S(1)}, bf16[256,1024]{1,0:T(8,128)(2,1...) custom-call(bf16[384,384]{1,0:T(8,128)(2,1)S(1)} %get-tuple-element.57.refs_0_, ...), custom_call_target="tpu_custom_call" | custom-call | tf_op jit(solution)/shard_map/end_of_backward/pallas_call | solution.py:1233
  404.3 0.7 slice_bitcast_fusion
  407.1 0.7 bitcast_convert_fusion.2
  407.8 1.1 bitcast_convert_fusion.1
  408.9 1.1 bitcast_convert_fusion
  410.0 1.0 maximum_convert_fusion
  (122 shorter events, 12.0 us)
Async XLA Ops:
  7.2 3.3 copy-start.20
  7.2 153.9 %all-gather.2.cloned.1.call-start = ((), (), s32[]{:S(2)}) async-start(), calls=%async_computation | async-start | bytes 1769472 | tf_op jit(solution)/shard_map/all_gather | solution.py:1399
  7.9 18.6 %copy-start.33 = (bf16[1,2048]{1,0:T(2,128)(2,1)S(1)}, bf16[1,2048]{1,0:T(2,128)(2,1)}, u32[]{:S(2)}) copy-start(bf16[1,2048]{1,0:T(2,128)(2,1)} %param.15) | copy-start | bytes 12292
  10.4 16.5 %copy-start.32 = (bf16[1,2048,256]{2,1,0:T(8,128)(2,1)S(1)}, bf16[1,2048,256]{2,1,0:T(8,128)(2,1)}, u32[]{:S(2)}) copy-start(bf16[1,2048,256]{2,1,0:T(8,128)(2,1)} %param.16) | copy-start | bytes 3145732
  27.3 1.2 copy-start.1
  27.3 1.3 copy-start.30
  28.6 16.2 %copy-start = (bf16[1,256,2048]{2,1,0:T(8,128)(2,1)S(1)}, bf16[1,256,2048]{2,1,0:T(8,128)(2,1)}, u32[]{:S(2)}) copy-start(bf16[1,256,2048]{2,1,0:T(8,128)(2,1)} %param.19) | copy-start | bytes 3145732
  30.1 15.2 %copy-start.4 = (f32[384,128]{1,0:T(8,128)}, f32[384,128]{1,0:T(8,128)S(1)}, u32[]{:S(2)}) copy-start(f32[384,128]{1,0:T(8,128)S(1)} %get-tuple-element.123.cosine.refs_2_.refs_8_) | copy-start | bytes 589828
  30.1 15.2 %copy-start.7 = (f32[384,128]{1,0:T(8,128)}, f32[384,128]{1,0:T(8,128)S(1)}, u32[]{:S(2)}) copy-start(f32[384,128]{1,0:T(8,128)S(1)} %get-tuple-element.124.kv_cosine.refs_4_.refs_10_) | copy-start | bytes 589828
  44.7 23.4 %copy-start.39 = (bf16[1,2048,1024]{2,1,0:T(8,128)(2,1)S(1)}, bf16[1,2048,1024]{2,1,0:T(8,128)(2,1)}, u32[]{:S(2)}) copy-start(bf16[1,2048,1024]{2,1,0:T(8,128)(2,1)} %param.21) | copy-start | bytes 12582916
  45.3 22.4 %copy-start.34 = (bf16[1,2048]{1,0:T(2,128)(2,1)S(1)}, bf16[1,2048]{1,0:T(2,128)(2,1)}, u32[]{:S(2)}) copy-start(bf16[1,2048]{1,0:T(2,128)(2,1)} %param.20) | copy-start | bytes 12292
  68.2 2.2 copy-start.37
  70.3 2.2 copy-start.35
  102.6 0.8 copy-start.16
  103.0 1.4 copy-start.2
  104.4 1.1 copy-start.31
  107.1 0.9 copy-start.5
  108.0 0.9 copy-start.8
  108.9 0.9 copy-start.29
  125.7 23.4 %copy-start.12 = (f32[2,128,768]{2,1,0:T(8,128)}, f32[2,128,768]{2,1,0:T(8,128)S(1)}, u32[]{:S(2)}) copy-start(f32[2,128,768]{2,1,0:T(8,128)S(1)} %get-tuple-element.46.refs_8_.refs_14_) | copy-start | bytes 2359300
  125.7 23.4 %copy-start.14 = (bf16[8,2,192,128]{3,2,1,0:T(8,128)(2,1)}, bf16[8,2,192,128]{3,2,1,0:T(8,128)(2,1)S(1)}, u32[]{:S(2)}) copy-start(bf16[8,2,192,128]{3,2,1,0:T(8,128)(2,1)S(1)} %get-tuple-element.44.refs_6_.refs_12_) | copy-start | bytes 2359300
  125.7 23.4 %copy-start.27 = (bf16[384,256]{1,0:T(8,128)(2,1)}, bf16[384,256]{1,0:T(8,128)(2,1)S(1)}, u32[]{:S(2)}) copy-start(bf16[384,256]{1,0:T(8,128)(2,1)S(1)} %get-tuple-element.47.refs_3_) | copy-start | bytes 589828
  125.7 1.2 copy-start.17
  149.1 0.7 copy-start.10
  149.9 1.1 copy-start.23
  152.2 5.9 %copy-start.24 = (bf16[384,2048]{1,0:T(8,128)(2,1)S(1)}, bf16[384,2048]{1,0:T(8,128)(2,1)}, u32[]{:S(2)}) copy-start(bf16[384,2048]{1,0:T(8,128)(2,1)} %copy-done.23) | copy-start | bytes 4718596
  152.2 5.9 %copy-start.40 = (bf16[1,2048,1024]{2,1,0:T(8,128)(2,1)S(1)}, bf16[1,2048,1024]{2,1,0:T(8,128)(2,1)}, u32[]{:S(2)}) copy-start(bf16[1,2048,1024]{2,1,0:T(8,128)(2,1)} %param.21) | copy-start | bytes 12582916
  161.1 4.6 %copy-start.38 = (bf16[1,2048,1024]{2,1,0:T(8,128)(2,1)S(1)}, bf16[1,2048,1024]{2,1,0:T(8,128)(2,1)}, u32[]{:S(2)}) copy-start(bf16[1,2048,1024]{2,1,0:T(8,128)(2,1)} %param.22) | copy-start | bytes 12582916
  161.1 4.7 %copy-start.43 = (f32[384,1024]{1,0:T(8,128)S(1)}, f32[384,1024]{1,0:T(8,128)}, u32[]{:S(2)}) copy-start(f32[384,1024]{1,0:T(8,128)} %fusion.20) | copy-start | bytes 4718596
  165.8 1.9 copy-start.25
  165.8 2.7 copy-start.41
  165.8 3.1 copy-start.42
  168.9 2.7 copy-start.11
  168.9 2.7 copy-start.21
  168.9 2.7 copy-start.22
  195.4 0.9 copy-start.6
  195.4 1.0 copy-start.9
  195.4 1.3 copy-start.13
  195.4 1.5 copy-start.15
  196.1 18.8 %copy-start.3 = (bf16[2048,384]{1,0:T(8,128)(2,1)S(1)}, bf16[2048,384]{1,0:T(8,128)(2,1)}, u32[]{:S(2)}) copy-start(bf16[2048,384]{1,0:T(8,128)(2,1)} %copy-done.1) | copy-start | bytes 4718596
  214.9 1.2 copy-start.18
  214.9 1.2 copy-start.19
  214.9 29.7 %copy-start.36 = (bf16[1,1024,2048]{2,1,0:T(8,128)(2,1)S(1)}, bf16[1,1024,2048]{2,1,0:T(8,128)(2,1)}, u32[]{:S(2)}) copy-start(bf16[1,1024,2048]{2,1,0:T(8,128)(2,1)} %param.23) | copy-start | bytes 12582916
  265.9 50.5 %copy-start.28 = (bf16[384,256]{1,0:T(8,128)(2,1)S(1)}, bf16[384,256]{1,0:T(8,128)(2,1)}, u32[]{:S(2)}) copy-start(bf16[384,256]{1,0:T(8,128)(2,1)} %copy-done.27) | copy-start | bytes 589828
  315.2 1.2 copy-start.26
Sparse Core Ops, SparseCore 0:
  9.7 29.0 all-gather.1
